TPU v7x, 32 devices: a whole 2x2x4 slice. The times are simulated.
32 devices in a mesh: leaf: 32 (over z, y, x, core).
Axes of the slice: x: 2, y: 2, z: 4, core: 2. Of those that a mesh axis runs over, the one named last changes fastest.
Arguments:
- points: bfloat16 [32768, 768], P('leaf'), may hold values from -4 to 4
- weights: bfloat16 [32768, 64], P('leaf'), may hold values from -0.0390625 to 0.0390625
- tree_slot: int32 [32768], P('leaf'), may hold values from 0 to 32767, as said below
- leaf_interp: bfloat16 [32, 256, 1024], P('leaf'), may hold values from -0.1875 to 0.1875
- skel_leaf: int32 [32, 256], P('leaf'), may hold values from 0 to 1023, as said below
- merge_interp: bfloat16 [32, 240, 512], P('leaf'), may hold values from -0.25 to 0.25
- merge_index: int32 [32, 240], P('leaf'), may hold values from 0 to 511, as said below
- near_mask: int32 [32, 8], P('leaf'), may hold values from 0 to 1, as said below
- far_mask: int32 [32, 4, 4], P('leaf'), may hold values from 0 to 1, as said below
Outputs:
- sums: float32 [32768, 64], P('leaf')
Inputs may be any that keep to these rules, and one draw needn't show every extreme that they name: `tree_slot`: A permutation of the tree positions; each aligned block of 1024 input points sends exactly 32 points into the block of every leaf. `skel_leaf`: each row lists 256 distinct positions. `merge_index`: for every node of every level, the 256 entries of I_k are distinct. Symmetric: near_mask[l, 4 + s - 1] equals near_mask[l + s, 4 - s] for 1 <= s <= 4; entries that name a leaf outside the tree are 0. `far_mask`: entries that name a node outside its level are 0.
All inputs are finite; a program needn't handle non-finite values.
Results may differ from a plain program's by a relative error of at most 0.0042.
Values may be sent and summed in bfloat16 or wider, within the bound.
No kernel may reach another device: no remote copies, remote signals or barrier semaphores. Data moves between devices by JAX's collectives and lax.ppermute only.
A program may use at most 128 MiB of HBM per device.

v0:
```python
import functools
import math

import jax
import jax.numpy as jnp
from jax import lax
from jax.experimental import pallas as pl
from jax.experimental.pallas import tpu as pltpu
from jax.sharding import PartitionSpec as P

LEVELS = 4
NWIN = 4
FWIN = 2
GROUP = 8
BF16 = jnp.bfloat16
F32 = jnp.float32
I32 = jnp.int32
NT = (((1,), (1,)), ((), ()))
TN = (((0,), (0,)), ((), ()))
CHUNK = 256


def call(kernel, grid_spec, out_shape, flops=0, moved=0, exps=0):
    return pl.pallas_call(
        kernel,
        grid_spec=grid_spec,
        out_shape=out_shape,
        compiler_params=pltpu.CompilerParams(vmem_limit_bytes=48 * 1024 * 1024),
        cost_estimate=pl.CostEstimate(flops=flops, bytes_accessed=moved, transcendentals=exps),
    )


def whole(shape):
    return pl.BlockSpec(shape, lambda *_: (0,) * len(shape))


def shapes(*specs):
    return [jax.ShapeDtypeStruct(shape, kind) for shape, kind in specs]


def mm(a, b):
    return jnp.dot(a, b, preferred_element_type=F32)


def mm_nt(a, b):
    return lax.dot_general(a, b, NT, preferred_element_type=F32)


def mm_tn(a, b):
    return lax.dot_general(a, b, TN, preferred_element_type=F32)


def device_of_leaf(leaf):
    group, chip = leaf // GROUP, (leaf // 2) % 4
    return group * GROUP + ((chip ^ (chip >> 1)) ^ ((group & 1) * 2)) * 2 + leaf % 2


def leaf_of_device(device):
    group, chip = device // GROUP, (device // 2) % 4 ^ ((device // GROUP & 1) * 2)
    return group * GROUP + (chip ^ (chip >> 1)) * 2 + device % 2


def move(value, target_of_leaf):
    leaves = lax.axis_size("leaf")
    pairs = []
    for leaf in range(leaves):
        target = target_of_leaf(leaf)
        if 0 <= target < leaves:
            pairs.append((device_of_leaf(leaf), device_of_leaf(target)))
    return lax.ppermute(value, "leaf", pairs)


def slot_sources(groups):
    slots = []
    for away in range(1, min(6, groups)):
        merge = away > 1 and groups <= 2 * away
        for steps in [(away, -away)] if merge else [(away,), (-away,)]:
            found = [[g + s for s in steps if 0 <= g + s < groups] for g in range(groups)]
            slots.append((away, [f[0] if f else -1 for f in found]))
    return slots


def send_slot(value, source):
    pairs = [
        (device_of_leaf(s * GROUP + i), device_of_leaf(g * GROUP + i))
        for g, s in enumerate(source)
        if s >= 0
        for i in range(GROUP)
    ]
    return lax.ppermute(value, "leaf", pairs)


LEAF, CORE, CHIP, NODE, AT, PHYS = range(6)
SLOT0 = 6


def iota(shape, dim):
    return lax.broadcasted_iota(I32, shape, dim)


def sort_kernel(rows, per_peer, leaves, lanes, slot_ref, points_ref, weights_ref, table_ref, send_ref, place_ref, place_s):
    step = pl.program_id(0)
    block = send_ref.shape[0]
    slot = slot_ref[...]

    @pl.when(step == 0)
    def _():
        dest = device_of_leaf(slot // rows)
        at = (iota((leaves, rows), 0) == dest).astype(BF16)
        earlier = (iota((rows, rows), 0) < iota((rows, rows), 1)).astype(BF16)
        rank = jnp.sum(at.astype(F32) * mm(at, earlier), axis=0, keepdims=True)
        place_s[...] = dest * per_peer + rank.astype(I32)
        place_ref[...] = place_s[...]

    pick = (iota((block, rows), 0) + step * block == place_s[...]).astype(BF16)
    width, columns = points_ref.shape[1], weights_ref.shape[0]
    wide = send_ref.shape[1]
    inner = slot % rows
    row = iota((16, rows), 0)
    parts = jnp.where(row == 0, inner // 32, jnp.where(row == 1, inner % 32, 0)).astype(F32).astype(BF16)
    send_ref[:, :width] = mm(pick, points_ref[...]).astype(BF16)
    send_ref[:, width : width + columns] = mm_nt(pick, weights_ref[...]).astype(BF16)
    send_ref[:, width + columns : width + columns + 16] = mm_nt(pick, parts).astype(BF16)
    send_ref[:, width + columns + 16 : wide - lanes] = jnp.zeros((block, wide - lanes - width - columns - 16), BF16)
    spread = (iota((block, per_peer), 0) % per_peer == iota((block, per_peer), 1)).astype(BF16)
    send_ref[:, wide - lanes :] = mm(spread, table_ref[...]).astype(BF16)


def tree_rows(extra):
    lane = iota((16, extra.shape[1]), 1)
    parts = jnp.where(lane == 0, 32.0, jnp.where(lane == 1, 1.0, 0.0)).astype(BF16)
    return mm_nt(parts, extra)[0:1].astype(I32)


def entries(table, low, high, leaf):
    lane = iota((1, GROUP), 1)
    return jnp.sum(jnp.where(lane == leaf, table[low:high], 0.0), axis=1, keepdims=True).astype(I32)


def table_of(table_ref, group):
    return jnp.transpose(table_ref[pl.ds(pl.multiple_of(group * GROUP, GROUP), GROUP)])


def bounds(rank):
    ends = [rank]
    for level in range(1, LEVELS + 1):
        ends.append(ends[-1] + (rank >> level))
    return ends


def node_picks(table, rank, level, first, count):
    low, high = bounds(rank)[level - 1 : level + 1]
    return jnp.concatenate([entries(table, low, high, first + i) for i in range(count)], axis=0)


def leaf_picks(table, rank, leaf, where):
    skeleton = (entries(table, 0, rank, leaf) == where).astype(BF16)
    index1 = node_picks(table, rank, 1, leaf // 2 * 2, 2) - rank * (leaf % 2)
    return skeleton, (index1 == iota((rank, rank), 1)).astype(BF16)


def level0_kernel(info, got_ref, interp_ref, table_ref, give_ref, keep_ref, weight0_ref):
    rank, columns = weight0_ref.shape
    rows, width = got_ref.shape[0], keep_ref.shape[1]
    half = rank // 2
    where = tree_rows(got_ref[:, width + columns :])
    order = (iota((rows, rows), 0) == where).astype(BF16)
    weights = mm(order, got_ref[:, width : width + columns]).astype(BF16)
    weight0 = mm(interp_ref[...], weights).astype(BF16)
    weight0_ref[...] = weight0
    table = table_of(table_ref, info[AT])
    skeleton, pick1 = leaf_picks(table, rank, info[LEAF] % GROUP, where)
    level0 = mm(skeleton, got_ref[:, :width]).astype(BF16)
    level1 = mm(pick1, level0).astype(BF16)
    core = info[CORE]

    def part(side):
        index2 = node_picks(table, rank, 2, 4 * info[NODE] + 2 * side, 2) - rank * (info[CHIP] % 2)
        return mm((index2 == iota((half, rank), 1)).astype(BF16), level1).astype(BF16)

    keep_ref[...] = part(core)
    give_ref[:, :width] = part(1 - core)
    give_ref[:, width : width + columns] = weight0[:half]
    give_ref[:, width + columns :] = weight0[half:]


def piece(info, pieces_ref, leaf):
    return pieces_ref.at[leaf % 2 ^ info[CORE], leaf // 2 ^ info[PHYS]]


def in_order(core, mine, other):
    return jnp.where(core == 0, jnp.concatenate([mine, other]), jnp.concatenate([other, mine]))


def level1_kernel(info, other_ref, keep_ref, weight0_ref, pieces_ref, out_ref, weight1_ref):
    rank, columns = weight1_ref.shape
    half, width = keep_ref.shape
    core = info[CORE]
    other0 = jnp.concatenate([other_ref[:, width : width + columns], other_ref[:, width + columns :]])
    both0 = in_order(core, weight0_ref[...], other0)
    pair = [mm(piece(info, pieces_ref, 2 * info[CHIP] + i)[:half], both0) for i in (0, 1)]
    weight1 = jnp.concatenate(pair).astype(BF16)
    weight1_ref[...] = weight1
    out_ref[:, :width] = keep_ref[...] + other_ref[:, :width]
    out_ref[:, width : width + columns] = weight1[:half]
    out_ref[:, width + columns :] = weight1[half:]


def level23_kernel(info, m0, m1, m2, m3, pieces_ref, out_ref, weight2_ref, weight3_ref, w1_s):
    half = m0.shape[0]
    rank = 2 * half
    columns = weight2_ref.shape[1]
    width = m0.shape[1] - 2 * columns
    core, chip, node = info[CORE], info[CHIP], info[NODE]
    for k, message in enumerate((m0, m1, m2, m3)):
        at = pl.ds(pl.multiple_of((chip ^ k) * rank, rank), rank)
        w1_s[at] = jnp.concatenate([message[:, width : width + columns], message[:, width + columns :]])
    r2, r3 = rank >> 2, rank >> 3
    for n in (0, 1):
        for i in range(4):
            rows2 = piece(info, pieces_ref, 4 * n + i)[half : half + r2]
            at = n * rank + i * r2
            weight2_ref[at : at + r2] = mm(rows2, w1_s[2 * n * rank : 2 * (n + 1) * rank]).astype(BF16)
    low = half + r2
    weight3 = jnp.concatenate(
        [mm(piece(info, pieces_ref, i)[low : low + r3], weight2_ref[...]) for i in range(GROUP)]
    )
    weight3_ref[...] = weight3.astype(BF16)
    own = m0[:, :width] + m1[:, :width]
    cross = m2[:, :width] + m3[:, :width]
    out_ref[:half, :width] = jnp.where(node == 0, own, cross)
    out_ref[half:, :width] = jnp.where(node == 0, cross, own)
    for n in (0, 1):
        at = pl.ds(pl.multiple_of(n * rank + core * half, half), half)
        out_ref[n * half : (n + 1) * half, width : width + columns] = weight2_ref[at]
    out_ref[:, width + columns :] = weight3.astype(BF16)


def level3_kernel(info, own_ref, other_ref, table_ref, out_ref):
    half = out_ref.shape[0]
    rank = 2 * half
    columns = 64
    width = own_ref.shape[1] - 2 * columns
    core = info[CORE]
    index = node_picks(table_of(table_ref, info[AT]), rank, 3, 4 * core, 4)
    entry = index % rank
    at = index // rank * half + entry % half
    hit = at == iota((half, rank), 1)
    mine = (hit & (entry // half == core)).astype(BF16)
    theirs = (hit & (entry // half != core)).astype(BF16)
    out_ref[:, :width] = (mm(mine, own_ref[:, :width]) + mm(theirs, other_ref[:, :width])).astype(BF16)
    out_ref[:, width : width + columns] = own_ref[:half, width + columns :]
    out_ref[:, width + columns :] = own_ref[half:, width + columns :]


def level4_kernel(info, weight3_ref, next_ref, before_ref, pieces_ref, out_ref):
    rank, columns = weight3_ref.shape
    low = rank - (rank >> 3)
    own = weight3_ref[...]
    sibling = jnp.where(info[AT] % 2 == 0, next_ref[:, columns:], before_ref[:, columns:])
    both = in_order(info[AT] % 2, own, sibling)
    r4 = rank >> 4
    for i in range(GROUP):
        out_ref[i * r4 : (i + 1) * r4] = mm(piece(info, pieces_ref, i)[low : low + r4], both).astype(BF16)


def far_masks(info, mask_ref, slots, source, node):
    row = info[LEAF]

    def at(level, step):
        column = jnp.clip(jnp.where(step < 0, step + FWIN, step + FWIN - 1), 0, 2 * FWIN - 1)
        value = mask_ref[row, 2 * NWIN + (level - 1) * 2 * FWIN + column]
        return jnp.where((step != 0) & (jnp.abs(step) <= FWIN) & (source >= 0), value, 0)

    two = [at(2, 2 * source + h - node) for h in (0, 1)]
    return two + [at(3, source - info[AT]), at(4, source // 2 - info[AT] // 2)]


def far_weight_kernel(away, info, mask_ref, own_ref, other_ref, cross_ref, table_ref, w4_ref, out_ref, w3_s, w4_s):
    slots = len(away)
    rank = w3_s.shape[1]
    half = rank // 2
    columns = w3_s.shape[2]
    core, node = info[CORE], info[NODE]
    blocks = own_ref.shape[0]
    starts, at = [], 0
    for distance in away:
        starts.append(at)
        at += rank if distance == 1 else half
    r4 = rank >> 4
    for i, distance in enumerate(away):
        s = starts[i]
        if distance == 1:
            w3_s[i] = own_ref[s : s + rank, columns:]
        else:
            w3_s[i] = jnp.concatenate([own_ref[s : s + half, :columns], own_ref[s : s + half, columns:]])
    out_ref[...] = jnp.zeros_like(out_ref)
    for i, distance in enumerate(away):
        source = info[SLOT0 + i]
        sibling = info[SLOT0 + slots + i]
        second = source % 2
        first_slot = jnp.where(second == 0, i, sibling)
        second_slot = jnp.where(second == 0, sibling, i)
        mask2a, mask2b, mask3, mask4 = far_masks(info, mask_ref, slots, source, 2 * info[AT] + node)
        mask2a, mask2b, mask3, mask4 = [m.astype(F32).astype(BF16) for m in (mask2a, mask2b, mask3, mask4)]
        w3 = w3_s[i]
        low4 = bounds(rank)[3]
        index = []
        for slot in (first_slot, second_slot):
            table = table_of(table_ref, jnp.maximum(info[SLOT0 + slot], 0))
            for j in range(GROUP):
                index.append(entries(table, low4, low4 + r4, j))
        index = jnp.concatenate(index) - rank * second
        w4 = jnp.concatenate([w4_ref[first_slot], w4_ref[second_slot]])
        w4 = mm_tn((index == iota((rank, rank), 1)).astype(BF16), w4).astype(BF16)
        s = starts[i]
        if distance == 1:
            index3 = node_picks(table_of(table_ref, jnp.maximum(source, 0)), rank, 3, 0, GROUP)
            for k, side in enumerate((core, 1 - core)):
                lane = iota((rank, rank), 1)
                code = lane // half * rank + side * half + lane % half
                hit = (index3 == code).astype(BF16)
                ref = own_ref if k == 0 else other_ref
                at = k * blocks + s
                out_ref[at : at + half, :columns] = ref[s : s + half, :columns] * mask2a
                out_ref[at + half : at + rank, :columns] = ref[s + half : s + rank, :columns] * mask2b
                out_ref[at : at + rank, columns : 2 * columns] = mm_tn(hit, w3).astype(BF16) * mask3
                out_ref[at : at + rank, 2 * columns :] = mm_tn(hit, w4).astype(BF16) * mask4
        else:
            w4_s[...] = w4
            for k, side in enumerate((core, 1 - core)):
                rows = pl.ds(pl.multiple_of(side * half, half), half)
                at = k * blocks + s
                out_ref[at : at + half, columns : 2 * columns] = w3_s[i, rows] * mask3
                out_ref[at : at + half, 2 * columns :] = w4_s[rows] * mask4
    mask2 = jnp.where(
        node == 0, mask_ref[info[LEAF], 2 * NWIN + 6], mask_ref[info[LEAF], 2 * NWIN + 5]
    )
    base = 2 * blocks
    for k, side in enumerate((core, 1 - core)):
        rows = pl.ds(pl.multiple_of((1 - node) * rank + side * half, half), half)
        at = base + k * half
        out_ref[at : at + half, :columns] = cross_ref[rows] * mask2.astype(F32).astype(BF16)


def row_offset(block, scale_inv):
    squares = jnp.sum(jnp.square(block.astype(F32)), axis=1, keepdims=True)
    return (squares - block.shape[1]) * (0.5 * scale_inv)


def as_row(column):
    return jnp.transpose(jnp.broadcast_to(column, (column.shape[0], 128)))[0:1]


def kernel_block(targets, sources, source_row, scale_inv):
    products = mm_nt(targets, sources)
    return jnp.exp(products * scale_inv - row_offset(targets, scale_inv) - source_row).astype(BF16)


def far_kernel(away, scale_inv, info, mask_ref, x_ref, own_ref, other_ref, half_ref, half_other_ref, w_ref, out_ref):
    step = pl.program_id(0)
    last = pl.num_programs(0) - 1
    columns = out_ref.shape[1]
    width = own_ref.shape[1] - 2 * columns
    rank = own_ref.shape[0]
    half = rank // 2
    slots = len(away)
    blocks = last * rank

    def add(sources, weights):
        kernel = kernel_block(x_ref[:, :width], sources, as_row(row_offset(sources, scale_inv)), scale_inv)
        sums = mm(kernel, weights)
        out_ref[...] += sums[:, :columns] + sums[:, columns : 2 * columns] + sums[:, 2 * columns :]

    @pl.when(step == 0)
    def _():
        out_ref[...] = jnp.zeros_like(out_ref)

    node = 2 * info[AT] + info[NODE]
    need, per_block = [], []
    for i, distance in enumerate(away):
        masks = far_masks(info, mask_ref, slots, info[SLOT0 + i], node)
        value = masks[2] + masks[3] + (masks[0] + masks[1] if distance == 1 else 0)
        if distance == 1:
            per_block.append(value)
        else:
            need.append(value)
    per_block += [need[i] + need[i + 1] for i in range(0, len(need), 2)]
    wanted = jnp.zeros((), I32)
    for i, value in enumerate(per_block):
        wanted = jnp.where(step == i, value, wanted)

    @pl.when(wanted > 0)
    def _():
        for k, ref in enumerate((own_ref, other_ref)):
            at = pl.ds(pl.multiple_of(k * blocks + step * rank, rank), rank)
            add(ref[:, :width], w_ref[at])

    @pl.when(step == last)
    def _():
        at = pl.ds(pl.multiple_of((1 - info[NODE]) * half, half), half)
        sources = jnp.concatenate([half_ref[at, :width], half_other_ref[at, :width]])
        add(sources, w_ref[2 * blocks :])


def halves(value):
    half = value.shape[1] // 2
    return value[:, :half] + value[:, half:]


def masked(weights, first, second):
    lane = iota((1, weights.shape[1]), 1)
    return (weights.astype(F32) * jnp.where(lane < weights.shape[1] // 2, first, second)).astype(BF16)


def own_kernel(scale_inv, width, info, mask_ref, own_ref, other_ref, out_ref, back_ref, acc, row_own, row_other):
    step = pl.program_id(0)
    tile, columns = out_ref.shape
    rows = own_ref.shape[0]
    half = rows // 2
    last = width + columns

    @pl.when(step == 0)
    def _():
        acc[...] = jnp.zeros_like(acc)
        row_own[...] = as_row(row_offset(own_ref[:, :width], scale_inv))
        row_other[...] = as_row(row_offset(other_ref[:, :width], scale_inv))

    start = pl.multiple_of(step * tile, tile)
    here = pl.ds(start, tile)
    mine = own_ref[here, :width]
    kernel = kernel_block(mine, own_ref[:, :width], row_own[...], scale_inv)
    out_ref[...] = mm(kernel, own_ref[:, width:last])
    near = mask_ref[info[LEAF] // 2 * 2, NWIN] > 0

    def pair(count):
        kernel = kernel_block(mine, other_ref[:count, :width], row_other[:, :count], scale_inv)
        out_ref[...] += mm(kernel, other_ref[:count, width:last])
        acc[:count] += mm_tn(kernel, own_ref[here, width:last])

    @pl.when(near & (info[CORE] == 0))
    def _():
        pair(half)

    @pl.when(near & (info[CORE] == 1) & (start >= half))
    def _():
        pair(rows)

    @pl.when(step == pl.num_programs(0) - 1)
    def _():
        back_ref[...] = acc[...]


def leaf_weights(x_ref, width, columns, weight1, table_ref, leaf):
    rank = weight1.shape[0]
    where = tree_rows(x_ref[:, width + columns :])
    skeleton, pick1 = leaf_picks(table_of(table_ref, leaf // GROUP), rank, leaf % GROUP, where)
    spread = mm_tn(skeleton, mm_tn(pick1, weight1).astype(BF16)).astype(BF16)
    return jnp.concatenate([x_ref[:, width : width + columns], spread], axis=1)


def pair_kernel(
    scale_inv, width, behind, per_leaf, info, mask_ref, a1_ref, a2_ref, wa_ref, r_ref, wr_ref, init_ref, acc_in_ref, table_ref,
    out1_ref, out2_ref, back_ref, acc, row_r, a_w, r_w,
):
    step = pl.program_id(0)
    tile, columns = out1_ref.shape
    core = info[CORE]
    chip = info[LEAF] // 2
    leaves = mask_ref.shape[0]
    r_leaf = jnp.minimum(2 * chip + 2, leaves - 2) + core

    @pl.when(step == 0)
    def _():
        acc[...] = acc_in_ref[...]
        row_r[...] = as_row(row_offset(r_ref[:, :width], scale_inv))
        r_w[...] = leaf_weights(r_ref, width, columns, wr_ref[...], table_ref, r_leaf)

    second = step >= per_leaf
    side = jnp.where(second, 1 - core, core)
    a_leaf = jnp.maximum(2 * chip - 2 * behind, 0) + side
    there = (2 * chip + 2 < leaves) & (chip >= behind)
    distance = 2 + 2 * behind + core - side
    near = jnp.where(distance <= NWIN, mask_ref[a_leaf, jnp.minimum(NWIN - 1 + distance, 2 * NWIN - 1)], 0)
    level1 = 2 * NWIN
    far_out = mask_ref[a_leaf, level1 + FWIN + behind]
    far_back = mask_ref[r_leaf, level1 + FWIN - 1 - behind]
    used = (near + far_out + far_back > 0) & there
    near, far_out, far_back = near.astype(F32), far_out.astype(F32), far_back.astype(F32)

    def part(a_ref, out_ref, at):
        base = pl.multiple_of(at * tile, tile)

        @pl.when(used)
        def _():
            @pl.when(at == 0)
            def _():
                a_w[...] = leaf_weights(a_ref, width, columns, wa_ref[...], table_ref, a_leaf)

            sources = masked(r_w[...], near, far_out)
            for start in range(0, tile, CHUNK):
                rows = pl.ds(base + start, CHUNK)
                kernel = kernel_block(a_ref[rows, :width], r_ref[:, :width], row_r[...], scale_inv)
                sums = halves(mm(kernel, sources))
                if out_ref is out2_ref and not behind:
                    sums += init_ref[rows]
                out_ref[start : start + CHUNK] = sums.astype(out_ref.dtype)
                acc[...] += mm_tn(masked(a_w[rows], near, far_back), kernel)

        @pl.when(jnp.logical_not(used))
        def _():
            if out_ref is out2_ref and not behind:
                out_ref[...] = init_ref[pl.ds(base, tile)].astype(out_ref.dtype)
            else:
                out_ref[...] = jnp.zeros_like(out_ref)

    @pl.when(jnp.logical_not(second))
    def _():
        part(a1_ref, out1_ref, step)

    @pl.when(second)
    def _():
        part(a2_ref, out2_ref, step - per_leaf)

    @pl.when(step == pl.num_programs(0) - 1)
    def _():
        if behind:
            back_ref[...] = halves(jnp.transpose(acc[...])).astype(back_ref.dtype)
        else:
            back_ref[...] = acc[...]


def home_kernel(place_ref, got_ref, out_ref):
    rows = got_ref.shape[0]
    pick = (iota((rows, rows), 0) == place_ref[...]).astype(BF16)
    out_ref[...] = mm_tn(got_ref[...], pick)


def local(
    points, weights, tree_slot, leaf_interp, skel_leaf, merge_interp, merge_index, near_mask, far_mask
):
    leaves = lax.axis_size("leaf")
    groups = leaves // GROUP
    rows, width = points.shape
    columns = weights.shape[1]
    per_peer = rows // leaves
    rank = skel_leaf.shape[1]
    lanes = 4 * rank // per_peer
    wide = width + -(-(columns + 16 + lanes) // 128) * 128
    half = rank // 2
    scale_inv = 1.0 / (1.75 * math.sqrt(width))
    message = width + 2 * columns
    slots = slot_sources(groups)
    away = [a for a, _ in slots]

    def prefetch(count, grid, ins, outs, scratch=()):
        return pltpu.PrefetchScalarGridSpec(
            num_scalar_prefetch=count, grid=grid, in_specs=ins, out_specs=outs, scratch_shapes=scratch
        )

    spare = 2 * rank - rank - merge_index.shape[1]
    picks = jnp.concatenate([skel_leaf, merge_index], axis=1)
    table = jnp.concatenate(
        [picks // 32, far_mask.reshape(1, -1), picks % 32, near_mask, jnp.zeros((1, spare - near_mask.shape[1]), I32)],
        axis=1,
    )
    table = table.astype(F32).astype(BF16).reshape(per_peer, lanes)

    send, place = call(
        functools.partial(sort_kernel, rows, per_peer, leaves, lanes),
        pl.GridSpec(
            grid=(4,),
            in_specs=[whole((1, rows)), whole((rows, width)), whole((columns, rows)), whole((per_peer, lanes))],
            out_specs=[pl.BlockSpec((rows // 4, wide), lambda i: (i, 0)), whole((1, rows))],
            scratch_shapes=[pltpu.VMEM((1, rows), I32)],
        ),
        shapes(((rows, wide), BF16), ((1, rows), I32)),
    )(tree_slot.reshape(1, rows), points, weights.T, table)
    got = lax.all_to_all(send, "leaf", split_axis=0, concat_axis=0, tiled=True)

    device = lax.axis_index("leaf")
    leaf = leaf_of_device(device)
    group = leaf // GROUP
    source = jnp.asarray([s for _, s in slots], I32)[:, group]
    sibling = jnp.argmax((source[None, :] == (source ^ 1)[:, None]).astype(I32), axis=1).astype(I32)
    info = jnp.concatenate(
        [
            jnp.stack([leaf, leaf % 2, leaf // 2 % 4, leaf // 4 % 2, group, device // 2 % 4]).astype(I32),
            source,
            sibling,
        ]
    )
    interp_in, merge_in, _ = lax.optimization_barrier((leaf_interp[0], merge_interp[0], place))
    interp = lax.ppermute(interp_in, "leaf", [(i, device_of_leaf(i)) for i in range(leaves)])
    near_pieces = jnp.stack(
        [merge_in]
        + [lax.ppermute(merge_in, "leaf", [(i, i ^ (2 * k)) for i in range(leaves)]) for k in (1, 2, 3)]
    )
    pieces = jnp.stack([near_pieces, lax.ppermute(near_pieces, "leaf", [(i, i ^ 1) for i in range(leaves)])])
    piece_shape = pieces.shape

    coded = got[:, wide - lanes :].reshape(leaves, 4 * rank).astype(F32)
    tables = coded[:, : 2 * rank] * 32.0 + coded[:, 2 * rank :]
    mask_at = rank + merge_index.shape[1]
    masks = jnp.concatenate(
        [
            coded[:, 2 * rank + mask_at : 2 * rank + mask_at + 2 * NWIN],
            coded[:, mask_at : mask_at + LEVELS * 2 * FWIN],
        ],
        axis=1,
    ).astype(I32)
    table_shape = tables.shape

    other = move(got, lambda i: i ^ 1)
    behind = move(got, lambda i: i + 2)
    ahead = move(got, lambda i: i - 2)

    give, keep, weight0 = call(
        level0_kernel,
        prefetch(1, (), [whole((rows, wide)), whole((rank, rows)), whole(table_shape)],
                 [whole((half, message)), whole((half, width)), whole((rank, columns))]),
        shapes(((half, message), BF16), ((half, width), BF16), ((rank, columns), BF16)),
    )(info, got, interp, tables)
    sent, weight1 = call(
        level1_kernel,
        prefetch(1, (), [whole((half, message)), whole((half, width)), whole((rank, columns)), whole(piece_shape)],
                 [whole((half, message)), whole((rank, columns))]),
        shapes(((half, message), BF16), ((rank, columns), BF16)),
    )(info, move(give, lambda i: i ^ 1), keep, weight0, pieces)
    behind1 = move(weight1, lambda i: i + 2)
    ahead1 = move(weight1, lambda i: i - 2)
    half2, weight2, weight3 = call(
        level23_kernel,
        prefetch(1, (), [whole((half, message))] * 4 + [whole(piece_shape)],
                 [whole((rank, message)), whole((2 * rank, columns)), whole((rank, columns))],
                 [pltpu.VMEM((4 * rank, columns), BF16)]),
        shapes(((rank, message), BF16), ((2 * rank, columns), BF16), ((rank, columns), BF16)),
    )(info, sent, *[move(sent, lambda i, k=k: i ^ (2 * k)) for k in (1, 2, 3)], pieces)
    half2_other = move(half2, lambda i: i ^ 1)
    half3 = call(
        level3_kernel,
        prefetch(1, (), [whole((rank, message))] * 2 + [whole(table_shape)], whole((half, message))),
        jax.ShapeDtypeStruct((half, message), BF16),
    )(info, half2, half2_other, tables)
    far_parts = [send_slot(half2 if a == 1 else half3, s) for a, s in slots]
    extra = pl.BlockSpec((rank, 2 * columns), lambda *_: (0, width // (2 * columns)))
    half4 = call(
        level4_kernel,
        prefetch(1, (1,), [whole((rank, columns)), extra, extra, whole(piece_shape)], whole((half, columns))),
        jax.ShapeDtypeStruct((half, columns), BF16),
    )(info, weight3, far_parts[0], far_parts[1], pieces)
    weight4 = jnp.stack([send_slot(half4, s) for _, s in slots])
    far_own = jnp.concatenate(far_parts)
    far_other = move(far_own, lambda i: i ^ 1)

    tile = rows // 4
    own_sum, other_sum = call(
        functools.partial(own_kernel, scale_inv, width),
        prefetch(2, (4,), [whole((rows, wide))] * 2,
                 [pl.BlockSpec((tile, columns), lambda i, *_: (i, 0)), whole((rows, columns))],
                 [pltpu.VMEM((rows, columns), F32), pltpu.VMEM((1, rows), F32), pltpu.VMEM((1, rows), F32)]),
        shapes(((rows, columns), F32), ((rows, columns), F32)),
        flops=3 * rows * rows * wide, exps=3 * rows * rows // 2, moved=4 * rows * wide,
    )(info, masks, got, other)

    blocks = far_own.shape[0] // rank
    far_rows = (2 * blocks + 1) * rank
    extra = pl.BlockSpec((blocks * rank, 2 * columns), lambda *_: (0, width // (2 * columns)))
    far_w = call(
        functools.partial(far_weight_kernel, away),
        prefetch(2, (1,), [extra, extra, whole((2 * rank, columns)), whole(table_shape), whole(weight4.shape)],
                 whole((far_rows, 3 * columns)),
                 [pltpu.VMEM((len(slots), rank, columns), BF16), pltpu.VMEM((rank, columns), BF16)]),
        jax.ShapeDtypeStruct((far_rows, 3 * columns), BF16),
    )(info, masks, far_own, far_other, weight2, tables, weight4)
    block = pl.BlockSpec((rank, message), lambda i, *_: (jnp.minimum(i, blocks - 1), 0))
    far_sum = call(
        functools.partial(far_kernel, away, scale_inv),
        prefetch(2, (blocks + 1,),
                 [whole((rows, wide)), block, block, whole((rank, message)), whole((rank, message)), whole((far_rows, 3 * columns))],
                 whole((rows, columns))),
        jax.ShapeDtypeStruct((rows, columns), F32),
        flops=2 * rows * far_rows * wide, exps=rows * far_rows, moved=4 * rows * wide,
    )(info, masks, got, far_own, far_other, half2, half2_other, far_w)

    tile = rows // 2
    per_leaf = rows // tile

    def pairs(behind_chip, a1, a2, a_w, init, acc_in, out_kinds):
        back = ((rows, columns), BF16) if behind_chip else ((2 * columns, rows), F32)
        return call(
            functools.partial(pair_kernel, scale_inv, width, behind_chip, per_leaf),
            prefetch(2, (2 * per_leaf,),
                     [whole((rows, wide))] * 2 + [whole((rank, columns)), whole((rows, wide)), whole((rank, columns)),
                      whole((rows, columns)), whole((2 * columns, rows)), whole(table_shape)],
                     [pl.BlockSpec((tile, columns), lambda i, *_: (jnp.minimum(i, per_leaf - 1), 0)),
                      pl.BlockSpec((tile, columns), lambda i, *_: (jnp.maximum(i - per_leaf, 0), 0)),
                      whole(back[0])],
                     [pltpu.VMEM((2 * columns, rows), F32), pltpu.VMEM((1, rows), F32),
                      pltpu.VMEM((rows, 2 * columns), BF16), pltpu.VMEM((rows, 2 * columns), BF16)]),
            shapes(((rows, columns), out_kinds[0]), ((rows, columns), out_kinds[1]), back),
            flops=4 * rows * rows * wide, exps=2 * rows * rows, moved=8 * rows * wide,
        )(info, masks, a1, a2, a_w, ahead, ahead1, init, acc_in, tables)

    zero = jnp.zeros((2 * columns, rows), F32)
    next_own, next_other, acc = pairs(0, got, other, weight1, other_sum, zero, (F32, BF16))
    behind_other = move(behind, lambda i: i ^ 1)
    behind_sum, behind_other_sum, ahead_sum = pairs(
        1, behind, behind_other, behind1, other_sum, acc, (BF16, BF16)
    )

    own = own_sum + far_sum + next_own
    own = own + move(next_other, lambda i: i ^ 1)
    own = own + move(behind_sum, lambda i: i - 2)
    own = own + move(behind_other_sum, lambda i: (i ^ 1) - 2)
    own = own + move(ahead_sum, lambda i: i + 2)
    home = lax.all_to_all(own.astype(BF16), "leaf", split_axis=0, concat_axis=0, tiled=True)
    return call(
        home_kernel,
        pl.GridSpec(grid=(), in_specs=[whole((1, rows)), whole((rows, columns))], out_specs=whole((columns, rows))),
        jax.ShapeDtypeStruct((columns, rows), F32),
    )(place, home).T


def solution(mesh):
    placed = (
        P("leaf", None),
        P("leaf", None),
        P("leaf"),
        P("leaf", None, None),
        P("leaf", None),
        P("leaf", None, None),
        P("leaf", None),
        P("leaf", None),
        P("leaf", None, None),
    )
    return jax.shard_map(
        local, mesh=mesh, in_specs=placed, out_specs=P("leaf", None), check_vma=False
    )
```

profile of v0, /device:TPU:0, one launch (start us, length us, event | category | flops | bytes accessed | tf_op | source)
XLA Modules:
  0.0 297.3 jit_solution(8155364114962368308)
XLA Ops:
  6.0 4.3 %shard_map.100 = (bf16[1024,896]{1,0:T(8,128)(2,1)S(1)}, s32[1,1024]{1,0:T(1,128)S(1)}) custom-call(s32[1,1024]{1,0:T(1,128)S(1)} %bitcast.41, bf16[1024,768]{1,0:T(8,128)(2,1)S(1)} %copy-done.2, bf16[64,1024]{1,0:T(8,128)(2,1)S(1)} %bitcast.40, bf16[32,32]{1,0:T(8,128)(2,1)S(1)} %convert_element_type.45.table_ref), custom_call_target="tpu_custom_call" | custom-call | tf_op jit(solution)/shard_map/pallas_call | solution.py:569
  11.6 7.3 %all-to-all-start = ((bf16[32,32,896]{2,1,0:T(8,128)(2,1)}), bf16[32,32,896]{2,1,0:T(8,128)(2,1)S(1)}, u32[]{:S(2)}, u32[]{:S(2)}) async-start(bf16[32,32,896]{2,1,0:T(8,128)(2,1)} %bitcast.38), calls=%async_computation | async-start | bytes 3670016 | tf_op jit(solution)/shard_map/all_to_all | solution.py:579
  18.9 1.8 collective-permute-start.3
  22.5 20.7 %collective-permute-done.3 = bf16[240,512]{1,0:T(8,128)(2,1)S(1)} collective-permute-done((bf16[240,512]{1,0:T(8,128)(2,1)S(1)}, bf16[240,512]{1,0:T(8,128)(2,1)S(1)}, u32[]{:S(2)}, u32[]{:S(2)}) %collective-permute-start.3) | collective-permute-done | bytes 245792 | tf_op jit(solution)/shard_map/ppermute | solution.py:597
  43.1 7.3 %collective-permute-done.5 = bf16[240,512]{1,0:T(8,128)(2,1)S(1)} collective-permute-done((bf16[240,512]{1,0:T(8,128)(2,1)S(1)}, bf16[240,512]{1,0:T(8,128)(2,1)S(1)}, u32[]{:S(2)}, u32[]{:S(2)}) %collective-permute-start.5) | collective-permute-done | bytes 245792 | tf_op jit(solution)/shard_map/ppermute | solution.py:597
  51.6 1.7 collective-permute-start.1
  54.0 8.3 %all-to-all-done = bf16[32,32,896]{2,1,0:T(8,128)(2,1)S(1)} async-done(((bf16[32,32,896]{2,1,0:T(8,128)(2,1)}), bf16[32,32,896]{2,1,0:T(8,128)(2,1)S(1)}, u32[]{:S(2)}, u32[]{:S(2)}) %all-to-all-start) | async-done | bytes 1835040 | tf_op jit(solution)/shard_map/all_to_all | solution.py:579
  62.2 4.4 %collective-permute-start.23 = (bf16[1024,896]{1,0:T(8,128)(2,1)S(1)}, bf16[1024,896]{1,0:T(8,128)(2,1)}, u32[]{:S(2)}, u32[]{:S(2)}) collective-permute-start(bf16[1024,896]{1,0:T(8,128)(2,1)S(1)} %bitcast.30), channel_id=1, source_target_pairs={{0,2},{1,3},{2,6},{3,7},{6,4},{7,5},{4,12},{5,13},{12,14},{13,15},... | collective-permute-start | bytes 5505032 | tf_op jit(solution)/shard_map/ppermute | solution.py:70
  69.7 3.4 %shard_map.102 = (bf16[128,896]{1,0:T(8,128)(2,1)S(1)}, bf16[128,768]{1,0:T(8,128)(2,1)S(1)}, bf16[256,64]{1,0:T(8,128)(2,1)S(1)}) custom-call(s32[14]{0:T(128)S(1)} %concatenate.73.info, bf16[1024,896]{1,0:T(8,128)(2,1)S(1)} %bitcast.32, bf16[256,1024]{1,0:T(8,128)(2,1)S(1)} %collective-permute-done.1.interp_ref, f32[32,512]{1,0:T(8,128)S(1)} %slice_add_fusion.table_ref), custom_call_target="tpu_custom_call" | custom-call | tf_op jit(solution)/shard_map/pallas_call | solution.py:618
  76.0 2.3 collective-permute-start.8
  79.1 31.7 %collective-permute-done.7.m1 = bf16[128,896]{1,0:T(8,128)(2,1)S(1)} collective-permute-done((bf16[128,896]{1,0:T(8,128)(2,1)S(1)}, bf16[128,896]{1,0:T(8,128)(2,1)S(1)}, u32[]{:S(2)}, u32[]{:S(2)}) %collective-permute-start.7) | collective-permute-done | bytes 229408 | tf_op jit(solution)/shard_map/ppermute | solution.py:70
  110.7 8.5 %collective-permute-done.8.m2 = bf16[128,896]{1,0:T(8,128)(2,1)S(1)} collective-permute-done((bf16[128,896]{1,0:T(8,128)(2,1)S(1)}, bf16[128,896]{1,0:T(8,128)(2,1)S(1)}, u32[]{:S(2)}, u32[]{:S(2)}) %collective-permute-start.8) | collective-permute-done | bytes 229408 | tf_op jit(solution)/shard_map/ppermute | solution.py:70
  122.3 5.5 %collective-permute-start.11 = (bf16[256,896]{1,0:T(8,128)(2,1)S(1)}, bf16[256,896]{1,0:T(8,128)(2,1)S(1)}, u32[]{:S(2)}, u32[]{:S(2)}) collective-permute-start(bf16[256,896]{1,0:T(8,128)(2,1)S(1)} %get-tuple-element.36.own_ref.half_ref), channel_id=1, source_target_pairs={{0,12},{1,13},{2,14},{3,15},{6,10},{7,11},{4,8},{5,9},{12,16},{13,... | collective-permute-start | bytes 1376264 | tf_op jit(solution)/shard_map/ppermute | solution.py:90
  130.2 7.0 %collective-permute-done.10.next_ref = bf16[256,896]{1,0:T(8,128)(2,1)S(1)} collective-permute-done((bf16[256,896]{1,0:T(8,128)(2,1)S(1)}, bf16[256,896]{1,0:T(8,128)(2,1)S(1)}, u32[]{:S(2)}, u32[]{:S(2)}) %collective-permute-start.10) | collective-permute-done | bytes 458784 | tf_op jit(solution)/shard_map/ppermute | solution.py:90
  137.2 9.3 %collective-permute-start.13 = (bf16[128,896]{1,0:T(8,128)(2,1)S(1)}, bf16[128,896]{1,0:T(8,128)(2,1)S(1)}, u32[]{:S(2)}, u32[]{:S(2)}) collective-permute-start(bf16[128,896]{1,0:T(8,128)(2,1)S(1)} %shard_map.105), channel_id=1, source_target_pairs={{16,0},{17,1},{18,2},{19,3},{22,6},{23,7},{20,4},{21,5},{28,12},{2... | collective-permute-start | bytes 688136 | tf_op jit(solution)/shard_map/ppermute | solution.py:90
  146.6 6.2 %collective-permute-start.14 = (bf16[128,896]{1,0:T(8,128)(2,1)S(1)}, bf16[128,896]{1,0:T(8,128)(2,1)S(1)}, u32[]{:S(2)}, u32[]{:S(2)}) collective-permute-start(bf16[128,896]{1,0:T(8,128)(2,1)S(1)} %shard_map.105), channel_id=1, source_target_pairs={{28,0},{29,1},{30,2},{31,3},{26,6},{27,7},{24,4},{25,5},{0,28},{1,... | collective-permute-start | bytes 688136 | tf_op jit(solution)/shard_map/ppermute | solution.py:90
  152.9 43.8 %collective-permute-done.13 = bf16[128,896]{1,0:T(8,128)(2,1)S(1)} collective-permute-done((bf16[128,896]{1,0:T(8,128)(2,1)S(1)}, bf16[128,896]{1,0:T(8,128)(2,1)S(1)}, u32[]{:S(2)}, u32[]{:S(2)}) %collective-permute-start.13) | collective-permute-done | bytes 229408 | tf_op jit(solution)/shard_map/ppermute | solution.py:90
  199.1 5.4 %collective-permute-done.16 = bf16[128,64]{1,0:T(8,128)(2,1)S(1)} collective-permute-done((bf16[128,64]{1,0:T(8,128)(2,1)S(1)}, bf16[128,64]{1,0:T(8,128)(2,1)S(1)}, u32[]{:S(2)}, u32[]{:S(2)}) %collective-permute-start.16) | collective-permute-done | bytes 16416 | tf_op jit(solution)/shard_map/ppermute | solution.py:90
  204.5 1.6 collective-permute-start.17
  206.1 1.6 collective-permute-done.17
  207.7 3.1 %collective-permute-start.18 = (bf16[128,64]{1,0:T(8,128)(2,1)S(1)}, bf16[128,64]{1,0:T(8,128)(2,1)S(1)}, u32[]{:S(2)}, u32[]{:S(2)}) collective-permute-start(bf16[128,64]{1,0:T(8,128)(2,1)S(1)} %shard_map.106), channel_id=1, source_target_pairs={{16,0},{17,1},{18,2},{19,3},{22,6},{23,7},{20,4},{21,5},{28,12},{2... | collective-permute-start | bytes 49160 | tf_op jit(solution)/shard_map/ppermute | solution.py:90
  210.9 1.7 collective-permute-done.18
  212.6 4.4 %collective-permute-start.19 = (bf16[128,64]{1,0:T(8,128)(2,1)S(1)}, bf16[128,64]{1,0:T(8,128)(2,1)S(1)}, u32[]{:S(2)}, u32[]{:S(2)}) collective-permute-start(bf16[128,64]{1,0:T(8,128)(2,1)S(1)} %shard_map.106), channel_id=1, source_target_pairs={{28,0},{29,1},{30,2},{31,3},{26,6},{27,7},{24,4},{25,5},{0,28},{1,... | collective-permute-start | bytes 49160 | tf_op jit(solution)/shard_map/ppermute | solution.py:90
  217.1 4.0 %collective-permute-done.19 = bf16[128,64]{1,0:T(8,128)(2,1)S(1)} collective-permute-done((bf16[128,64]{1,0:T(8,128)(2,1)S(1)}, bf16[128,64]{1,0:T(8,128)(2,1)S(1)}, u32[]{:S(2)}, u32[]{:S(2)}) %collective-permute-start.19) | collective-permute-done | bytes 16416 | tf_op jit(solution)/shard_map/ppermute | solution.py:90
  222.5 4.7 %collective-permute-start.25 = (bf16[256,64]{1,0:T(8,128)(2,1)S(1)}, bf16[256,64]{1,0:T(8,128)(2,1)S(1)}, u32[]{:S(2)}, u32[]{:S(2)}) collective-permute-start(bf16[256,64]{1,0:T(8,128)(2,1)S(1)} %get-tuple-element.39.wa_ref), channel_id=1, source_target_pairs={{0,2},{1,3},{2,6},{3,7},{6,4},{7,5},{4,12},{5,13},{12,14},{13,15},... | collective-permute-start | bytes 98312 | tf_op jit(solution)/shard_map/ppermute | solution.py:70
  227.2 8.0 %shard_map.101 = (f32[1024,64]{1,0:T(8,128)S(1)}, f32[1024,64]{1,0:T(8,128)S(1)}) custom-call(s32[14]{0:T(128)S(1)} %concatenate.73.info, s32[32,24]{1,0:T(8,128)S(1)} %maximum_convert_fusion.mask_ref, bf16[1024,896]{1,0:T(8,128)(2,1)S(1)} %bitcast.35, bf16[1024,896]{1,0:T(8,128)(2,1)S(1)} %collective-permute-done.other_ref.a2_ref), custom_call_target="tpu_custom_call" | custom-call | flops 2818572288 | bytes 3670016 | tf_op jit(solution)/shard_map/pallas_call | solution.py:657
  236.5 13.1 %shard_map.109 = (f32[1024,64]{1,0:T(8,128)S(1)}, bf16[1024,64]{1,0:T(8,128)(2,1)S(1)}, f32[128,1024]{1,0:T(8,128)S(1)}) custom-call(s32[14]{0:T(128)S(1)} %concatenate.73.info, s32[32,24]{1,0:T(8,128)S(1)} %maximum_convert_fusion.mask_ref, bf16[1024,896]{1,0:T(8,128)(2,1)S(1)} %bitcast.36, bf16[1024,896]{1,0:T(8,128)(2,1)} %copy-done.5, ...), custom_call_target="tpu_custom_call" | custom-call | flops 3758096384 | bytes 7340032 | tf_op jit(solution)/shard_map/pallas_call | solution.py:691
  249.8 3.4 %shard_map.107.w_ref = bf16[1792,192]{1,0:T(8,128)(2,1)S(1)} custom-call(s32[14]{0:T(128)S(1)} %concatenate.73.info, s32[32,24]{1,0:T(8,128)S(1)} %maximum_convert_fusion.mask_ref, bf16[768,896]{1,0:T(8,128)(2,1)S(1)} %constant_dynamic-update-slice_fusion.2.own_ref, bf16[768,896]{1,0:T(8,128)(2,1)S(1)} %collective-permute-done.15.other_ref, ...), custom_call_target="tpu_custom_call" | custom-call | tf_op jit(solution)/shard_map/pallas_call | solution.py:669
  253.2 5.1 %shard_map.110 = (bf16[1024,64]{1,0:T(8,128)(2,1)S(1)}, bf16[1024,64]{1,0:T(8,128)(2,1)S(1)}, bf16[1024,64]{1,0:T(8,128)(2,1)S(1)}) custom-call(s32[14]{0:T(128)S(1)} %concatenate.73.info, s32[32,24]{1,0:T(8,128)S(1)} %maximum_convert_fusion.mask_ref, bf16[1024,896]{1,0:T(8,128)(2,1)} %collective-permute-done.23.a1_ref, ...), custom_call_target="tpu_custom_call" | custom-call | flops 3758096384 | bytes 7340032 | tf_op jit(solution)/shard_map/pallas_call | solution.py:691
  260.9 7.4 %collective-permute-start.28 = (bf16[1024,64]{1,0:T(8,128)(2,1)S(1)}, bf16[1024,64]{1,0:T(8,128)(2,1)S(1)}, u32[]{:S(2)}, u32[]{:S(2)}) collective-permute-start(bf16[1024,64]{1,0:T(8,128)(2,1)S(1)} %get-tuple-element.46), channel_id=1, source_target_pairs={{0,2},{1,3},{2,6},{3,7},{6,4},{7,5},{4,12},{5,13},{12,14},{13,15},... | collective-permute-start | bytes 393224 | tf_op jit(solution)/shard_map/ppermute | solution.py:70
  268.3 8.8 %shard_map.108 = f32[1024,64]{1,0:T(8,128)S(1)} custom-call(s32[14]{0:T(128)S(1)} %concatenate.73.info, s32[32,24]{1,0:T(8,128)S(1)} %maximum_convert_fusion.mask_ref, bf16[1024,896]{1,0:T(8,128)(2,1)} %bitcast.37, bf16[768,896]{1,0:T(8,128)(2,1)S(1)} %constant_dynamic-update-slice_fusion.2.own_ref, bf16[768,896]{1,0:T(8,128)(2,1)S(1)} %collective-permute-done.15.other_ref, ...), custom_call_target="tpu_custom_call" | custom-call | flops 3288334336 | bytes 3670016 | tf_op jit(solution)/shard_map/pallas_call | solution.py:677
  277.6 18.2 %all_to_all.22 = bf16[32,2,1024]{2,1,0:T(2,128)(2,1)S(1)} all-to-all(bf16[32,2,1024]{2,1,0:T(2,128)(2,1)S(1)} %reshape.256), channel_id=1, replica_groups=mesh['leaf'=32] {'leaf'}, dimensions={0} | all-to-all | bytes 262144 | tf_op jit(solution)/shard_map/all_to_all | solution.py:717
  (86 shorter events, 32.8 us)
Async XLA Ops:
  11.6 50.6 %all-to-all-start = ((bf16[32,32,896]{2,1,0:T(8,128)(2,1)}), bf16[32,32,896]{2,1,0:T(8,128)(2,1)S(1)}, u32[]{:S(2)}, u32[]{:S(2)}) async-start(bf16[32,32,896]{2,1,0:T(8,128)(2,1)} %bitcast.38), calls=%async_computation | async-start | bytes 3670016 | tf_op jit(solution)/shard_map/all_to_all | solution.py:579
  18.9 24.2 %collective-permute-start.3 = (bf16[240,512]{1,0:T(8,128)(2,1)S(1)}, bf16[240,512]{1,0:T(8,128)(2,1)S(1)}, u32[]{:S(2)}, u32[]{:S(2)}) collective-permute-start(bf16[240,512]{1,0:T(8,128)(2,1)S(1)} %bitcast.43), channel_id=1, source_target_pairs={{0,2},{1,3},{2,0},{3,1},{4,6},{5,7},{6,4},{7,5},{8,10},{9,11},{10,... | collective-permute-start | bytes 737288 | tf_op jit(solution)/shard_map/ppermute | solution.py:597
  20.7 22.4 %collective-permute-start.4 = (bf16[240,512]{1,0:T(8,128)(2,1)S(1)}, bf16[240,512]{1,0:T(8,128)(2,1)S(1)}, u32[]{:S(2)}, u32[]{:S(2)}) collective-permute-start(bf16[240,512]{1,0:T(8,128)(2,1)S(1)} %bitcast.44), channel_id=1, source_target_pairs={{0,4},{1,5},{2,6},{3,7},{4,0},{5,1},{6,2},{7,3},{8,12},{9,13},{10,... | collective-permute-start | bytes 737288 | tf_op jit(solution)/shard_map/ppermute | solution.py:597
  22.2 28.2 %collective-permute-start.5 = (bf16[240,512]{1,0:T(8,128)(2,1)S(1)}, bf16[240,512]{1,0:T(8,128)(2,1)S(1)}, u32[]{:S(2)}, u32[]{:S(2)}) collective-permute-start(bf16[240,512]{1,0:T(8,128)(2,1)S(1)} %bitcast.45), channel_id=1, source_target_pairs={{0,6},{1,7},{2,4},{3,5},{4,2},{5,3},{6,0},{7,1},{8,14},{9,15},{10,... | collective-permute-start | bytes 737288 | tf_op jit(solution)/shard_map/ppermute | solution.py:597
  51.6 21.6 %collective-permute-start.6 = (bf16[4,240,512]{2,1,0:T(8,128)(2,1)}, bf16[4,240,512]{2,1,0:T(8,128)(2,1)}, u32[]{:S(2)}, u32[]{:S(2)}) collective-permute-start(bf16[4,240,512]{2,1,0:T(8,128)(2,1)} %get-tuple-element.50), channel_id=1, source_target_pairs={{0,1},{1,0},{2,3},{3,2},{4,5},{5,4},{6,7},{7,6},{8,9},{9,8},{10,11... | collective-permute-start | bytes 2949128 | tf_op jit(solution)/shard_map/ppermute | solution.py:599
  51.6 18.1 %collective-permute-start.1 = (bf16[256,1024]{1,0:T(8,128)(2,1)}, bf16[256,1024]{1,0:T(8,128)(2,1)S(1)}, u32[]{:S(2)}, u32[]{:S(2)}) collective-permute-start(bf16[256,1024]{1,0:T(8,128)(2,1)} %bitcast.12), channel_id=1, source_target_pairs={{0,0},{1,1},{2,2},{3,3},{4,6},{5,7},{6,4},{7,5},{8,12},{9,13},{10,... | collective-permute-start | bytes 1572872 | tf_op jit(solution)/shard_map/ppermute | solution.py:594
  62.2 173.1 %copy-start = (bf16[32,32,896]{2,1,0:T(8,128)(2,1)}, bf16[32,32,896]{2,1,0:T(8,128)(2,1)S(1)}, u32[]{:S(2)}) copy-start(bf16[32,32,896]{2,1,0:T(8,128)(2,1)S(1)} %all-to-all-done) | copy-start | bytes 5505028
  62.2 84.3 %collective-permute-start.23 = (bf16[1024,896]{1,0:T(8,128)(2,1)S(1)}, bf16[1024,896]{1,0:T(8,128)(2,1)}, u32[]{:S(2)}, u32[]{:S(2)}) collective-permute-start(bf16[1024,896]{1,0:T(8,128)(2,1)S(1)} %bitcast.30), channel_id=1, source_target_pairs={{0,2},{1,3},{2,6},{3,7},{6,4},{7,5},{4,12},{5,13},{12,14},{13,15},... | collective-permute-start | bytes 5505032 | tf_op jit(solution)/shard_map/ppermute | solution.py:70
  73.1 1.6 collective-permute-start.2
  75.5 35.2 %collective-permute-start.7 = (bf16[128,896]{1,0:T(8,128)(2,1)S(1)}, bf16[128,896]{1,0:T(8,128)(2,1)S(1)}, u32[]{:S(2)}, u32[]{:S(2)}) collective-permute-start(bf16[128,896]{1,0:T(8,128)(2,1)S(1)} %get-tuple-element.35.m0), channel_id=1, source_target_pairs={{0,2},{1,3},{2,0},{3,1},{6,4},{7,5},{4,6},{5,7},{12,14},{13,15},{1... | collective-permute-start | bytes 688136 | tf_op jit(solution)/shard_map/ppermute | solution.py:70
  76.0 43.2 %collective-permute-start.8 = (bf16[128,896]{1,0:T(8,128)(2,1)S(1)}, bf16[128,896]{1,0:T(8,128)(2,1)S(1)}, u32[]{:S(2)}, u32[]{:S(2)}) collective-permute-start(bf16[128,896]{1,0:T(8,128)(2,1)S(1)} %get-tuple-element.35.m0), channel_id=1, source_target_pairs={{0,6},{1,7},{2,4},{3,5},{6,0},{7,1},{4,2},{5,3},{12,10},{13,11},{1... | collective-permute-start | bytes 688136 | tf_op jit(solution)/shard_map/ppermute | solution.py:70
  78.3 40.9 %collective-permute-start.9 = (bf16[128,896]{1,0:T(8,128)(2,1)S(1)}, bf16[128,896]{1,0:T(8,128)(2,1)S(1)}, u32[]{:S(2)}, u32[]{:S(2)}) collective-permute-start(bf16[128,896]{1,0:T(8,128)(2,1)S(1)} %get-tuple-element.35.m0), channel_id=1, source_target_pairs={{0,4},{1,5},{2,6},{3,7},{6,2},{7,3},{4,0},{5,1},{12,8},{13,9},{14,... | collective-permute-start | bytes 688136 | tf_op jit(solution)/shard_map/ppermute | solution.py:70
  120.5 7.3 %collective-permute-start.12 = (bf16[256,896]{1,0:T(8,128)(2,1)S(1)}, bf16[256,896]{1,0:T(8,128)(2,1)S(1)}, u32[]{:S(2)}, u32[]{:S(2)}) collective-permute-start(bf16[256,896]{1,0:T(8,128)(2,1)S(1)} %get-tuple-element.36.own_ref.half_ref), channel_id=1, source_target_pairs={{0,1},{1,0},{2,3},{3,2},{6,7},{7,6},{4,5},{5,4},{12,13},{13,12},{1... | collective-permute-start | bytes 1376264 | tf_op jit(solution)/shard_map/ppermute | solution.py:70
  120.6 101.9 %collective-permute-start = (bf16[1024,896]{1,0:T(8,128)(2,1)S(1)}, bf16[1024,896]{1,0:T(8,128)(2,1)S(1)}, u32[]{:S(2)}, u32[]{:S(2)}) collective-permute-start(bf16[1024,896]{1,0:T(8,128)(2,1)S(1)} %bitcast.33), channel_id=1, source_target_pairs={{0,1},{1,0},{2,3},{3,2},{6,7},{7,6},{4,5},{5,4},{12,13},{13,12},{1... | collective-permute-start | bytes 5505032 | tf_op jit(solution)/shard_map/ppermute | solution.py:70
  121.1 16.2 %collective-permute-start.10 = (bf16[256,896]{1,0:T(8,128)(2,1)S(1)}, bf16[256,896]{1,0:T(8,128)(2,1)S(1)}, u32[]{:S(2)}, u32[]{:S(2)}) collective-permute-start(bf16[256,896]{1,0:T(8,128)(2,1)S(1)} %get-tuple-element.36.own_ref.half_ref), channel_id=1, source_target_pairs={{12,0},{13,1},{14,2},{15,3},{10,6},{11,7},{8,4},{9,5},{16,12},{17,... | collective-permute-start | bytes 1376264 | tf_op jit(solution)/shard_map/ppermute | solution.py:90
  122.3 24.2 %collective-permute-start.11 = (bf16[256,896]{1,0:T(8,128)(2,1)S(1)}, bf16[256,896]{1,0:T(8,128)(2,1)S(1)}, u32[]{:S(2)}, u32[]{:S(2)}) collective-permute-start(bf16[256,896]{1,0:T(8,128)(2,1)S(1)} %get-tuple-element.36.own_ref.half_ref), channel_id=1, source_target_pairs={{0,12},{1,13},{2,14},{3,15},{6,10},{7,11},{4,8},{5,9},{12,16},{13,... | collective-permute-start | bytes 1376264 | tf_op jit(solution)/shard_map/ppermute | solution.py:90
  127.8 107.4 %collective-permute-start.20 = (bf16[1024,896]{1,0:T(8,128)(2,1)S(1)}, bf16[1024,896]{1,0:T(8,128)(2,1)S(1)}, u32[]{:S(2)}, u32[]{:S(2)}) collective-permute-start(bf16[1024,896]{1,0:T(8,128)(2,1)S(1)} %bitcast.34), channel_id=1, source_target_pairs={{2,0},{3,1},{6,2},{7,3},{4,6},{5,7},{12,4},{13,5},{14,12},{15,13},... | collective-permute-start | bytes 5505032 | tf_op jit(solution)/shard_map/ppermute | solution.py:70
  137.2 59.5 %collective-permute-start.13 = (bf16[128,896]{1,0:T(8,128)(2,1)S(1)}, bf16[128,896]{1,0:T(8,128)(2,1)S(1)}, u32[]{:S(2)}, u32[]{:S(2)}) collective-permute-start(bf16[128,896]{1,0:T(8,128)(2,1)S(1)} %shard_map.105), channel_id=1, source_target_pairs={{16,0},{17,1},{18,2},{19,3},{22,6},{23,7},{20,4},{21,5},{28,12},{2... | collective-permute-start | bytes 688136 | tf_op jit(solution)/shard_map/ppermute | solution.py:90
  146.5 106.6 %collective-permute-start.24 = (bf16[1024,896]{1,0:T(8,128)(2,1)}, bf16[1024,896]{1,0:T(8,128)(2,1)S(1)}, u32[]{:S(2)}, u32[]{:S(2)}) collective-permute-start(bf16[1024,896]{1,0:T(8,128)(2,1)} %collective-permute-done.23.a1_ref), channel_id=1, source_target_pairs={{0,1},{1,0},{2,3},{3,2},{6,7},{7,6},{4,5},{5,4},{12,13},{13,12},{1... | collective-permute-start | bytes 5505032 | tf_op jit(solution)/shard_map/ppermute | solution.py:70
  146.6 50.1 %collective-permute-start.14 = (bf16[128,896]{1,0:T(8,128)(2,1)S(1)}, bf16[128,896]{1,0:T(8,128)(2,1)S(1)}, u32[]{:S(2)}, u32[]{:S(2)}) collective-permute-start(bf16[128,896]{1,0:T(8,128)(2,1)S(1)} %shard_map.105), channel_id=1, source_target_pairs={{28,0},{29,1},{30,2},{31,3},{26,6},{27,7},{24,4},{25,5},{0,28},{1,... | collective-permute-start | bytes 688136 | tf_op jit(solution)/shard_map/ppermute | solution.py:90
  196.8 53.0 %collective-permute-start.15 = (bf16[768,896]{1,0:T(8,128)(2,1)S(1)}, bf16[768,896]{1,0:T(8,128)(2,1)S(1)}, u32[]{:S(2)}, u32[]{:S(2)}) collective-permute-start(bf16[768,896]{1,0:T(8,128)(2,1)S(1)} %constant_dynamic-update-slice_fusion.2.own_ref), channel_id=1, source_target_pairs={{0,1},{1,0},{2,3},{3,2},{6,7},{7,6},{4,5},{5,4},{12,13},{13,12},{1... | collective-permute-start | bytes 4128776 | tf_op jit(solution)/shard_map/ppermute | solution.py:70
  197.8 6.7 %collective-permute-start.16 = (bf16[128,64]{1,0:T(8,128)(2,1)S(1)}, bf16[128,64]{1,0:T(8,128)(2,1)S(1)}, u32[]{:S(2)}, u32[]{:S(2)}) collective-permute-start(bf16[128,64]{1,0:T(8,128)(2,1)S(1)} %shard_map.106), channel_id=1, source_target_pairs={{12,0},{13,1},{14,2},{15,3},{10,6},{11,7},{8,4},{9,5},{16,12},{17,... | collective-permute-start | bytes 49160 | tf_op jit(solution)/shard_map/ppermute | solution.py:90
  204.5 3.2 %collective-permute-start.17 = (bf16[128,64]{1,0:T(8,128)(2,1)S(1)}, bf16[128,64]{1,0:T(8,128)(2,1)S(1)}, u32[]{:S(2)}, u32[]{:S(2)}) collective-permute-start(bf16[128,64]{1,0:T(8,128)(2,1)S(1)} %shard_map.106), channel_id=1, source_target_pairs={{0,12},{1,13},{2,14},{3,15},{6,10},{7,11},{4,8},{5,9},{12,16},{13,... | collective-permute-start | bytes 49160 | tf_op jit(solution)/shard_map/ppermute | solution.py:90
  207.7 4.9 %collective-permute-start.18 = (bf16[128,64]{1,0:T(8,128)(2,1)S(1)}, bf16[128,64]{1,0:T(8,128)(2,1)S(1)}, u32[]{:S(2)}, u32[]{:S(2)}) collective-permute-start(bf16[128,64]{1,0:T(8,128)(2,1)S(1)} %shard_map.106), channel_id=1, source_target_pairs={{16,0},{17,1},{18,2},{19,3},{22,6},{23,7},{20,4},{21,5},{28,12},{2... | collective-permute-start | bytes 49160 | tf_op jit(solution)/shard_map/ppermute | solution.py:90
  212.6 8.5 %collective-permute-start.19 = (bf16[128,64]{1,0:T(8,128)(2,1)S(1)}, bf16[128,64]{1,0:T(8,128)(2,1)S(1)}, u32[]{:S(2)}, u32[]{:S(2)}) collective-permute-start(bf16[128,64]{1,0:T(8,128)(2,1)S(1)} %shard_map.106), channel_id=1, source_target_pairs={{28,0},{29,1},{30,2},{31,3},{26,6},{27,7},{24,4},{25,5},{0,28},{1,... | collective-permute-start | bytes 49160 | tf_op jit(solution)/shard_map/ppermute | solution.py:90
  221.1 14.1 %collective-permute-start.21 = (bf16[256,64]{1,0:T(8,128)(2,1)S(1)}, bf16[256,64]{1,0:T(8,128)(2,1)S(1)}, u32[]{:S(2)}, u32[]{:S(2)}) collective-permute-start(bf16[256,64]{1,0:T(8,128)(2,1)S(1)} %get-tuple-element.39.wa_ref), channel_id=1, source_target_pairs={{2,0},{3,1},{6,2},{7,3},{4,6},{5,7},{12,4},{13,5},{14,12},{15,13},... | collective-permute-start | bytes 98312 | tf_op jit(solution)/shard_map/ppermute | solution.py:70
  222.5 12.8 %copy-start.5 = (bf16[1024,896]{1,0:T(8,128)(2,1)}, bf16[1024,896]{1,0:T(8,128)(2,1)S(1)}, u32[]{:S(2)}) copy-start(bf16[1024,896]{1,0:T(8,128)(2,1)S(1)} %collective-permute-done.other_ref.a2_ref) | copy-start | bytes 5505028
  222.5 30.7 %collective-permute-start.25 = (bf16[256,64]{1,0:T(8,128)(2,1)S(1)}, bf16[256,64]{1,0:T(8,128)(2,1)S(1)}, u32[]{:S(2)}, u32[]{:S(2)}) collective-permute-start(bf16[256,64]{1,0:T(8,128)(2,1)S(1)} %get-tuple-element.39.wa_ref), channel_id=1, source_target_pairs={{0,2},{1,3},{2,6},{3,7},{6,4},{7,5},{4,12},{5,13},{12,14},{13,15},... | collective-permute-start | bytes 98312 | tf_op jit(solution)/shard_map/ppermute | solution.py:70
  249.7 27.5 %collective-permute-start.22 = (bf16[1024,64]{1,0:T(8,128)(2,1)S(1)}, bf16[1024,64]{1,0:T(8,128)(2,1)S(1)}, u32[]{:S(2)}, u32[]{:S(2)}) collective-permute-start(bf16[1024,64]{1,0:T(8,128)(2,1)S(1)} %get-tuple-element.42), channel_id=1, source_target_pairs={{0,1},{1,0},{2,3},{3,2},{6,7},{7,6},{4,5},{5,4},{12,13},{13,12},{1... | collective-permute-start | bytes 393224 | tf_op jit(solution)/shard_map/ppermute | solution.py:70
  258.3 18.9 %collective-permute-start.26 = (bf16[1024,64]{1,0:T(8,128)(2,1)S(1)}, bf16[1024,64]{1,0:T(8,128)(2,1)S(1)}, u32[]{:S(2)}, u32[]{:S(2)}) collective-permute-start(bf16[1024,64]{1,0:T(8,128)(2,1)S(1)} %get-tuple-element.44), channel_id=1, source_target_pairs={{2,0},{3,1},{6,2},{7,3},{4,6},{5,7},{12,4},{13,5},{14,12},{15,13},... | collective-permute-start | bytes 393224 | tf_op jit(solution)/shard_map/ppermute | solution.py:70
  259.6 17.6 %collective-permute-start.27 = (bf16[1024,64]{1,0:T(8,128)(2,1)S(1)}, bf16[1024,64]{1,0:T(8,128)(2,1)S(1)}, u32[]{:S(2)}, u32[]{:S(2)}) collective-permute-start(bf16[1024,64]{1,0:T(8,128)(2,1)S(1)} %get-tuple-element.45), channel_id=1, source_target_pairs={{2,1},{3,0},{6,3},{7,2},{4,7},{5,6},{12,5},{13,4},{14,13},{15,12},... | collective-permute-start | bytes 393224 | tf_op jit(solution)/shard_map/ppermute | solution.py:70
  260.9 16.3 %collective-permute-start.28 = (bf16[1024,64]{1,0:T(8,128)(2,1)S(1)}, bf16[1024,64]{1,0:T(8,128)(2,1)S(1)}, u32[]{:S(2)}, u32[]{:S(2)}) collective-permute-start(bf16[1024,64]{1,0:T(8,128)(2,1)S(1)} %get-tuple-element.46), channel_id=1, source_target_pairs={{0,2},{1,3},{2,6},{3,7},{6,4},{7,5},{4,12},{5,13},{12,14},{13,15},... | collective-permute-start | bytes 393224 | tf_op jit(solution)/shard_map/ppermute | solution.py:70
  (6 other events, 12.8 us)
where the time goes:
time: 298 us; the launch traced here: 297 us
  waiting for transfers between devices  140 us (47%)
  starting transfers between devices  71.2 us (24%)
  Pallas kernels  51.6 us (17%)
  blocking collectives  18.2 us (6%)
  local copies, waits for them, and re-layouts  10.5 us (4%)
  other arithmetic  5.22 us (2%)
    ppermute x8, waiting for transfers between devices, send_slot(): return lax.ppermute(value, 'leaf', pairs)  63.5 us
    ppermute x16, waiting for transfers between devices, move(): return lax.ppermute(value, 'leaf', pairs)  40.2 us
    ppermute x8, starting transfers between devices, send_slot(): return lax.ppermute(value, 'leaf', pairs)  32.6 us
    ppermute x3, waiting for transfers between devices, local(): lax.ppermute(merge_in, 'leaf', [(i, i ^ 2 * k) for i in range(leaves)])  28 us
    ppermute x16, starting transfers between devices, move(): return lax.ppermute(value, 'leaf', pairs)  26 us
    pallas_call x2, Pallas kernels, pairs(): call(functools.partial(pair_kernel, scale_inv, width, behind_chip, per_le...  18.2 us
    all_to_all x1, blocking collectives, local(): lax.all_to_all(own.astype(BF16), 'leaf', split_axis=0, concat_axis=0, til...  18.2 us
    pallas_call x1, Pallas kernels, local(): call(functools.partial(far_kernel, away, scale_inv), prefetch(2, (blocks...  8.83 us
  transfers between devices with their start and end apart: 30, of which 12 were waited for; matrix products, arithmetic and copies ran while one was open for 2% of the time, Pallas kernels for 15%

commit v1 on v0

v1 whole, which is shorter than its diff:
```python
import functools
import math

import jax
import jax.numpy as jnp
from jax import lax
from jax.experimental import pallas as pl
from jax.experimental.pallas import tpu as pltpu
from jax.sharding import PartitionSpec as P

LEVELS = 4
NWIN = 4
FWIN = 2
GROUP = 8
BF16 = jnp.bfloat16
F32 = jnp.float32
I32 = jnp.int32
NT = (((1,), (1,)), ((), ()))
TN = (((0,), (0,)), ((), ()))
CHUNK = 256


def call(kernel, grid_spec, out_shape, vmem=40, flops=0):
    return pl.pallas_call(
        kernel,
        grid_spec=grid_spec,
        out_shape=out_shape,
        compiler_params=pltpu.CompilerParams(vmem_limit_bytes=vmem * 1024 * 1024),
        cost_estimate=pl.CostEstimate(flops=flops, bytes_accessed=0, transcendentals=0),
    )


def after(value, *others):
    return lax.optimization_barrier((value, *others))[0]


def whole(shape):
    return pl.BlockSpec(shape, lambda *_: (0,) * len(shape))


def shapes(*specs):
    return [jax.ShapeDtypeStruct(shape, kind) for shape, kind in specs]


def mm(a, b):
    return jnp.dot(a, b, preferred_element_type=F32)


def mm_nt(a, b):
    return lax.dot_general(a, b, NT, preferred_element_type=F32)


def mm_tn(a, b):
    return lax.dot_general(a, b, TN, preferred_element_type=F32)


def device_of_leaf(leaf):
    group, chip = leaf // GROUP, (leaf // 2) % 4
    return group * GROUP + ((chip ^ (chip >> 1)) ^ ((group & 1) * 2)) * 2 + leaf % 2


def leaf_of_device(device):
    group, chip = device // GROUP, (device // 2) % 4 ^ ((device // GROUP & 1) * 2)
    return group * GROUP + (chip ^ (chip >> 1)) * 2 + device % 2


def move(value, target_of_leaf):
    leaves = lax.axis_size("leaf")
    pairs = []
    for leaf in range(leaves):
        target = target_of_leaf(leaf)
        if 0 <= target < leaves:
            pairs.append((device_of_leaf(leaf), device_of_leaf(target)))
    return lax.ppermute(value, "leaf", pairs)


def slot_sources(groups):
    slots = []
    for away in range(1, min(6, groups)):
        merge = away > 1 and groups <= 2 * away
        for steps in [(away, -away)] if merge else [(away,), (-away,)]:
            found = [[g + s for s in steps if 0 <= g + s < groups] for g in range(groups)]
            slots.append((away, [f[0] if f else -1 for f in found]))
    return slots


def send_each(value, source):
    pairs = [
        (device_of_leaf(s * GROUP + i), device_of_leaf(g * GROUP + i))
        for g, s in enumerate(source)
        if s >= 0
        for i in range(GROUP)
    ]
    return lax.ppermute(value, "leaf", pairs)


LEAF, CORE, CHIP, NODE, AT, PHYS = range(6)
SLOT0 = 6


def iota(shape, dim):
    return lax.broadcasted_iota(I32, shape, dim)


def sort_kernel(
    rows, per_peer, leaves, lanes, slot_ref, points_ref, weights_ref, skel_ref, merge_ref, near_ref, far_ref,
    send_ref, place_ref, place_s, table_s,
):
    step = pl.program_id(0)
    block = send_ref.shape[0]
    slot = slot_ref[...]

    @pl.when(step == 0)
    def _():
        dest = device_of_leaf(slot // rows)
        at = (iota((leaves, rows), 0) == dest).astype(BF16)
        earlier = (iota((rows, rows), 0) < iota((rows, rows), 1)).astype(BF16)
        rank = jnp.sum(at.astype(F32) * mm(at, earlier), axis=0, keepdims=True)
        place_s[...] = dest * per_peer + rank.astype(I32)
        place_ref[...] = place_s[...]
        skel, merge = skel_ref[...], merge_ref[...]
        end = skel.shape[1] + merge.shape[1]
        second = 2 * skel.shape[1]
        table = jnp.zeros((per_peer, lanes), F32)
        for base, values in (
            (0, skel // 32),
            (skel.shape[1], merge // 32),
            (end, far_ref[...]),
            (second, skel % 32),
            (second + skel.shape[1], merge % 32),
            (second + end, near_ref[...]),
        ):
            count = values.shape[1]
            row = (base + iota((per_peer, count), 1)) // lanes == iota((per_peer, count), 0)
            spread = jnp.where(row, values, 0).astype(F32).astype(BF16)
            fold = ((base + iota((count, lanes), 0)) % lanes == iota((count, lanes), 1)).astype(BF16)
            table += mm(spread, fold)
        table_s[...] = table.astype(BF16)

    pick = (iota((block, rows), 0) + step * block == place_s[...]).astype(BF16)
    width, columns = points_ref.shape[1], weights_ref.shape[0]
    wide = send_ref.shape[1]
    inner = slot % rows
    row = iota((16, rows), 0)
    parts = jnp.where(row == 0, inner // 32, jnp.where(row == 1, inner % 32, 0)).astype(F32).astype(BF16)
    send_ref[:, :width] = mm(pick, points_ref[...]).astype(BF16)
    send_ref[:, width : width + columns] = mm_nt(pick, weights_ref[...]).astype(BF16)
    send_ref[:, width + columns : width + columns + 16] = mm_nt(pick, parts).astype(BF16)
    send_ref[:, width + columns + 16 : wide - lanes] = jnp.zeros((block, wide - lanes - width - columns - 16), BF16)
    spread = (iota((block, per_peer), 0) % per_peer == iota((block, per_peer), 1)).astype(BF16)
    send_ref[:, wide - lanes :] = mm(spread, table_s[...]).astype(BF16)


def tree_rows(extra):
    lane = iota((16, extra.shape[1]), 1)
    parts = jnp.where(lane == 0, 32.0, jnp.where(lane == 1, 1.0, 0.0)).astype(BF16)
    return mm_nt(parts, extra)[0:1].astype(I32)


def entries(table, low, high, leaf):
    lane = iota((1, GROUP), 1)
    return jnp.sum(jnp.where(lane == leaf, table[low:high], 0.0), axis=1, keepdims=True).astype(I32)


def table_of(table_ref, group):
    return jnp.transpose(table_ref[pl.ds(pl.multiple_of(group * GROUP, GROUP), GROUP)])


def bounds(rank):
    ends = [rank]
    for level in range(1, LEVELS + 1):
        ends.append(ends[-1] + (rank >> level))
    return ends


def node_picks(table, rank, level, first, count):
    low, high = bounds(rank)[level - 1 : level + 1]
    rows = high - low
    several = jnp.concatenate([table[low:high]] * count)
    lane = iota((1, GROUP), 1) - first
    row = iota((rows * count, 1), 0) // rows
    return jnp.sum(jnp.where(lane == row, several, 0.0), axis=1, keepdims=True).astype(I32)


def leaf_picks(table, rank, leaf, where):
    skeleton = (entries(table, 0, rank, leaf) == where).astype(BF16)
    index1 = node_picks(table, rank, 1, leaf // 2 * 2, 2) - rank * (leaf % 2)
    return skeleton, (index1 == iota((rank, rank), 1)).astype(BF16)


def level0_kernel(info, got_ref, interp_ref, table_ref, give_ref, keep_ref, weight0_ref):
    rank, columns = weight0_ref.shape
    rows, width = got_ref.shape[0], keep_ref.shape[1]
    half = rank // 2
    where = tree_rows(got_ref[:, width + columns :])
    order = (iota((rows, rows), 0) == where).astype(BF16)
    weights = mm(order, got_ref[:, width : width + columns]).astype(BF16)
    weight0 = mm(interp_ref[...], weights).astype(BF16)
    weight0_ref[...] = weight0
    table = table_of(table_ref, info[AT])
    skeleton, pick1 = leaf_picks(table, rank, info[LEAF] % GROUP, where)
    level0 = mm(skeleton, got_ref[:, :width]).astype(BF16)
    level1 = mm(pick1, level0).astype(BF16)
    core = info[CORE]

    def part(side):
        index2 = node_picks(table, rank, 2, 4 * info[NODE] + 2 * side, 2) - rank * (info[CHIP] % 2)
        return mm((index2 == iota((half, rank), 1)).astype(BF16), level1).astype(BF16)

    keep_ref[...] = part(core)
    give_ref[:, :width] = part(1 - core)
    give_ref[:, width : width + columns] = weight0[:half]
    give_ref[:, width + columns :] = weight0[half:]


def piece(info, pieces_ref, leaf):
    return pieces_ref.at[leaf % 2 ^ info[CORE], leaf // 2 ^ info[PHYS]]


def in_order(core, mine, other):
    return jnp.where(core == 0, jnp.concatenate([mine, other]), jnp.concatenate([other, mine]))


def level1_kernel(info, other_ref, keep_ref, weight0_ref, own_piece_ref, other_piece_ref, out_ref, weight1_ref):
    rank, columns = weight1_ref.shape
    half, width = keep_ref.shape
    core = info[CORE]
    other0 = jnp.concatenate([other_ref[:, width : width + columns], other_ref[:, width + columns :]])
    both0 = in_order(core, weight0_ref[...], other0)
    weight1 = in_order(core, mm(own_piece_ref[...], both0), mm(other_piece_ref[...], both0)).astype(BF16)
    weight1_ref[...] = weight1
    out_ref[:, :width] = keep_ref[...] + other_ref[:, :width]
    out_ref[:, width : width + columns] = weight1[:half]
    out_ref[:, width + columns :] = weight1[half:]


def level23_kernel(info, m0, m1, m2, m3, pieces_ref, out_ref, weight2_ref, weight3_ref, w1_s):
    half = m0.shape[0]
    rank = 2 * half
    columns = weight2_ref.shape[1]
    width = m0.shape[1] - 2 * columns
    core, chip, node = info[CORE], info[CHIP], info[NODE]
    for k, message in enumerate((m0, m1, m2, m3)):
        at = pl.ds(pl.multiple_of((chip ^ k) * rank, rank), rank)
        w1_s[at] = jnp.concatenate([message[:, width : width + columns], message[:, width + columns :]])
    r2, r3 = rank >> 2, rank >> 3
    for n in (0, 1):
        for i in range(4):
            rows2 = piece(info, pieces_ref, 4 * n + i)[:r2]
            at = n * rank + i * r2
            weight2_ref[at : at + r2] = mm(rows2, w1_s[2 * n * rank : 2 * (n + 1) * rank]).astype(BF16)
    low = r2
    weight3 = jnp.concatenate(
        [mm(piece(info, pieces_ref, i)[low : low + r3], weight2_ref[...]) for i in range(GROUP)]
    )
    weight3_ref[...] = weight3.astype(BF16)
    own = m0[:, :width] + m1[:, :width]
    cross = m2[:, :width] + m3[:, :width]
    out_ref[:half, :width] = jnp.where(node == 0, own, cross)
    out_ref[half:, :width] = jnp.where(node == 0, cross, own)
    for n in (0, 1):
        at = pl.ds(pl.multiple_of(n * rank + core * half, half), half)
        out_ref[n * half : (n + 1) * half, width : width + columns] = weight2_ref[at]
    out_ref[:, width + columns :] = weight3.astype(BF16)


def level3_kernel(info, own_ref, other_ref, table_ref, out_ref):
    half = out_ref.shape[0]
    rank = 2 * half
    columns = 64
    width = own_ref.shape[1] - 2 * columns
    core = info[CORE]
    index = node_picks(table_of(table_ref, info[AT]), rank, 3, 4 * core, 4)
    entry = index % rank
    at = index // rank * half + entry % half
    hit = at == iota((half, rank), 1)
    mine = (hit & (entry // half == core)).astype(BF16)
    theirs = (hit & (entry // half != core)).astype(BF16)
    out_ref[:, :width] = (mm(mine, own_ref[:, :width]) + mm(theirs, other_ref[:, :width])).astype(BF16)
    out_ref[:, width : width + columns] = own_ref[:half, width + columns :]
    out_ref[:, width + columns :] = own_ref[half:, width + columns :]


def level4_kernel(info, weight3_ref, next_ref, before_ref, pieces_ref, out_ref):
    rank, columns = weight3_ref.shape
    low = (rank >> 2) + (rank >> 3)
    own = weight3_ref[...]
    sibling = jnp.where(info[AT] % 2 == 0, next_ref[:, columns:], before_ref[:, columns:])
    both = in_order(info[AT] % 2, own, sibling)
    r4 = rank >> 4
    for i in range(GROUP):
        out_ref[i * r4 : (i + 1) * r4] = mm(piece(info, pieces_ref, i)[low : low + r4], both).astype(BF16)


def far_masks(info, mask_ref, leaf, source):
    def at(level, step):
        column = jnp.clip(jnp.where(step < 0, step + FWIN, step + FWIN - 1), 0, 2 * FWIN - 1)
        value = mask_ref[leaf, 2 * NWIN + (level - 1) * 2 * FWIN + column]
        return jnp.where((step != 0) & (jnp.abs(step) <= FWIN) & (source >= 0), value, 0)

    node = 2 * info[AT] + info[NODE]
    return [
        at(2, 2 * source - node),
        at(2, 2 * source + 1 - node),
        at(3, source - info[AT]),
        at(4, source // 2 - info[AT] // 2),
    ]


def row_offset(block, scale_inv):
    squares = jnp.sum(jnp.square(block.astype(F32)), axis=1, keepdims=True)
    return (squares - block.shape[1]) * (0.5 * scale_inv)


def as_row(column):
    return jnp.transpose(jnp.broadcast_to(column, (column.shape[0], 128)))[0:1]


def kernel_block(targets, target_column, sources, source_row, scale_inv):
    products = mm_nt(targets, sources)
    return jnp.exp(products * scale_inv - target_column - source_row).astype(BF16)


def as_bf16(value):
    return value.astype(F32).astype(BF16)


def far_kernel(away, parents, scale_inv, width, info, mask_ref, x1_ref, x2_ref, c1_ref, c2_ref, half_ref, w2_ref, w4_ref, table_ref,
               init1_ref, init2_ref, pairs_ref, *rest):
    parts, (result, out1_ref, out2_ref, w_s, w4_s) = rest[: len(away)], rest[len(away) :]
    columns = out1_ref.shape[1]
    half = half_ref.shape[0] // 2
    rank = 2 * half
    core, node = info[CORE], info[NODE]
    offsets = (c1_ref, c2_ref)
    out1_ref[...] = init1_ref[...]
    out2_ref[...] = init2_ref[...]
    side = [info[LEAF], info[LEAF] ^ 1]

    def run(sources, weights, masks):
        row = as_row(row_offset(sources, scale_inv))
        count = weights.shape[0] // 2
        for x_ref, offset, out_ref, mask in zip((x1_ref, x2_ref), offsets, (out1_ref, out2_ref), masks, strict=True):
            scaled = jnp.concatenate(
                [
                    jnp.concatenate([weights[i * count : (i + 1) * count, j * columns : (j + 1) * columns] * as_bf16(mask[i][j])
                                     for j in range(3)], axis=1)
                    for i in (0, 1)
                ]
            )
            kernel = kernel_block(x_ref[:, :width], offset[...], sources, row, scale_inv)
            sums = mm(kernel, scaled)
            out_ref[...] += sums[:, :columns] + sums[:, columns : 2 * columns] + sums[:, 2 * columns :]

    def spread_of(i, distance, part, source):
        if distance == 1:
            w3 = part[:, width + columns :]
        else:
            w3 = jnp.concatenate([part[:, width : width + columns], part[:, width + columns :]])
        step = source // 2 - info[AT] // 2
        parent = 0 if parents == 1 else jnp.clip(jnp.where(step < 0, step + FWIN, step + FWIN - 1), 0, 2 * FWIN - 1)
        even = source - source % 2
        index = [node_picks(table_of(table_ref, group), rank, 4, 0, GROUP) for group in (even, even + 1)]
        index = jnp.concatenate(index) - rank * (source % 2)
        w4 = in_order(info[AT] % 2, w4_ref[2 * parent], w4_ref[2 * parent + 1])
        w4 = mm_tn((index == iota((rank, rank), 1)).astype(BF16), w4).astype(BF16)
        if distance == 1:
            index3 = node_picks(table_of(table_ref, source), rank, 3, 0, GROUP)
            lane = iota((rank, rank), 1)
            hit = (index3 == lane // half * rank + core * half + lane % half).astype(BF16)
            both = mm_tn(hit, jnp.concatenate([w3, w4], axis=1)).astype(BF16)
            return jnp.concatenate([part[:, width : width + columns], both], axis=1)
        w4_s[:, :columns] = w3
        w4_s[:, columns:] = w4
        rows = pl.ds(pl.multiple_of(core * half, half), half)
        return jnp.concatenate([jnp.zeros((half, columns), BF16), w4_s[rows]], axis=1)

    zero = jnp.zeros((), I32)
    joined = away.index(2) if 2 in away else -1
    for i, distance in enumerate(away):
        source = info[SLOT0 + i]
        known = jnp.maximum(source, 0)
        masks = [far_masks(info, mask_ref, leaf, source) for leaf in side]
        if distance == 1:
            used = sum(sum(m) for m in masks) > 0
            lists = [[[m[0], m[2], m[3]], [m[1], m[2], m[3]]] for m in masks]
        else:
            used = sum(m[2] + m[3] for m in masks) > 0
            lists = [[[zero, m[2], m[3]]] * 2 for m in masks]
        if i != joined:

            @pl.when(used)
            def _(i=i, distance=distance, known=known, lists=lists):
                run(parts[i][:, :width], spread_of(i, distance, parts[i], known), lists)

            continue
        cross = pl.ds(pl.multiple_of((1 - node) * half, half), half)
        column = jnp.where(node == 0, 2 * NWIN + 2 * FWIN + FWIN, 2 * NWIN + 2 * FWIN + FWIN - 1)
        w_s[:half, :columns] = w2_ref[pl.ds(pl.multiple_of((1 - node) * rank + core * half, half), half)]
        w_s[:half, columns:] = jnp.zeros((half, 2 * columns), BF16)
        w_s[half:] = spread_of(i, distance, parts[i], known)
        lists = [
            [[mask_ref[leaf, column], zero, zero], entry[0]] for leaf, entry in zip(side, lists, strict=True)
        ]
        run(jnp.concatenate([half_ref[cross, :width], parts[i][:, :width]]), w_s[...], lists)
    result[:, :columns] = out1_ref[...].astype(BF16)
    result[:, columns : 2 * columns] = out2_ref[...].astype(BF16)
    result[:, 2 * columns :] = pairs_ref[...]


def halves(value):
    half = value.shape[1] // 2
    return value[:, :half] + value[:, half:]


def masked(weights, first, second):
    lane = iota((1, weights.shape[1]), 1)
    return (weights.astype(F32) * jnp.where(lane < weights.shape[1] // 2, first, second)).astype(BF16)


def own_kernel(scale_inv, width, info, mask_ref, own_ref, other_ref, out_ref, back_ref, column_ref, column_other_ref):
    rows, columns = out_ref.shape
    half = rows // 2
    last = width + columns
    own_column = row_offset(own_ref[:, :width], scale_inv)
    other_column = row_offset(other_ref[:, :width], scale_inv)
    column_ref[...] = own_column
    column_other_ref[...] = other_column
    kernel = kernel_block(own_ref[:, :width], own_column, own_ref[:, :width], as_row(own_column), scale_inv)
    out_ref[...] = mm(kernel, own_ref[:, width:last])
    back_ref[...] = jnp.zeros_like(back_ref)
    near = mask_ref[info[LEAF] // 2 * 2, NWIN] > 0

    def pair(first, count):
        mine = own_ref[first:, :width]
        theirs = other_ref[:count, :width]
        kernel = kernel_block(mine, own_column[first:], theirs, as_row(other_column[:count]), scale_inv)
        out_ref[first:] += mm(kernel, other_ref[:count, width:last])
        back_ref[:count] = mm_tn(kernel, own_ref[first:, width:last])

    @pl.when(near & (info[CORE] == 0))
    def _():
        pair(0, half)

    @pl.when(near & (info[CORE] == 1))
    def _():
        pair(half, rows)


def leaf_weights(x, width, columns, weight1, table_ref, leaf):
    rank = weight1.shape[0]
    half = rank // 2
    extra = x[:, width:]
    row = iota((extra.shape[1], 128), 0)
    parts = jnp.where(row == columns, 32.0, jnp.where(row == columns + 1, 1.0, 0.0)).astype(BF16)
    where = mm(extra, parts)
    group = table_ref[pl.ds(pl.multiple_of(leaf // GROUP * GROUP, GROUP), GROUP), : rank + half]
    at = iota((GROUP, 1), 0)

    def of(index, low, high):
        return jnp.sum(jnp.where(at == index, group[:, low:high], 0.0), axis=0, keepdims=True)

    base = leaf % GROUP // 2 * 2
    index1 = jnp.concatenate([of(base + i, rank, rank + half) for i in (0, 1)], axis=1)
    index1 = index1 - (leaf % 2 * rank).astype(F32)
    pick1 = (iota((rank, rank), 0).astype(F32) == index1).astype(BF16)
    level0 = mm(pick1, weight1).astype(BF16)
    skeleton = of(leaf % GROUP, 0, rank)
    hit = [(where == skeleton[:, i : i + 128]).astype(BF16) for i in range(0, rank, 128)]
    spread = mm(jnp.concatenate(hit, axis=1), level0).astype(BF16)
    return jnp.concatenate([extra[:, :columns], spread], axis=1)


def pair_masks(info, mask_ref):
    core = info[CORE]
    chip = info[LEAF] // 2
    leaves = mask_ref.shape[0]
    r_leaf = jnp.minimum(2 * chip + 2, leaves - 2) + core
    level1 = 2 * NWIN
    masks, names = [], []
    for behind in (0, 1):
        for side in (core, 1 - core):
            leaf = jnp.maximum(2 * chip - 2 * behind, 0) + side
            there = (2 * chip + 2 < leaves) & (chip >= behind)
            distance = 2 + 2 * behind + core - side
            near = jnp.where(distance <= NWIN, mask_ref[leaf, jnp.minimum(NWIN - 1 + distance, 2 * NWIN - 1)], 0)
            values = (near, mask_ref[leaf, level1 + FWIN + behind], mask_ref[r_leaf, level1 + FWIN - 1 - behind])
            masks.append([jnp.where(there, v, 0) for v in values])
            names.append(leaf)
    return masks, names, r_leaf


def pair_sums(scale_inv, width, jobs, r, r_row, r_weights, acc):
    sums = []
    for mask, ref, column, weights in jobs:
        near, far_out, far_back = (m.astype(F32) for m in mask)
        kernel = kernel_block(ref[:, :width], column, r, r_row, scale_inv)
        sums.append(halves(mm(kernel, masked(r_weights, near, far_out))))
        acc += mm_tn(masked(weights, near, far_back), kernel)
    return sums, acc


def next_kernel(scale_inv, width, info, mask_ref, q1, q2, c1, c2, r, w_q, w_r, init1, init2, table_ref,
                out1, out2, acc, wr, rr):
    columns = out1.shape[1]
    masks, names, r_leaf = pair_masks(info, mask_ref)
    weights = [
        leaf_weights(ref, width, columns, w_q[...], table_ref, leaf) for ref, leaf in zip((q1, q2), names[:2], strict=True)
    ]
    wr[...] = leaf_weights(r, width, columns, w_r[...], table_ref, r_leaf)
    r_column = row_offset(r[:, :width], scale_inv)
    r_row = as_row(r_column)
    rr[...] = r_row
    jobs = zip(masks[:2], (q1, q2), (c1[...], c2[...]), weights, strict=True)
    sums, total = pair_sums(scale_inv, width, jobs, r[:, :width], r_row, wr[...], jnp.zeros(acc.shape, F32))
    out1[...] = init1[...] + sums[0]
    out2[...] = init2[...] + sums[1]
    acc[...] = total


def before_kernel(scale_inv, width, info, mask_ref, p1, p2, r, w_p, acc, wr, rr, table_ref, result):
    columns = result.shape[1] // 3
    masks, names, _ = pair_masks(info, mask_ref)
    weights = [
        leaf_weights(ref, width, columns, w_p[...], table_ref, leaf) for ref, leaf in zip((p1, p2), names[2:], strict=True)
    ]
    offsets = [row_offset(ref[:, :width], scale_inv) for ref in (p1, p2)]
    jobs = zip(masks[2:], (p1, p2), offsets, weights, strict=True)
    sums, total = pair_sums(scale_inv, width, jobs, r[:, :width], rr[...], wr[...], acc[...])
    for i, value in enumerate((*sums, halves(jnp.transpose(total)))):
        result[:, i * columns : (i + 1) * columns] = value.astype(BF16)


def home_kernel(leaves, place_ref, got_ref, out_ref, sum_s):
    columns, rows = out_ref.shape
    count = rows // leaves
    for leaf in range(leaves):
        sources = (leaf, leaf ^ 1, leaf + 2, (leaf ^ 1) + 2, leaf - 2)
        total = 0.0
        for part, source in enumerate(sources):
            if 0 <= source < leaves:
                at = device_of_leaf(source) * count
                total += got_ref[at : at + count, part * columns : (part + 1) * columns].astype(F32)
        at = device_of_leaf(leaf) * count
        sum_s[at : at + count] = total
    total = sum_s[...]
    high = total.astype(BF16)
    low = (total - high.astype(F32)).astype(BF16)
    pick = (iota((rows, rows), 0) == place_ref[...]).astype(BF16)
    both = mm_tn(jnp.concatenate([high, low], axis=1), pick)
    out_ref[...] = both[:columns] + both[columns:]


def local(
    points, weights, tree_slot, leaf_interp, skel_leaf, merge_interp, merge_index, near_mask, far_mask
):
    leaves = lax.axis_size("leaf")
    groups = leaves // GROUP
    rows, width = points.shape
    columns = weights.shape[1]
    per_peer = rows // leaves
    rank = skel_leaf.shape[1]
    lanes = 4 * rank // per_peer
    wide = width + -(-(columns + 16 + lanes) // 128) * 128
    half = rank // 2
    scale_inv = 1.0 / (1.75 * math.sqrt(width))
    message = width + 2 * columns
    slots = slot_sources(groups)
    away = [a for a, _ in slots]

    def prefetch(count, grid, ins, outs, scratch=()):
        return pltpu.PrefetchScalarGridSpec(
            num_scalar_prefetch=count, grid=grid, in_specs=ins, out_specs=outs, scratch_shapes=scratch
        )

    send, place = call(
        functools.partial(sort_kernel, rows, per_peer, leaves, lanes),
        pl.GridSpec(
            grid=(4,),
            in_specs=[whole((1, rows)), whole((rows, width)), whole((columns, rows))]
            + [whole((1, count)) for count in (rank, merge_index.shape[1], 2 * NWIN, LEVELS * 2 * FWIN)],
            out_specs=[pl.BlockSpec((rows // 4, wide), lambda i: (i, 0)), whole((1, rows))],
            scratch_shapes=[pltpu.VMEM((1, rows), I32), pltpu.VMEM((per_peer, lanes), BF16)],
        ),
        shapes(((rows, wide), BF16), ((1, rows), I32)),
        vmem=62,
    )(tree_slot.reshape(1, rows), points, weights.T, skel_leaf, merge_index, near_mask, far_mask.reshape(1, -1))
    got = lax.all_to_all(send, "leaf", split_axis=0, concat_axis=0, tiled=True)

    device = lax.axis_index("leaf")
    leaf = leaf_of_device(device)
    group = leaf // GROUP
    source = jnp.asarray([s for _, s in slots], I32)[:, group]
    info = jnp.concatenate(
        [jnp.stack([leaf, leaf % 2, leaf // 2 % 4, leaf // 4 % 2, group, device // 2 % 4]).astype(I32), source]
    )
    interp_in, merge_in, _ = lax.optimization_barrier((leaf_interp[0], merge_interp[0], place))
    to_holder = [(i, device_of_leaf(i)) for i in range(leaves)]
    interp = lax.ppermute(interp_in, "leaf", to_holder)
    first = lax.ppermute(merge_in[:half], "leaf", to_holder)
    upper = merge_in[half:]
    uppers = [lax.ppermute(upper, "leaf", [(i, i ^ (2 * k)) for i in range(leaves)]) for k in (1, 2, 3)]
    got, interp, info, first, *uppers = lax.optimization_barrier((got, interp, info, first, *uppers))
    first_other = move(first, lambda i: i ^ 1)
    group_pieces = jnp.stack([upper] + uppers)
    pieces = jnp.stack([group_pieces, move(group_pieces, lambda i: i ^ 1)])
    piece_shape = pieces.shape

    coded = got[:, wide - lanes :].reshape(leaves, 4 * rank).astype(F32)
    tables = coded[:, : 2 * rank] * 32.0 + coded[:, 2 * rank :]
    mask_at = rank + merge_index.shape[1]
    masks = jnp.concatenate(
        [
            coded[:, 2 * rank + mask_at : 2 * rank + mask_at + 2 * NWIN],
            coded[:, mask_at : mask_at + LEVELS * 2 * FWIN],
        ],
        axis=1,
    ).astype(I32)
    table_shape = tables.shape

    other = move(got, lambda i: i ^ 1)
    behind = move(got, lambda i: i + 2)
    ahead = move(got, lambda i: i - 2)

    give, keep, weight0 = call(
        level0_kernel,
        prefetch(1, (), [whole((rows, wide)), whole((rank, rows)), whole(table_shape)],
                 [whole((half, message)), whole((half, width)), whole((rank, columns))]),
        shapes(((half, message), BF16), ((half, width), BF16), ((rank, columns), BF16)),
    )(info, got, interp, tables)
    sent, weight1 = call(
        level1_kernel,
        prefetch(1, (), [whole((half, message)), whole((half, width)), whole((rank, columns))] + [whole((half, 2 * rank))] * 2,
                 [whole((half, message)), whole((rank, columns))]),
        shapes(((half, message), BF16), ((rank, columns), BF16)),
    )(info, move(give, lambda i: i ^ 1), keep, weight0, first, first_other)
    plane = [move(sent, lambda i, k=k: i ^ (2 * k)) for k in (1, 2, 3)]
    own_sum, other_sum, own_column, other_column = call(
        functools.partial(own_kernel, scale_inv, width),
        prefetch(2, (), [whole((rows, wide))] * 2, [whole((rows, columns))] * 2 + [whole((rows, 1))] * 2),
        shapes(*[((rows, columns), F32)] * 2, *[((rows, 1), F32)] * 2),
        flops=3 * rows * rows * width,
    )(info, masks, got, after(other, sent))
    weight1_sent = after(weight1, own_sum)
    behind1 = move(weight1_sent, lambda i: i + 2)
    ahead1 = move(weight1_sent, lambda i: i - 2)

    half2, weight2, weight3 = call(
        level23_kernel,
        prefetch(1, (), [whole((half, message))] * 4 + [whole(piece_shape)],
                 [whole((rank, message)), whole((2 * rank, columns)), whole((rank, columns))],
                 [pltpu.VMEM((4 * rank, columns), BF16)]),
        shapes(((rank, message), BF16), ((2 * rank, columns), BF16), ((rank, columns), BF16)),
    )(info, after(sent, own_sum, behind1, ahead1, behind, ahead), *plane, pieces)
    half2_other = move(half2, lambda i: i ^ 1)
    half3 = call(
        level3_kernel,
        prefetch(1, (), [whole((rank, message))] * 2 + [whole(table_shape)], whole((half, message))),
        jax.ShapeDtypeStruct((half, message), BF16),
    )(info, half2, half2_other, tables)
    far_parts = [send_each(half2 if a == 1 else half3, s) for a, s in slots]
    extra = pl.BlockSpec((rank, 2 * columns), lambda *_: (0, width // (2 * columns)))
    leaf_x, weight_1, sums = whole((rows, wide)), whole((rank, columns)), whole((rows, columns))
    leaf_w, leaf_c, row_c, acc_shape = (rows, 2 * columns), (rows, 1), (1, rows), (2 * columns, rows)
    next_1, next_2, acc, ahead_w, ahead_row = call(
        functools.partial(next_kernel, scale_inv, width),
        prefetch(2, (), [leaf_x] * 2 + [whole(leaf_c)] * 2 + [leaf_x] + [weight_1] * 2 + [sums] * 2 + [whole(table_shape)],
                 [sums] * 2 + [whole(acc_shape), whole(leaf_w), whole(row_c)]),
        shapes(((rows, columns), F32), ((rows, columns), F32), (acc_shape, F32), (leaf_w, BF16), (row_c, F32)),
    )(info, masks, after(got, half3), other, own_column, other_column, ahead, weight1, ahead1, own_sum, other_sum, tables)

    behind_other = move(after(behind, half3), lambda i: i ^ 1)
    pair_sum = call(
        functools.partial(before_kernel, scale_inv, width),
        prefetch(2, (), [leaf_x] * 3 + [weight_1, whole(acc_shape), whole(leaf_w), whole(row_c), whole(table_shape)],
                 whole((rows, 3 * columns))),
        jax.ShapeDtypeStruct((rows, 3 * columns), BF16),
        flops=4 * rows * rows * width,
    )(info, masks, behind, behind_other, ahead, behind1, acc, ahead_w, ahead_row, tables)

    half4 = call(
        level4_kernel,
        prefetch(1, (1,), [whole((rank, columns)), extra, extra, whole(piece_shape)], whole((half, columns))),
        jax.ShapeDtypeStruct((half, columns), BF16),
    )(info, after(weight3, pair_sum), far_parts[0], far_parts[1], pieces)
    nodes4 = groups // 2
    steps4 = [(-1, 1)] if nodes4 == 2 else [(s,) for s in (-2, -1, 1, 2)]
    weight4 = []
    for steps in steps4:
        for h in (0, 1):
            found = [[2 * (g // 2 + s) + (g % 2 ^ h) for s in steps if 0 <= g // 2 + s < nodes4] for g in range(groups)]
            weight4.append(send_each(half4, [f[0] if f else -1 for f in found]))
    weight4 = jnp.stack(weight4)
    all_sums = call(
        functools.partial(far_kernel, away, len(steps4), scale_inv, width),
        prefetch(2, (), [leaf_x] * 2 + [whole(leaf_c)] * 2 + [whole((rank, message)), whole((2 * rank, columns)),
                 whole(weight4.shape), whole(table_shape), sums, sums, whole((rows, 3 * columns))]
                 + [whole(p.shape) for p in far_parts], whole((rows, 5 * columns)),
                 [pltpu.VMEM((rows, columns), F32)] * 2
                 + [pltpu.VMEM((rank, 3 * columns), BF16), pltpu.VMEM((rank, 2 * columns), BF16)]),
        jax.ShapeDtypeStruct((rows, 5 * columns), BF16),
        flops=4 * rows * rows * width,
    )(info, masks, got, other, own_column, other_column, half2, weight2, weight4, tables, next_1, next_2, pair_sum,
      *far_parts)

    home = lax.all_to_all(all_sums, "leaf", split_axis=0, concat_axis=0, tiled=True)
    return call(
        functools.partial(home_kernel, leaves),
        pl.GridSpec(grid=(), in_specs=[whole((1, rows)), whole((rows, 5 * columns))], out_specs=whole((columns, rows)),
                    scratch_shapes=[pltpu.VMEM((rows, columns), F32)]),
        jax.ShapeDtypeStruct((columns, rows), F32),
    )(place, home).T


def solution(mesh):
    placed = (
        P("leaf", None),
        P("leaf", None),
        P("leaf"),
        P("leaf", None, None),
        P("leaf", None),
        P("leaf", None, None),
        P("leaf", None),
        P("leaf", None),
        P("leaf", None, None),
    )
    return jax.shard_map(
        local, mesh=mesh, in_specs=placed, out_specs=P("leaf", None), check_vma=False
    )
```

time: 298 us -> 203 us (0.68)
  waiting for transfers between devices: 140 us -> 67.6 us
  starting transfers between devices: 71.2 us -> 50.8 us
  blocking collectives: 18.2 us -> 25.5 us
  local copies, waits for them, and re-layouts: 10.5 us -> 4.55 us
    ppermute x13 -> x11, waiting for transfers between devices: 91.5 us -> 39.2 us  [the longest x3 32.5 us: local(): lax.ppermute(upper, 'leaf', [(i, i ^ 2 * k) for i in range(leaves)])]
    ppermute x16 -> x13, waiting for transfers between devices: 40.2 us -> 27.6 us  [move(): return lax.ppermute(value, 'leaf', pairs)]
    ppermute x13 -> x11, starting transfers between devices: 37.9 us -> 26.9 us  [the longest x6 17.8 us: send_each(): return lax.ppermute(value, 'leaf', pairs)]
    ppermute x16 -> x13, starting transfers between devices: 26 us -> 16.6 us  [move(): return lax.ppermute(value, 'leaf', pairs)]
    all_to_all x1, waiting for transfers between devices: 8.26 us -> 0.77 us  [local(): got = lax.all_to_all(send, 'leaf', split_axis=0, concat_axis=0, tiled=True)]
    all_to_all x1, blocking collectives: 18.2 us -> 25.5 us  [local(): lax.all_to_all(all_sums, 'leaf', split_axis=0, concat_axis=0, tiled=True)]
    unnamed x22 -> x4, local copies, waits for them, and re-layouts: 6.67 us -> 0.01 us
    pallas_call x6 -> x5, Pallas kernels: 39.7 us -> 34.9 us  [the longest x1 9.94 us: local(): call(functools.partial(before_kernel, scale_inv, width), prefetch(2, (),...]
  transfers between devices with their start and end apart: 30 -> 25, of which waited for: 12 -> 10; matrix products, arithmetic and copies ran while one was open for 2% -> 4% of each run, Pallas kernels for 15% -> 15%
where the time goes in v1:
time: 203 us; the launch traced here: 202 us
  waiting for transfers between devices  67.6 us (33%)
  starting transfers between devices  50.8 us (25%)
  Pallas kernels  49.2 us (24%)
  blocking collectives  25.5 us (13%)
  local copies, waits for them, and re-layouts  4.55 us (2%)
  other arithmetic  3.98 us (2%)
    ppermute x3, waiting for transfers between devices, local(): lax.ppermute(upper, 'leaf', [(i, i ^ 2 * k) for i in range(leaves)])  32.5 us
    ppermute x13, waiting for transfers between devices, move(): return lax.ppermute(value, 'leaf', pairs)  27.6 us
    all_to_all x1, blocking collectives, local(): lax.all_to_all(all_sums, 'leaf', split_axis=0, concat_axis=0, tiled=True)  25.5 us
    ppermute x6, starting transfers between devices, send_each(): return lax.ppermute(value, 'leaf', pairs)  17.8 us
    ppermute x13, starting transfers between devices, move(): return lax.ppermute(value, 'leaf', pairs)  16.6 us
    pallas_call x1, Pallas kernels, local(): call(functools.partial(before_kernel, scale_inv, width), prefetch(2, (),...  9.94 us
    pallas_call x1, Pallas kernels, local(): call(functools.partial(next_kernel, scale_inv, width), prefetch(2, (), [l...  9 us
    pallas_call x1, Pallas kernels, local(): call(functools.partial(far_kernel, away, len(steps4), scale_inv, width),...  7.48 us
  transfers between devices with their start and end apart: 25, of which 10 were waited for; matrix products, arithmetic and copies ran while one was open for 4% of the time, Pallas kernels for 15%

profile of v1, /device:TPU:0, one launch (start us, length us, event | category | flops | bytes accessed | tf_op | source)
XLA Modules:
  0.0 201.8 jit_solution(5182882237016885583)
XLA Ops:
  1.3 6.6 %shard_map.100 = (bf16[1024,896]{1,0:T(8,128)(2,1)}, s32[1,1024]{1,0:T(1,128)}) custom-call(s32[1,1024]{1,0:T(1,128)} %bitcast.45, bf16[1024,768]{1,0:T(8,128)(2,1)} %points_ref.1, bf16[64,1024]{1,0:T(8,128)(2,1)} %bitcast.40, s32[1,256]{1,0:T(1,128)} %skel_ref.1, s32[1,240]{1,0:T(1,128)} %merge_ref.1, s32[1,8]{1,0:T(1,128)} %near_ref.1, ...), custom_call_target="tpu_custom_call" | custom-call | tf_op jit(solution)/shard_map/pallas_call | solution.py:576
  7.9 7.3 %all-to-all-start = ((bf16[32,32,896]{2,1,0:T(8,128)(2,1)}), bf16[32,32,896]{2,1,0:T(8,128)(2,1)S(1)}, u32[]{:S(2)}, u32[]{:S(2)}) async-start(bf16[32,32,896]{2,1,0:T(8,128)(2,1)} %bitcast.37), calls=%async_computation | async-start | bytes 3670016 | tf_op jit(solution)/shard_map/all_to_all | solution.py:588
  15.2 1.7 collective-permute-start
  17.6 1.8 collective-permute-start.2
  19.4 5.0 %collective-permute-start.3 = (bf16[112,512]{1,0:T(8,128)(2,1)S(1)}, bf16[112,512]{1,0:T(8,128)(2,1)S(1)}, u32[]{:S(2)}, u32[]{:S(2)}) collective-permute-start(bf16[112,512]{1,0:T(8,128)(2,1)S(1)} %get-tuple-element.76), channel_id=1, source_target_pairs={{0,4},{1,5},{2,6},{3,7},{4,0},{5,1},{6,2},{7,3},{8,12},{9,13},{10,... | collective-permute-start | bytes 344072 | tf_op jit(solution)/shard_map/ppermute | solution.py:602
  25.2 7.5 %collective-permute-done.2 = bf16[112,512]{1,0:T(8,128)(2,1)S(1)} collective-permute-done((bf16[112,512]{1,0:T(8,128)(2,1)S(1)}, bf16[112,512]{1,0:T(8,128)(2,1)S(1)}, u32[]{:S(2)}, u32[]{:S(2)}) %collective-permute-start.2) | collective-permute-done | bytes 114720 | tf_op jit(solution)/shard_map/ppermute | solution.py:602
  32.6 25.1 %collective-permute-done.4 = bf16[112,512]{1,0:T(8,128)(2,1)} collective-permute-done((bf16[112,512]{1,0:T(8,128)(2,1)S(1)}, bf16[112,512]{1,0:T(8,128)(2,1)}, u32[]{:S(2)}, u32[]{:S(2)}) %collective-permute-start.4) | collective-permute-done | bytes 114720 | tf_op jit(solution)/shard_map/ppermute | solution.py:602
  58.5 4.5 %collective-permute-start.10 = (bf16[1024,896]{1,0:T(8,128)(2,1)S(1)}, bf16[1024,896]{1,0:T(8,128)(2,1)}, u32[]{:S(2)}, u32[]{:S(2)}) collective-permute-start(bf16[1024,896]{1,0:T(8,128)(2,1)S(1)} %bitcast.28), channel_id=1, source_target_pairs={{0,2},{1,3},{2,6},{3,7},{6,4},{7,5},{4,12},{5,13},{12,14},{13,15},... | collective-permute-start | bytes 5505032 | tf_op jit(solution)/shard_map/ppermute | solution.py:74
  62.9 1.3 collective-permute-start.11
  64.2 1.8 fusion
  68.4 3.3 %shard_map.101 = (bf16[128,896]{1,0:T(8,128)(2,1)S(1)}, bf16[128,768]{1,0:T(8,128)(2,1)S(1)}, bf16[256,64]{1,0:T(8,128)(2,1)S(1)}) custom-call(s32[10]{0:T(128)S(1)} %concatenate.6.info, bf16[1024,896]{1,0:T(8,128)(2,1)S(1)} %bitcast.31, bf16[256,1024]{1,0:T(8,128)(2,1)S(1)} %collective-permute-done.interp_ref, f32[32,512]{1,0:T(8,128)S(1)} %slice_add_fusion.table_ref), custom_call_target="tpu_custom_call" | custom-call | tf_op jit(solution)/shard_map/pallas_call | solution.py:625
  74.6 2.5 %collective-permute-start.12 = (bf16[128,896]{1,0:T(8,128)(2,1)S(1)}, bf16[128,896]{1,0:T(8,128)(2,1)S(1)}, u32[]{:S(2)}, u32[]{:S(2)}) collective-permute-start(bf16[128,896]{1,0:T(8,128)(2,1)S(1)} %get-tuple-element.57.m0), channel_id=1, source_target_pairs={{0,2},{1,3},{2,0},{3,1},{6,4},{7,5},{4,6},{5,7},{12,14},{13,15},{1... | collective-permute-start | bytes 688136 | tf_op jit(solution)/shard_map/ppermute | solution.py:74
  77.4 1.3 collective-permute-start.14
  78.7 6.8 %shard_map.103 = (f32[1024,64]{1,0:T(8,128)S(1)}, f32[1024,64]{1,0:T(8,128)S(1)}, f32[1024,1]{1,0:T(8,128)S(1)}, f32[1024,1]{1,0:T(8,128)S(1)}) custom-call(s32[10]{0:T(128)S(1)} %concatenate.6.info, s32[32,24]{1,0:T(8,128)S(1)} %maximum_convert_fusion.mask_ref, bf16[1024,896]{1,0:T(8,128)(2,1)S(1)} %bitcast.32, ...), custom_call_target="tpu_custom_call" | custom-call | flops 2415919104 | tf_op jit(solution)/shard_map/pallas_call | solution.py:638
  85.5 16.5 %collective-permute-done.10.p1 = bf16[1024,896]{1,0:T(8,128)(2,1)} collective-permute-done((bf16[1024,896]{1,0:T(8,128)(2,1)S(1)}, bf16[1024,896]{1,0:T(8,128)(2,1)}, u32[]{:S(2)}, u32[]{:S(2)}) %collective-permute-start.10) | collective-permute-done | bytes 1835040 | tf_op jit(solution)/shard_map/ppermute | solution.py:74
  102.0 4.5 %collective-permute-start.8 = (bf16[256,64]{1,0:T(8,128)(2,1)S(1)}, bf16[256,64]{1,0:T(8,128)(2,1)S(1)}, u32[]{:S(2)}, u32[]{:S(2)}) collective-permute-start(bf16[256,64]{1,0:T(8,128)(2,1)S(1)} %get-tuple-element.56.w_q), channel_id=1, source_target_pairs={{0,2},{1,3},{2,6},{3,7},{6,4},{7,5},{4,12},{5,13},{12,14},{13,15},... | collective-permute-start | bytes 98312 | tf_op jit(solution)/shard_map/ppermute | solution.py:74
  106.5 1.3 collective-permute-done.11.r
  107.8 1.3 collective-permute-start.9
  110.2 2.7 %collective-permute-done.8.w_p = bf16[256,64]{1,0:T(8,128)(2,1)S(1)} collective-permute-done((bf16[256,64]{1,0:T(8,128)(2,1)S(1)}, bf16[256,64]{1,0:T(8,128)(2,1)S(1)}, u32[]{:S(2)}, u32[]{:S(2)}) %collective-permute-start.8) | collective-permute-done | bytes 32800 | tf_op jit(solution)/shard_map/ppermute | solution.py:74
  112.9 5.3 %collective-permute-done.9.w_r = bf16[256,64]{1,0:T(8,128)(2,1)S(1)} collective-permute-done((bf16[256,64]{1,0:T(8,128)(2,1)S(1)}, bf16[256,64]{1,0:T(8,128)(2,1)S(1)}, u32[]{:S(2)}, u32[]{:S(2)}) %collective-permute-start.9) | collective-permute-done | bytes 32800 | tf_op jit(solution)/shard_map/ppermute | solution.py:74
  119.6 1.8 collective-permute-done.16.other_ref
  122.6 1.3 collective-permute-start.18
  123.9 5.5 %collective-permute-start.19 = (bf16[256,896]{1,0:T(8,128)(2,1)S(1)}, bf16[256,896]{1,0:T(8,128)(2,1)S(1)}, u32[]{:S(2)}, u32[]{:S(2)}) collective-permute-start(bf16[256,896]{1,0:T(8,128)(2,1)S(1)} %get-tuple-element.61.own_ref.half_ref), channel_id=1, source_target_pairs={{0,12},{1,13},{2,14},{3,15},{6,10},{7,11},{4,8},{5,9},{12,16},{13,... | collective-permute-start | bytes 1376264 | tf_op jit(solution)/shard_map/ppermute | solution.py:94
  129.9 5.9 %collective-permute-start.23 = (bf16[128,896]{1,0:T(8,128)(2,1)S(1)}, bf16[128,896]{1,0:T(8,128)(2,1)S(1)}, u32[]{:S(2)}, u32[]{:S(2)}) collective-permute-start(bf16[128,896]{1,0:T(8,128)(2,1)S(1)} %shard_map.105), channel_id=1, source_target_pairs={{28,0},{29,1},{30,2},{31,3},{26,6},{27,7},{24,4},{25,5},{0,28},{1,... | collective-permute-start | bytes 688136 | tf_op jit(solution)/shard_map/ppermute | solution.py:94
  135.8 9.0 %shard_map.106 = (f32[1024,64]{1,0:T(8,128)S(1)}, f32[1024,64]{1,0:T(8,128)S(1)}, f32[128,1024]{1,0:T(8,128)S(1)}, bf16[1024,128]{1,0:T(8,128)(2,1)S(1)}, f32[1,1024]{1,0:T(1,128)S(1)}) custom-call(s32[10]{0:T(128)S(1)} %concatenate.6.info, s32[32,24]{1,0:T(8,128)S(1)} %maximum_convert_fusion.mask_ref, bf16[1024,896]{1,0:T(8,128)(2,1)S(1)} %bitcast.33, ...), custom_call_target="tpu_custom_call" | custom-call | tf_op jit(solution)/shard_map/pallas_call | solution.py:665
  144.8 9.9 %shard_map.107.pairs_ref = bf16[1024,192]{1,0:T(8,128)(2,1)S(1)} custom-call(s32[10]{0:T(128)S(1)} %concatenate.6.info, s32[32,24]{1,0:T(8,128)S(1)} %maximum_convert_fusion.mask_ref, bf16[1024,896]{1,0:T(8,128)(2,1)} %collective-permute-done.10.p1, bf16[1024,896]{1,0:T(8,128)(2,1)S(1)} %collective-permute-done.17.p2, ...), custom_call_target="tpu_custom_call" | custom-call | flops 3221225472 | tf_op jit(solution)/shard_map/pallas_call | solution.py:673
  155.9 4.6 %collective-permute-start.20 = (bf16[128,64]{1,0:T(8,128)(2,1)S(1)}, bf16[128,64]{1,0:T(8,128)(2,1)S(1)}, u32[]{:S(2)}, u32[]{:S(2)}) collective-permute-start(bf16[128,64]{1,0:T(8,128)(2,1)S(1)} %shard_map.108), channel_id=1, source_target_pairs={{16,0},{17,1},{18,2},{19,3},{22,6},{23,7},{20,4},{21,5},{28,12},{2... | collective-permute-start | bytes 49160 | tf_op jit(solution)/shard_map/ppermute | solution.py:94
  160.5 1.9 collective-permute-done.20
  162.4 4.7 %collective-permute-done.21 = bf16[128,64]{1,0:T(8,128)(2,1)S(1)} collective-permute-done((bf16[128,64]{1,0:T(8,128)(2,1)S(1)}, bf16[128,64]{1,0:T(8,128)(2,1)S(1)}, u32[]{:S(2)}, u32[]{:S(2)}) %collective-permute-start.21) | collective-permute-done | bytes 16416 | tf_op jit(solution)/shard_map/ppermute | solution.py:94
  167.2 7.5 %shard_map.109 = bf16[1024,320]{1,0:T(8,128)(2,1)S(1)} custom-call(s32[10]{0:T(128)S(1)} %concatenate.6.info, s32[32,24]{1,0:T(8,128)S(1)} %maximum_convert_fusion.mask_ref, bf16[1024,896]{1,0:T(8,128)(2,1)S(1)} %bitcast.34, bf16[1024,896]{1,0:T(8,128)(2,1)} %collective-permute-done.5.other_ref.q2.x2_ref, f32[1024,1]{1,0:T(8,128)S(1)} %get-tuple-element.52.c1.c1_ref, ...), custom_call_target="tpu_custom_call" | custom-call | flops 3221225472 | tf_op jit(solution)/shard_map/pallas_call | solution.py:694
  174.7 25.5 %all_to_all.23 = bf16[32,32,320]{2,1,0:T(8,128)(2,1)S(1)} all-to-all(bf16[32,32,320]{2,1,0:T(8,128)(2,1)S(1)} %bitcast.36), channel_id=1, replica_groups=mesh['leaf'=32] {'leaf'}, dimensions={0} | all-to-all | bytes 1310720 | tf_op jit(solution)/shard_map/all_to_all | solution.py:706
  200.1 1.6 shard_map.110
  (48 shorter events, 14.4 us)
Async XLA Ops:
  7.9 9.0 %copy-start.1 = (bf16[1,240,512]{2,1,0:T(8,128)(2,1)S(1)}, bf16[1,240,512]{2,1,0:T(8,128)(2,1)}, u32[]{:S(2)}) copy-start(bf16[1,240,512]{2,1,0:T(8,128)(2,1)} %param.15) | copy-start | bytes 737284
  7.9 50.6 %all-to-all-start = ((bf16[32,32,896]{2,1,0:T(8,128)(2,1)}), bf16[32,32,896]{2,1,0:T(8,128)(2,1)S(1)}, u32[]{:S(2)}, u32[]{:S(2)}) async-start(bf16[32,32,896]{2,1,0:T(8,128)(2,1)} %bitcast.37), calls=%async_computation | async-start | bytes 3670016 | tf_op jit(solution)/shard_map/all_to_all | solution.py:588
  15.2 42.5 %collective-permute-start = (bf16[256,1024]{1,0:T(8,128)(2,1)}, bf16[256,1024]{1,0:T(8,128)(2,1)S(1)}, u32[]{:S(2)}, u32[]{:S(2)}) collective-permute-start(bf16[256,1024]{1,0:T(8,128)(2,1)} %bitcast.4), channel_id=1, source_target_pairs={{0,0},{1,1},{2,2},{3,3},{4,6},{5,7},{6,4},{7,5},{8,12},{9,13},{10,... | collective-permute-start | bytes 1572872 | tf_op jit(solution)/shard_map/ppermute | solution.py:599
  16.9 40.8 %collective-permute-start.1 = (bf16[128,512]{1,0:T(8,128)(2,1)S(1)}, bf16[128,512]{1,0:T(8,128)(2,1)S(1)}, u32[]{:S(2)}, u32[]{:S(2)}) collective-permute-start(bf16[128,512]{1,0:T(8,128)(2,1)S(1)} %slice.21), channel_id=1, source_target_pairs={{0,0},{1,1},{2,2},{3,3},{4,6},{5,7},{6,4},{7,5},{8,12},{9,13},{10,... | collective-permute-start | bytes 393224 | tf_op jit(solution)/shard_map/ppermute | solution.py:600
  17.6 15.0 %collective-permute-start.2 = (bf16[112,512]{1,0:T(8,128)(2,1)S(1)}, bf16[112,512]{1,0:T(8,128)(2,1)S(1)}, u32[]{:S(2)}, u32[]{:S(2)}) collective-permute-start(bf16[112,512]{1,0:T(8,128)(2,1)S(1)} %get-tuple-element.76), channel_id=1, source_target_pairs={{0,2},{1,3},{2,0},{3,1},{4,6},{5,7},{6,4},{7,5},{8,10},{9,11},{10,... | collective-permute-start | bytes 344072 | tf_op jit(solution)/shard_map/ppermute | solution.py:602
  19.4 13.2 %collective-permute-start.3 = (bf16[112,512]{1,0:T(8,128)(2,1)S(1)}, bf16[112,512]{1,0:T(8,128)(2,1)S(1)}, u32[]{:S(2)}, u32[]{:S(2)}) collective-permute-start(bf16[112,512]{1,0:T(8,128)(2,1)S(1)} %get-tuple-element.76), channel_id=1, source_target_pairs={{0,4},{1,5},{2,6},{3,7},{4,0},{5,1},{6,2},{7,3},{8,12},{9,13},{10,... | collective-permute-start | bytes 344072 | tf_op jit(solution)/shard_map/ppermute | solution.py:602
  24.4 33.3 %collective-permute-start.4 = (bf16[112,512]{1,0:T(8,128)(2,1)S(1)}, bf16[112,512]{1,0:T(8,128)(2,1)}, u32[]{:S(2)}, u32[]{:S(2)}) collective-permute-start(bf16[112,512]{1,0:T(8,128)(2,1)S(1)} %get-tuple-element.76), channel_id=1, source_target_pairs={{0,6},{1,7},{2,4},{3,5},{4,2},{5,3},{6,0},{7,1},{8,14},{9,15},{10,... | collective-permute-start | bytes 344072 | tf_op jit(solution)/shard_map/ppermute | solution.py:602
  58.5 18.6 %collective-permute-start.5 = (bf16[1024,896]{1,0:T(8,128)(2,1)S(1)}, bf16[1024,896]{1,0:T(8,128)(2,1)}, u32[]{:S(2)}, u32[]{:S(2)}) collective-permute-start(bf16[1024,896]{1,0:T(8,128)(2,1)S(1)} %bitcast.27), channel_id=1, source_target_pairs={{0,1},{1,0},{2,3},{3,2},{6,7},{7,6},{4,5},{5,4},{12,13},{13,12},{1... | collective-permute-start | bytes 5505032 | tf_op jit(solution)/shard_map/ppermute | solution.py:74
  58.5 43.5 %collective-permute-start.10 = (bf16[1024,896]{1,0:T(8,128)(2,1)S(1)}, bf16[1024,896]{1,0:T(8,128)(2,1)}, u32[]{:S(2)}, u32[]{:S(2)}) collective-permute-start(bf16[1024,896]{1,0:T(8,128)(2,1)S(1)} %bitcast.28), channel_id=1, source_target_pairs={{0,2},{1,3},{2,6},{3,7},{6,4},{7,5},{4,12},{5,13},{12,14},{13,15},... | collective-permute-start | bytes 5505032 | tf_op jit(solution)/shard_map/ppermute | solution.py:74
  62.9 44.8 %collective-permute-start.11 = (bf16[1024,896]{1,0:T(8,128)(2,1)S(1)}, bf16[1024,896]{1,0:T(8,128)(2,1)}, u32[]{:S(2)}, u32[]{:S(2)}) collective-permute-start(bf16[1024,896]{1,0:T(8,128)(2,1)S(1)} %bitcast.29), channel_id=1, source_target_pairs={{2,0},{3,1},{6,2},{7,3},{4,6},{5,7},{12,4},{13,5},{14,12},{15,13},... | collective-permute-start | bytes 5505032 | tf_op jit(solution)/shard_map/ppermute | solution.py:74
  66.0 11.4 %collective-permute-start.15 = (bf16[4,112,512]{2,1,0:T(8,128)(2,1)}, bf16[4,112,512]{2,1,0:T(8,128)(2,1)}, u32[]{:S(2)}, u32[]{:S(2)}) collective-permute-start(bf16[4,112,512]{2,1,0:T(8,128)(2,1)} %get-tuple-element.74), channel_id=1, source_target_pairs={{0,1},{1,0},{2,3},{3,2},{6,7},{7,6},{4,5},{5,4},{12,13},{13,12},{1... | collective-permute-start | bytes 1376264 | tf_op jit(solution)/shard_map/ppermute | solution.py:74
  67.2 4.5 %collective-permute-start.7 = (bf16[128,512]{1,0:T(8,128)(2,1)S(1)}, bf16[128,512]{1,0:T(8,128)(2,1)S(1)}, u32[]{:S(2)}, u32[]{:S(2)}) collective-permute-start(bf16[128,512]{1,0:T(8,128)(2,1)S(1)} %collective-permute-done.1.own_piece_ref), channel_id=1, source_target_pairs={{0,1},{1,0},{2,3},{3,2},{6,7},{7,6},{4,5},{5,4},{12,13},{13,12},{1... | collective-permute-start | bytes 393224 | tf_op jit(solution)/shard_map/ppermute | solution.py:74
  71.8 2.0 collective-permute-start.6
  74.6 43.6 %collective-permute-start.12 = (bf16[128,896]{1,0:T(8,128)(2,1)S(1)}, bf16[128,896]{1,0:T(8,128)(2,1)S(1)}, u32[]{:S(2)}, u32[]{:S(2)}) collective-permute-start(bf16[128,896]{1,0:T(8,128)(2,1)S(1)} %get-tuple-element.57.m0), channel_id=1, source_target_pairs={{0,2},{1,3},{2,0},{3,1},{6,4},{7,5},{4,6},{5,7},{12,14},{13,15},{1... | collective-permute-start | bytes 688136 | tf_op jit(solution)/shard_map/ppermute | solution.py:74
  77.1 41.1 %collective-permute-start.13 = (bf16[128,896]{1,0:T(8,128)(2,1)S(1)}, bf16[128,896]{1,0:T(8,128)(2,1)S(1)}, u32[]{:S(2)}, u32[]{:S(2)}) collective-permute-start(bf16[128,896]{1,0:T(8,128)(2,1)S(1)} %get-tuple-element.57.m0), channel_id=1, source_target_pairs={{0,6},{1,7},{2,4},{3,5},{6,0},{7,1},{4,2},{5,3},{12,10},{13,11},{1... | collective-permute-start | bytes 688136 | tf_op jit(solution)/shard_map/ppermute | solution.py:74
  77.4 40.9 %collective-permute-start.14 = (bf16[128,896]{1,0:T(8,128)(2,1)S(1)}, bf16[128,896]{1,0:T(8,128)(2,1)S(1)}, u32[]{:S(2)}, u32[]{:S(2)}) collective-permute-start(bf16[128,896]{1,0:T(8,128)(2,1)S(1)} %get-tuple-element.57.m0), channel_id=1, source_target_pairs={{0,4},{1,5},{2,6},{3,7},{6,2},{7,3},{4,0},{5,1},{12,8},{13,9},{14,... | collective-permute-start | bytes 688136 | tf_op jit(solution)/shard_map/ppermute | solution.py:74
  102.0 10.9 %collective-permute-start.8 = (bf16[256,64]{1,0:T(8,128)(2,1)S(1)}, bf16[256,64]{1,0:T(8,128)(2,1)S(1)}, u32[]{:S(2)}, u32[]{:S(2)}) collective-permute-start(bf16[256,64]{1,0:T(8,128)(2,1)S(1)} %get-tuple-element.56.w_q), channel_id=1, source_target_pairs={{0,2},{1,3},{2,6},{3,7},{6,4},{7,5},{4,12},{5,13},{12,14},{13,15},... | collective-permute-start | bytes 98312 | tf_op jit(solution)/shard_map/ppermute | solution.py:74
  107.8 10.4 %collective-permute-start.9 = (bf16[256,64]{1,0:T(8,128)(2,1)S(1)}, bf16[256,64]{1,0:T(8,128)(2,1)S(1)}, u32[]{:S(2)}, u32[]{:S(2)}) collective-permute-start(bf16[256,64]{1,0:T(8,128)(2,1)S(1)} %get-tuple-element.56.w_q), channel_id=1, source_target_pairs={{2,0},{3,1},{6,2},{7,3},{4,6},{5,7},{12,4},{13,5},{14,12},{15,13},... | collective-permute-start | bytes 98312 | tf_op jit(solution)/shard_map/ppermute | solution.py:74
  119.5 1.9 collective-permute-start.16
  122.4 22.4 %collective-permute-start.17 = (bf16[1024,896]{1,0:T(8,128)(2,1)}, bf16[1024,896]{1,0:T(8,128)(2,1)S(1)}, u32[]{:S(2)}, u32[]{:S(2)}) collective-permute-start(bf16[1024,896]{1,0:T(8,128)(2,1)} %collective-permute-done.10.p1), channel_id=1, source_target_pairs={{0,1},{1,0},{2,3},{3,2},{6,7},{7,6},{4,5},{5,4},{12,13},{13,12},{1... | collective-permute-start | bytes 5505032 | tf_op jit(solution)/shard_map/ppermute | solution.py:74
  122.6 32.1 %collective-permute-start.18 = (bf16[256,896]{1,0:T(8,128)(2,1)S(1)}, bf16[256,896]{1,0:T(8,128)(2,1)S(1)}, u32[]{:S(2)}, u32[]{:S(2)}) collective-permute-start(bf16[256,896]{1,0:T(8,128)(2,1)S(1)} %get-tuple-element.61.own_ref.half_ref), channel_id=1, source_target_pairs={{12,0},{13,1},{14,2},{15,3},{10,6},{11,7},{8,4},{9,5},{16,12},{17,... | collective-permute-start | bytes 1376264 | tf_op jit(solution)/shard_map/ppermute | solution.py:94
  123.9 30.9 %collective-permute-start.19 = (bf16[256,896]{1,0:T(8,128)(2,1)S(1)}, bf16[256,896]{1,0:T(8,128)(2,1)S(1)}, u32[]{:S(2)}, u32[]{:S(2)}) collective-permute-start(bf16[256,896]{1,0:T(8,128)(2,1)S(1)} %get-tuple-element.61.own_ref.half_ref), channel_id=1, source_target_pairs={{0,12},{1,13},{2,14},{3,15},{6,10},{7,11},{4,8},{5,9},{12,16},{13,... | collective-permute-start | bytes 1376264 | tf_op jit(solution)/shard_map/ppermute | solution.py:94
  129.4 37.8 %collective-permute-start.22 = (bf16[128,896]{1,0:T(8,128)(2,1)S(1)}, bf16[128,896]{1,0:T(8,128)(2,1)S(1)}, u32[]{:S(2)}, u32[]{:S(2)}) collective-permute-start(bf16[128,896]{1,0:T(8,128)(2,1)S(1)} %shard_map.105), channel_id=1, source_target_pairs={{16,0},{17,1},{18,2},{19,3},{22,6},{23,7},{20,4},{21,5},{28,12},{2... | collective-permute-start | bytes 688136 | tf_op jit(solution)/shard_map/ppermute | solution.py:94
  129.9 37.3 %collective-permute-start.23 = (bf16[128,896]{1,0:T(8,128)(2,1)S(1)}, bf16[128,896]{1,0:T(8,128)(2,1)S(1)}, u32[]{:S(2)}, u32[]{:S(2)}) collective-permute-start(bf16[128,896]{1,0:T(8,128)(2,1)S(1)} %shard_map.105), channel_id=1, source_target_pairs={{28,0},{29,1},{30,2},{31,3},{26,6},{27,7},{24,4},{25,5},{0,28},{1,... | collective-permute-start | bytes 688136 | tf_op jit(solution)/shard_map/ppermute | solution.py:94
  155.9 6.5 %collective-permute-start.20 = (bf16[128,64]{1,0:T(8,128)(2,1)S(1)}, bf16[128,64]{1,0:T(8,128)(2,1)S(1)}, u32[]{:S(2)}, u32[]{:S(2)}) collective-permute-start(bf16[128,64]{1,0:T(8,128)(2,1)S(1)} %shard_map.108), channel_id=1, source_target_pairs={{16,0},{17,1},{18,2},{19,3},{22,6},{23,7},{20,4},{21,5},{28,12},{2... | collective-permute-start | bytes 49160 | tf_op jit(solution)/shard_map/ppermute | solution.py:94
  160.5 6.6 %collective-permute-start.21 = (bf16[128,64]{1,0:T(8,128)(2,1)S(1)}, bf16[128,64]{1,0:T(8,128)(2,1)S(1)}, u32[]{:S(2)}, u32[]{:S(2)}) collective-permute-start(bf16[128,64]{1,0:T(8,128)(2,1)S(1)} %shard_map.108), channel_id=1, source_target_pairs={{28,0},{29,1},{30,2},{31,3},{26,6},{27,7},{24,4},{25,5},{16,12},{1... | collective-permute-start | bytes 49160 | tf_op jit(solution)/shard_map/ppermute | solution.py:94
  167.2 32.9 %copy-start = (s32[1,1024]{1,0:T(1,128)S(1)}, s32[1,1024]{1,0:T(1,128)}, u32[]{:S(2)}) copy-start(s32[1,1024]{1,0:T(1,128)} %get-tuple-element.39.place_ref) | copy-start | bytes 12292

commit v2 on v1

--- a/solution.py
+++ b/solution.py
@@ -85,12 +85,7 @@
 
 
 def send_each(value, source):
-    pairs = [
-        (device_of_leaf(s * GROUP + i), device_of_leaf(g * GROUP + i))
-        for g, s in enumerate(source)
-        if s >= 0
-        for i in range(GROUP)
-    ]
+    pairs = [(s * GROUP + i, g * GROUP + i) for g, s in enumerate(source) if s >= 0 for i in range(GROUP)]
     return lax.ppermute(value, "leaf", pairs)
 
 
@@ -107,7 +102,7 @@
     send_ref, place_ref, place_s, table_s,
 ):
     step = pl.program_id(0)
-    block = send_ref.shape[0]
+    block, wide = send_ref.shape
     slot = slot_ref[...]
 
     @pl.when(step == 0)
@@ -125,7 +120,7 @@
         for base, values in (
             (0, skel // 32),
             (skel.shape[1], merge // 32),
-            (end, far_ref[...]),
+            *((end + 2 * FWIN * i, far_ref[0, i : i + 1]) for i in range(LEVELS)),
             (second, skel % 32),
             (second + skel.shape[1], merge % 32),
             (second + end, near_ref[...]),
@@ -139,16 +134,25 @@
 
     pick = (iota((block, rows), 0) + step * block == place_s[...]).astype(BF16)
     width, columns = points_ref.shape[1], weights_ref.shape[0]
-    wide = send_ref.shape[1]
     inner = slot % rows
     row = iota((16, rows), 0)
     parts = jnp.where(row == 0, inner // 32, jnp.where(row == 1, inner % 32, 0)).astype(F32).astype(BF16)
-    send_ref[:, :width] = mm(pick, points_ref[...]).astype(BF16)
-    send_ref[:, width : width + columns] = mm_nt(pick, weights_ref[...]).astype(BF16)
-    send_ref[:, width + columns : width + columns + 16] = mm_nt(pick, parts).astype(BF16)
-    send_ref[:, width + columns + 16 : wide - lanes] = jnp.zeros((block, wide - lanes - width - columns - 16), BF16)
     spread = (iota((block, per_peer), 0) % per_peer == iota((block, per_peer), 1)).astype(BF16)
-    send_ref[:, wide - lanes :] = mm(spread, table_s[...]).astype(BF16)
+    values = (
+        (0, mm(pick, points_ref[...])),
+        (width, mm_nt(pick, weights_ref[...])),
+        (width + columns, mm_nt(pick, parts)),
+        (width + columns + 16, jnp.zeros((block, wide - lanes - width - columns - 16), F32)),
+        (wide - lanes, mm(spread, table_s[...])),
+    )
+    for at, value in values:
+        send_ref[:, at : at + value.shape[1]] = value.astype(BF16)
+
+
+def join(whole_ref, first_ref, second_ref):
+    cut = first_ref.shape[0]
+    whole_ref[:cut] = first_ref[...]
+    whole_ref[cut:] = second_ref[...]
 
 
 def tree_rows(extra):
@@ -284,9 +288,8 @@
 def level4_kernel(info, weight3_ref, next_ref, before_ref, pieces_ref, out_ref):
     rank, columns = weight3_ref.shape
     low = (rank >> 2) + (rank >> 3)
-    own = weight3_ref[...]
     sibling = jnp.where(info[AT] % 2 == 0, next_ref[:, columns:], before_ref[:, columns:])
-    both = in_order(info[AT] % 2, own, sibling)
+    both = in_order(info[AT] % 2, weight3_ref[...], sibling)
     r4 = rank >> 4
     for i in range(GROUP):
         out_ref[i * r4 : (i + 1) * r4] = mm(piece(info, pieces_ref, i)[low : low + r4], both).astype(BF16)
@@ -325,9 +328,10 @@
     return value.astype(F32).astype(BF16)
 
 
-def far_kernel(away, parents, scale_inv, width, info, mask_ref, x1_ref, x2_ref, c1_ref, c2_ref, half_ref, w2_ref, w4_ref, table_ref,
+def far_kernel(away, parents, sides, share, scale_inv, width, info, mask_ref, x1_ref, x2_ref, c1_ref, c2_ref, half_ref, w2_ref, table_ref,
                init1_ref, init2_ref, pairs_ref, *rest):
-    parts, (result, out1_ref, out2_ref, w_s, w4_s) = rest[: len(away)], rest[len(away) :]
+    parts, rest = rest[: len(away)], rest[len(away) :]
+    w4_refs, (result, out1_ref, out2_ref, w_s, w4_s) = rest[: 2 * parents], rest[2 * parents :]
     columns = out1_ref.shape[1]
     half = half_ref.shape[0] // 2
     rank = 2 * half
@@ -358,11 +362,15 @@
         else:
             w3 = jnp.concatenate([part[:, width : width + columns], part[:, width + columns :]])
         step = source // 2 - info[AT] // 2
-        parent = 0 if parents == 1 else jnp.clip(jnp.where(step < 0, step + FWIN, step + FWIN - 1), 0, 2 * FWIN - 1)
+        parent = jnp.clip(jnp.where(step < 0, step + FWIN, step + FWIN - 1), 0, 2 * FWIN - 1)
+        same, cross = w4_refs[0][...], w4_refs[1][...]
+        for k in range(1, parents):
+            same = jnp.where(parent == k, w4_refs[2 * k][...], same)
+            cross = jnp.where(parent == k, w4_refs[2 * k + 1][...], cross)
         even = source - source % 2
         index = [node_picks(table_of(table_ref, group), rank, 4, 0, GROUP) for group in (even, even + 1)]
         index = jnp.concatenate(index) - rank * (source % 2)
-        w4 = in_order(info[AT] % 2, w4_ref[2 * parent], w4_ref[2 * parent + 1])
+        w4 = in_order(info[AT] % 2, same, cross)
         w4 = mm_tn((index == iota((rank, rank), 1)).astype(BF16), w4).astype(BF16)
         if distance == 1:
             index3 = node_picks(table_of(table_ref, source), rank, 3, 0, GROUP)
@@ -403,9 +411,15 @@
             [[mask_ref[leaf, column], zero, zero], entry[0]] for leaf, entry in zip(side, lists, strict=True)
         ]
         run(jnp.concatenate([half_ref[cross, :width], parts[i][:, :width]]), w_s[...], lists)
-    result[:, :columns] = out1_ref[...].astype(BF16)
-    result[:, columns : 2 * columns] = out2_ref[...].astype(BF16)
-    result[:, 2 * columns :] = pairs_ref[...]
+    parts = (out1_ref[...].astype(BF16), out2_ref[...].astype(BF16), pairs_ref[...])
+    at = 0
+    for i in range(sides):
+        for value in parts:
+            lanes = value.shape[1]
+            if sides == 2:
+                value = value.reshape(-1, 2, share, lanes)[:, i].reshape(-1, lanes)
+            result[:, at : at + lanes] = value
+            at += lanes
 
 
 def halves(value):
@@ -500,49 +514,51 @@
     return sums, acc
 
 
-def next_kernel(scale_inv, width, info, mask_ref, q1, q2, c1, c2, r, w_q, w_r, init1, init2, table_ref,
-                out1, out2, acc, wr, rr):
+def pair_kernel(scale_inv, width, info, mask_ref, q1, q2, c1, c2, p1a, p1b, p2a, p2b, ra, rb, w_all, w_cross,
+                init1, init2, table_ref, out1, out2, result, p1, p2, r):
+    for ref, parts in ((p1, (p1a, p1b)), (p2, (p2a, p2b)), (r, (ra, rb))):
+        join(ref, *parts)
     columns = out1.shape[1]
     masks, names, r_leaf = pair_masks(info, mask_ref)
-    weights = [
-        leaf_weights(ref, width, columns, w_q[...], table_ref, leaf) for ref, leaf in zip((q1, q2), names[:2], strict=True)
-    ]
-    wr[...] = leaf_weights(r, width, columns, w_r[...], table_ref, r_leaf)
-    r_column = row_offset(r[:, :width], scale_inv)
-    r_row = as_row(r_column)
-    rr[...] = r_row
-    jobs = zip(masks[:2], (q1, q2), (c1[...], c2[...]), weights, strict=True)
-    sums, total = pair_sums(scale_inv, width, jobs, r[:, :width], r_row, wr[...], jnp.zeros(acc.shape, F32))
+    refs = (q1, q2, p1, p2)
+    chip, rank = info[CHIP], w_cross.shape[0]
+    last = w_all.shape[0] // rank - 1
+
+    def of(index, inside):
+        at = pl.ds(pl.multiple_of(jnp.clip(index, 0, last) * rank, rank), rank)
+        return jnp.where(inside, w_all[at], w_cross[...])
+
+    w_q, w_p, w_r = of(chip, True), of(chip - 1, chip > 0), of(chip + 1, chip < last)
+    r_weights = leaf_weights(r, width, columns, w_r, table_ref, r_leaf)
+    r_row = as_row(row_offset(r[:, :width], scale_inv))
+    acc = jnp.zeros((2 * columns, r.shape[0]), F32)
+    sums = []
+    for i, (mask, ref, leaf) in enumerate(zip(masks, refs, names, strict=True)):
+        weights = leaf_weights(ref, width, columns, w_q if i < 2 else w_p, table_ref, leaf)
+        column = (c1, c2)[i][...] if i < 2 else row_offset(ref[:, :width], scale_inv)
+        near, far_out, far_back = (m.astype(F32) for m in mask)
+        kernel = kernel_block(ref[:, :width], column, r[:, :width], r_row, scale_inv)
+        sums.append(halves(mm(kernel, masked(r_weights, near, far_out))))
+        acc += mm_tn(masked(weights, near, far_back), kernel)
     out1[...] = init1[...] + sums[0]
     out2[...] = init2[...] + sums[1]
-    acc[...] = total
-
-
-def before_kernel(scale_inv, width, info, mask_ref, p1, p2, r, w_p, acc, wr, rr, table_ref, result):
-    columns = result.shape[1] // 3
-    masks, names, _ = pair_masks(info, mask_ref)
-    weights = [
-        leaf_weights(ref, width, columns, w_p[...], table_ref, leaf) for ref, leaf in zip((p1, p2), names[2:], strict=True)
-    ]
-    offsets = [row_offset(ref[:, :width], scale_inv) for ref in (p1, p2)]
-    jobs = zip(masks[2:], (p1, p2), offsets, weights, strict=True)
-    sums, total = pair_sums(scale_inv, width, jobs, r[:, :width], rr[...], wr[...], acc[...])
-    for i, value in enumerate((*sums, halves(jnp.transpose(total)))):
+    for i, value in enumerate((sums[2], sums[3], halves(jnp.transpose(acc)))):
         result[:, i * columns : (i + 1) * columns] = value.astype(BF16)
 
 
-def home_kernel(leaves, place_ref, got_ref, out_ref, sum_s):
+def home_kernel(leaves, sides, place_ref, got_ref, out_ref, sum_s):
     columns, rows = out_ref.shape
-    count = rows // leaves
+    count = rows // leaves // sides
     for leaf in range(leaves):
         sources = (leaf, leaf ^ 1, leaf + 2, (leaf ^ 1) + 2, leaf - 2)
-        total = 0.0
-        for part, source in enumerate(sources):
-            if 0 <= source < leaves:
-                at = device_of_leaf(source) * count
-                total += got_ref[at : at + count, part * columns : (part + 1) * columns].astype(F32)
-        at = device_of_leaf(leaf) * count
-        sum_s[at : at + count] = total
+        for i in range(sides):
+            total = 0.0
+            for part, source in enumerate(sources):
+                if 0 <= source < leaves:
+                    at, lane = device_of_leaf(source) * count, (5 * i + part) * columns
+                    total += got_ref[at : at + count, lane : lane + columns].astype(F32)
+            at = (device_of_leaf(leaf) * sides + i) * count
+            sum_s[at : at + count] = total
     total = sum_s[...]
     high = total.astype(BF16)
     low = (total - high.astype(F32)).astype(BF16)
@@ -578,14 +594,33 @@
         pl.GridSpec(
             grid=(4,),
             in_specs=[whole((1, rows)), whole((rows, width)), whole((columns, rows))]
-            + [whole((1, count)) for count in (rank, merge_index.shape[1], 2 * NWIN, LEVELS * 2 * FWIN)],
-            out_specs=[pl.BlockSpec((rows // 4, wide), lambda i: (i, 0)), whole((1, rows))],
+            + [whole(a.shape) for a in (skel_leaf, merge_index, near_mask, far_mask)],
+            out_specs=[
+                pl.BlockSpec((rows // 4, wide), lambda i: (i, 0)),
+                whole((1, rows)),
+            ],
             scratch_shapes=[pltpu.VMEM((1, rows), I32), pltpu.VMEM((per_peer, lanes), BF16)],
         ),
         shapes(((rows, wide), BF16), ((1, rows), I32)),
         vmem=62,
-    )(tree_slot.reshape(1, rows), points, weights.T, skel_leaf, merge_index, near_mask, far_mask.reshape(1, -1))
+    )(tree_slot.reshape(1, rows), points, weights.T, skel_leaf, merge_index, near_mask, far_mask)
     got = lax.all_to_all(send, "leaf", split_axis=0, concat_axis=0, tiled=True)
+
+    def halo(value):
+        def inside(by):
+            return lambda i: i + by if (i + by) // GROUP == i // GROUP else -1
+
+        return move(value, inside(2)), move(value, inside(-2))
+
+    ends = []
+    for g in range(1, groups):
+        for i in (0, 1):
+            pair = device_of_leaf(g * GROUP - 2 + i), device_of_leaf(g * GROUP + i)
+            ends += [pair, pair[::-1]]
+
+    def over_end(value):
+        return lax.ppermute(value, "leaf", ends)
+
 
     device = lax.axis_index("leaf")
     leaf = leaf_of_device(device)
@@ -601,88 +636,81 @@
     upper = merge_in[half:]
     uppers = [lax.ppermute(upper, "leaf", [(i, i ^ (2 * k)) for i in range(leaves)]) for k in (1, 2, 3)]
     got, interp, info, first, *uppers = lax.optimization_barrier((got, interp, info, first, *uppers))
+    cut = rows * 3 // 8
+    got_a, got_b = got[:cut], got[cut:]
+    behind_a, ahead_a = halo(got_a)
+    over_a = over_end(got_a)
+    other = move(got, lambda i: i ^ 1)
     first_other = move(first, lambda i: i ^ 1)
     group_pieces = jnp.stack([upper] + uppers)
     pieces = jnp.stack([group_pieces, move(group_pieces, lambda i: i ^ 1)])
     piece_shape = pieces.shape
 
     coded = got[:, wide - lanes :].reshape(leaves, 4 * rank).astype(F32)
-    tables = coded[:, : 2 * rank] * 32.0 + coded[:, 2 * rank :]
+    high, low = coded[:, : 2 * rank], coded[:, 2 * rank :]
+    tables = high * 32.0 + low
     mask_at = rank + merge_index.shape[1]
     masks = jnp.concatenate(
         [
-            coded[:, 2 * rank + mask_at : 2 * rank + mask_at + 2 * NWIN],
-            coded[:, mask_at : mask_at + LEVELS * 2 * FWIN],
+            low[:, mask_at : mask_at + 2 * NWIN],
+            high[:, mask_at : mask_at + LEVELS * 2 * FWIN],
         ],
         axis=1,
     ).astype(I32)
     table_shape = tables.shape
 
-    other = move(got, lambda i: i ^ 1)
-    behind = move(got, lambda i: i + 2)
-    ahead = move(got, lambda i: i - 2)
+    leaf_x, joined = whole((rows, wide)), pltpu.VMEM((rows, wide), BF16)
+    own_sum, other_sum, own_column, other_column = call(
+        functools.partial(own_kernel, scale_inv, width),
+        prefetch(2, (), [leaf_x] * 2, [whole((rows, columns))] * 2 + [whole((rows, 1))] * 2),
+        shapes(*[((rows, columns), F32)] * 2, *[((rows, 1), F32)] * 2),
+        flops=3 * rows * rows * width,
+    )(info, masks, got, other)
 
     give, keep, weight0 = call(
         level0_kernel,
-        prefetch(1, (), [whole((rows, wide)), whole((rank, rows)), whole(table_shape)],
+        prefetch(1, (), [leaf_x, whole((rank, rows)), whole(table_shape)],
                  [whole((half, message)), whole((half, width)), whole((rank, columns))]),
         shapes(((half, message), BF16), ((half, width), BF16), ((rank, columns), BF16)),
-    )(info, got, interp, tables)
+    )(info, after(got, own_sum), interp, tables)
     sent, weight1 = call(
         level1_kernel,
         prefetch(1, (), [whole((half, message)), whole((half, width)), whole((rank, columns))] + [whole((half, 2 * rank))] * 2,
                  [whole((half, message)), whole((rank, columns))]),
         shapes(((half, message), BF16), ((rank, columns), BF16)),
     )(info, move(give, lambda i: i ^ 1), keep, weight0, first, first_other)
+    sent, behind_a, ahead_a, over_a = lax.optimization_barrier((sent, behind_a, ahead_a, over_a))
+    over_b = over_end(after(got_b, over_a))
+
+    def merged(behind, ahead, over):
+        chip = leaf // 2 % 4
+        return jnp.where(chip == 0, over, behind), jnp.where(chip == 3, over, ahead)
+
+    behind_a, ahead_a = merged(behind_a, ahead_a, over_a)
     plane = [move(sent, lambda i, k=k: i ^ (2 * k)) for k in (1, 2, 3)]
-    own_sum, other_sum, own_column, other_column = call(
-        functools.partial(own_kernel, scale_inv, width),
-        prefetch(2, (), [whole((rows, wide))] * 2, [whole((rows, columns))] * 2 + [whole((rows, 1))] * 2),
-        shapes(*[((rows, columns), F32)] * 2, *[((rows, 1), F32)] * 2),
-        flops=3 * rows * rows * width,
-    )(info, masks, got, after(other, sent))
-    weight1_sent = after(weight1, own_sum)
-    behind1 = move(weight1_sent, lambda i: i + 2)
-    ahead1 = move(weight1_sent, lambda i: i - 2)
-
-    half2, weight2, weight3 = call(
+    cross1 = over_end(after(weight1, sent))
+    behind_other_a = move(behind_a, lambda i: i ^ 1)
+    behind_b, ahead_b = halo(after(got_b, *plane))
+    half2, weight2, weight3, weight1_all = call(
         level23_kernel,
         prefetch(1, (), [whole((half, message))] * 4 + [whole(piece_shape)],
-                 [whole((rank, message)), whole((2 * rank, columns)), whole((rank, columns))],
-                 [pltpu.VMEM((4 * rank, columns), BF16)]),
-        shapes(((rank, message), BF16), ((2 * rank, columns), BF16), ((rank, columns), BF16)),
-    )(info, after(sent, own_sum, behind1, ahead1, behind, ahead), *plane, pieces)
+                 [whole((rank, message)), whole((2 * rank, columns)), whole((rank, columns)), whole((4 * rank, columns))]),
+        shapes(((rank, message), BF16), ((2 * rank, columns), BF16), ((rank, columns), BF16), ((4 * rank, columns), BF16)),
+    )(info, after(sent, behind_other_a), *plane, pieces)
     half2_other = move(half2, lambda i: i ^ 1)
     half3 = call(
         level3_kernel,
         prefetch(1, (), [whole((rank, message))] * 2 + [whole(table_shape)], whole((half, message))),
         jax.ShapeDtypeStruct((half, message), BF16),
     )(info, half2, half2_other, tables)
-    far_parts = [send_each(half2 if a == 1 else half3, s) for a, s in slots]
+    half3_late = after(half3, over_b)
+    far_parts = [send_each(half2 if a == 1 else half3_late, s) for a, s in slots]
     extra = pl.BlockSpec((rank, 2 * columns), lambda *_: (0, width // (2 * columns)))
-    leaf_x, weight_1, sums = whole((rows, wide)), whole((rank, columns)), whole((rows, columns))
-    leaf_w, leaf_c, row_c, acc_shape = (rows, 2 * columns), (rows, 1), (1, rows), (2 * columns, rows)
-    next_1, next_2, acc, ahead_w, ahead_row = call(
-        functools.partial(next_kernel, scale_inv, width),
-        prefetch(2, (), [leaf_x] * 2 + [whole(leaf_c)] * 2 + [leaf_x] + [weight_1] * 2 + [sums] * 2 + [whole(table_shape)],
-                 [sums] * 2 + [whole(acc_shape), whole(leaf_w), whole(row_c)]),
-        shapes(((rows, columns), F32), ((rows, columns), F32), (acc_shape, F32), (leaf_w, BF16), (row_c, F32)),
-    )(info, masks, after(got, half3), other, own_column, other_column, ahead, weight1, ahead1, own_sum, other_sum, tables)
-
-    behind_other = move(after(behind, half3), lambda i: i ^ 1)
-    pair_sum = call(
-        functools.partial(before_kernel, scale_inv, width),
-        prefetch(2, (), [leaf_x] * 3 + [weight_1, whole(acc_shape), whole(leaf_w), whole(row_c), whole(table_shape)],
-                 whole((rows, 3 * columns))),
-        jax.ShapeDtypeStruct((rows, 3 * columns), BF16),
-        flops=4 * rows * rows * width,
-    )(info, masks, behind, behind_other, ahead, behind1, acc, ahead_w, ahead_row, tables)
-
     half4 = call(
         level4_kernel,
         prefetch(1, (1,), [whole((rank, columns)), extra, extra, whole(piece_shape)], whole((half, columns))),
         jax.ShapeDtypeStruct((half, columns), BF16),
-    )(info, after(weight3, pair_sum), far_parts[0], far_parts[1], pieces)
+    )(info, after(weight3, half3), far_parts[0], far_parts[1], pieces)
     nodes4 = groups // 2
     steps4 = [(-1, 1)] if nodes4 == 2 else [(s,) for s in (-2, -1, 1, 2)]
     weight4 = []
@@ -690,23 +718,36 @@
         for h in (0, 1):
             found = [[2 * (g // 2 + s) + (g % 2 ^ h) for s in steps if 0 <= g // 2 + s < nodes4] for g in range(groups)]
             weight4.append(send_each(half4, [f[0] if f else -1 for f in found]))
-    weight4 = jnp.stack(weight4)
+    weight_1, sums, leaf_c = whole((rank, columns)), whole((rows, columns)), whole((rows, 1))
+    behind_b, ahead_b = merged(behind_b, ahead_b, over_b)
+    before_b = after(behind_b, ahead_b, half3, *far_parts[:2])
+    behind_other = [behind_other_a, move(before_b, lambda i: i ^ 1)]
+    pair_1, pair_2, pair_sum = call(
+        functools.partial(pair_kernel, scale_inv, width),
+        prefetch(2, (), [leaf_x] * 2 + [leaf_c] * 2 + [whole((cut, wide)), whole((rows - cut, wide))] * 3 + [whole((4 * rank, columns)), weight_1] + [sums] * 2 + [whole(table_shape)],
+                 [sums] * 2 + [whole((rows, 3 * columns))], [joined] * 3),
+        shapes(((rows, columns), F32), ((rows, columns), F32), ((rows, 3 * columns), BF16)),
+        flops=8 * rows * rows * width,
+    )(info, masks, after(got, half4), other, own_column, other_column, behind_a, behind_b,
+      *behind_other, ahead_a, ahead_b, weight1_all, cross1, own_sum, other_sum, tables)
+
+    sides = 2 if per_peer % 32 == 0 else 1
     all_sums = call(
-        functools.partial(far_kernel, away, len(steps4), scale_inv, width),
-        prefetch(2, (), [leaf_x] * 2 + [whole(leaf_c)] * 2 + [whole((rank, message)), whole((2 * rank, columns)),
-                 whole(weight4.shape), whole(table_shape), sums, sums, whole((rows, 3 * columns))]
-                 + [whole(p.shape) for p in far_parts], whole((rows, 5 * columns)),
+        functools.partial(far_kernel, away, len(steps4), sides, per_peer // sides, scale_inv, width),
+        prefetch(2, (), [leaf_x] * 2 + [leaf_c] * 2 + [whole((rank, message)), whole((2 * rank, columns)),
+                 whole(table_shape), sums, sums, whole((rows, 3 * columns))]
+                 + [whole(p.shape) for p in (*far_parts, *weight4)], whole((rows // sides, 5 * sides * columns)),
                  [pltpu.VMEM((rows, columns), F32)] * 2
                  + [pltpu.VMEM((rank, 3 * columns), BF16), pltpu.VMEM((rank, 2 * columns), BF16)]),
-        jax.ShapeDtypeStruct((rows, 5 * columns), BF16),
+        jax.ShapeDtypeStruct((rows // sides, 5 * sides * columns), BF16),
         flops=4 * rows * rows * width,
-    )(info, masks, got, other, own_column, other_column, half2, weight2, weight4, tables, next_1, next_2, pair_sum,
-      *far_parts)
+    )(info, masks, got, other, own_column, other_column, half2, weight2, tables, pair_1, pair_2, pair_sum,
+      *far_parts, *weight4)
 
     home = lax.all_to_all(all_sums, "leaf", split_axis=0, concat_axis=0, tiled=True)
     return call(
-        functools.partial(home_kernel, leaves),
-        pl.GridSpec(grid=(), in_specs=[whole((1, rows)), whole((rows, 5 * columns))], out_specs=whole((columns, rows)),
+        functools.partial(home_kernel, leaves, sides),
+        pl.GridSpec(grid=(), in_specs=[whole((1, rows)), whole((rows // sides, 5 * sides * columns))], out_specs=whole((columns, rows)),
                     scratch_shapes=[pltpu.VMEM((rows, columns), F32)]),
         jax.ShapeDtypeStruct((columns, rows), F32),
     )(place, home).T

time: 203 us -> 190 us (0.936)
  blocking collectives: 25.5 us -> 20.7 us
  waiting for transfers between devices: 67.6 us -> 64.4 us
  Pallas kernels: 49.2 us -> 46.4 us
  starting transfers between devices: 50.8 us -> 53.6 us
  local copies, waits for them, and re-layouts: 4.55 us -> 2.25 us
    ppermute x6, starting transfers between devices: 17.8 us -> 13 us  [send_each(): return lax.ppermute(value, 'leaf', pairs)]
    all_to_all x1, blocking collectives: 25.5 us -> 20.7 us  [local(): lax.all_to_all(all_sums, 'leaf', split_axis=0, concat_axis=0, tiled=True)]
    ppermute x6, waiting for transfers between devices: 6.62 us -> 2.07 us  [send_each(): return lax.ppermute(value, 'leaf', pairs)]
    ppermute x13 -> x14, starting transfers between devices: 16.6 us -> 21 us  [move(): return lax.ppermute(value, 'leaf', pairs)]
    ppermute x0 -> x3, starting transfers between devices: none -> 3.05 us  [over_end(): return lax.ppermute(value, 'leaf', ends)]
    ppermute x3, waiting for transfers between devices: 32.5 us -> 29.7 us  [local(): lax.ppermute(upper, 'leaf', [(i, i ^ 2 * k) for i in range(leaves)])]
    all_to_all x1, waiting for transfers between devices: 0.77 us -> 3.55 us  [local(): got = lax.all_to_all(send, 'leaf', split_axis=0, concat_axis=0, tiled=True)]
    another operation x2, other arithmetic: 2.87 us -> 0.16 us  [local(): pieces = jnp.stack([group_pieces, move(group_pieces, lambda i: i ^ 1)])]
  transfers between devices with their start and end apart: 25 -> 29, of which waited for: 10 -> 12; matrix products, arithmetic and copies ran while one was open for 4% -> 2% of each run, Pallas kernels for 15% -> 15%
where the time goes in v2:
time: 190 us
  waiting for transfers between devices  64.4 us (34%)
  starting transfers between devices  53.6 us (28%)
  Pallas kernels  46.4 us (24%)
  blocking collectives  20.7 us (11%)
  local copies, waits for them, and re-layouts  2.25 us (1%)
  other arithmetic  2.04 us (1%)
    ppermute x3, waiting for transfers between devices, local(): lax.ppermute(upper, 'leaf', [(i, i ^ 2 * k) for i in range(leaves)])  29.7 us
    ppermute x14, waiting for transfers between devices, move(): return lax.ppermute(value, 'leaf', pairs)  29.1 us
    ppermute x14, starting transfers between devices, move(): return lax.ppermute(value, 'leaf', pairs)  21 us
    all_to_all x1, blocking collectives, local(): lax.all_to_all(all_sums, 'leaf', split_axis=0, concat_axis=0, tiled=True)  20.7 us
    pallas_call x1, Pallas kernels, local(): call(functools.partial(pair_kernel, scale_inv, width), prefetch(2, (), [l...  15.3 us
    ppermute x6, starting transfers between devices, send_each(): return lax.ppermute(value, 'leaf', pairs)  13 us
    pallas_call x1, Pallas kernels, local(): call(functools.partial(far_kernel, away, len(steps4), sides, per_peer //...  10.3 us
    all_to_all x1, starting transfers between devices, local(): got = lax.all_to_all(send, 'leaf', split_axis=0, concat_axis=0, tiled=True)  7.29 us
  transfers between devices with their start and end apart: 29, of which 12 were waited for; matrix products, arithmetic and copies ran while one was open for 2% of the time, Pallas kernels for 15%

profile of v2, /device:TPU:0, one launch (start us, length us, event | category | flops | bytes accessed | tf_op | source)
XLA Modules:
  0.0 189.8 jit_solution(12073674726017298886)
XLA Ops:
  0.0 6.6 %shard_map.100 = (bf16[1024,896]{1,0:T(8,128)(2,1)}, s32[1,1024]{1,0:T(1,128)}) custom-call(s32[1,1024]{1,0:T(1,128)} %bitcast.43, bf16[1024,768]{1,0:T(8,128)(2,1)} %points_ref.1, bf16[64,1024]{1,0:T(8,128)(2,1)} %bitcast.39, s32[1,256]{1,0:T(1,128)} %skel_ref.1, s32[1,240]{1,0:T(1,128)} %merge_ref.1, s32[1,8]{1,0:T(1,128)} %near_ref.1, s32[1,4,4]{2,1,0:T(4,128)} %far_ref.1), custom_call_target="tpu_custom_call" | custom-call | tf_op jit(solution)/shard_map/pallas_call | solution.py:592
  6.6 7.3 %all-to-all-start = ((bf16[32,32,896]{2,1,0:T(8,128)(2,1)}), bf16[32,32,896]{2,1,0:T(8,128)(2,1)S(1)}, u32[]{:S(2)}, u32[]{:S(2)}) async-start(bf16[32,32,896]{2,1,0:T(8,128)(2,1)} %bitcast.35), calls=%async_computation | async-start | bytes 3670016 | tf_op jit(solution)/shard_map/all_to_all | solution.py:607
  13.9 1.7 collective-permute-start
  16.3 6.2 %collective-permute-start.4 = (bf16[112,512]{1,0:T(8,128)(2,1)S(1)}, bf16[112,512]{1,0:T(8,128)(2,1)S(1)}, u32[]{:S(2)}, u32[]{:S(2)}) collective-permute-start(bf16[112,512]{1,0:T(8,128)(2,1)S(1)} %get-tuple-element.92), channel_id=1, source_target_pairs={{0,6},{1,7},{2,4},{3,5},{4,2},{5,3},{6,0},{7,1},{8,14},{9,15},{10,... | collective-permute-start | bytes 344072 | tf_op jit(solution)/shard_map/ppermute | solution.py:637
  23.9 29.7 %collective-permute-done.4 = bf16[112,512]{1,0:T(8,128)(2,1)S(1)} collective-permute-done((bf16[112,512]{1,0:T(8,128)(2,1)S(1)}, bf16[112,512]{1,0:T(8,128)(2,1)S(1)}, u32[]{:S(2)}, u32[]{:S(2)}) %collective-permute-start.4) | collective-permute-done | bytes 114720 | tf_op jit(solution)/shard_map/ppermute | solution.py:637
  53.7 3.6 %all-to-all-done = bf16[32,32,896]{2,1,0:T(8,128)(2,1)S(1)} async-done(((bf16[32,32,896]{2,1,0:T(8,128)(2,1)}), bf16[32,32,896]{2,1,0:T(8,128)(2,1)S(1)}, u32[]{:S(2)}, u32[]{:S(2)}) %all-to-all-start) | async-done | bytes 1835040 | tf_op jit(solution)/shard_map/all_to_all | solution.py:607
  58.8 1.5 collective-permute-start.10
  60.3 1.3 collective-permute-start.9
  61.6 5.4 %collective-permute-start.8 = (bf16[384,896]{1,0:T(8,128)(2,1)}, bf16[384,896]{1,0:T(8,128)(2,1)}, u32[]{:S(2)}, u32[]{:S(2)}) collective-permute-start(bf16[384,896]{1,0:T(8,128)(2,1)} %slice.36), channel_id=1, source_target_pairs={{0,2},{1,3},{2,6},{3,7},{6,4},{7,5},{12,14},{13,15},{14,10},{15,11... | collective-permute-start | bytes 2064392 | tf_op jit(solution)/shard_map/ppermute | solution.py:74
  67.1 5.1 %shard_map.101 = (f32[1024,64]{1,0:T(8,128)S(1)}, f32[1024,64]{1,0:T(8,128)S(1)}, f32[1024,1]{1,0:T(8,128)S(1)}, f32[1024,1]{1,0:T(8,128)S(1)}) custom-call(s32[10]{0:T(128)S(1)} %concatenate.6.info, s32[32,24]{1,0:T(8,128)S(1)} %maximum_convert_fusion.mask_ref, bf16[1024,896]{1,0:T(8,128)(2,1)S(1)} %bitcast.28, ...), custom_call_target="tpu_custom_call" | custom-call | flops 2415919104 | tf_op jit(solution)/shard_map/pallas_call | solution.py:663
  72.3 3.3 %shard_map.102 = (bf16[128,896]{1,0:T(8,128)(2,1)S(1)}, bf16[128,768]{1,0:T(8,128)(2,1)S(1)}, bf16[256,64]{1,0:T(8,128)(2,1)S(1)}) custom-call(s32[10]{0:T(128)S(1)} %concatenate.6.info, bf16[1024,896]{1,0:T(8,128)(2,1)S(1)} %bitcast.29, bf16[256,1024]{1,0:T(8,128)(2,1)S(1)} %collective-permute-done.interp_ref, f32[32,512]{1,0:T(8,128)S(1)} %slice_add_fusion.table_ref), custom_call_target="tpu_custom_call" | custom-call | tf_op jit(solution)/shard_map/pallas_call | solution.py:670
  78.3 2.1 %collective-permute-done.9 = bf16[384,896]{1,0:T(8,128)(2,1)} collective-permute-done((bf16[384,896]{1,0:T(8,128)(2,1)}, bf16[384,896]{1,0:T(8,128)(2,1)}, u32[]{:S(2)}, u32[]{:S(2)}) %collective-permute-start.9) | collective-permute-done | bytes 688160 | tf_op jit(solution)/shard_map/ppermute | solution.py:74
  81.6 5.6 %collective-permute-start.14 = (bf16[128,896]{1,0:T(8,128)(2,1)S(1)}, bf16[128,896]{1,0:T(8,128)(2,1)S(1)}, u32[]{:S(2)}, u32[]{:S(2)}) collective-permute-start(bf16[128,896]{1,0:T(8,128)(2,1)S(1)} %get-tuple-element.64.m0), channel_id=1, source_target_pairs={{0,4},{1,5},{2,6},{3,7},{6,2},{7,3},{4,0},{5,1},{12,8},{13,9},{14,... | collective-permute-start | bytes 688136 | tf_op jit(solution)/shard_map/ppermute | solution.py:74
  87.2 1.5 collective-permute-start.12
  88.7 1.4 broadcast_select_fusion.2
  91.0 6.3 %collective-permute-done.14.m3 = bf16[128,896]{1,0:T(8,128)(2,1)S(1)} collective-permute-done((bf16[128,896]{1,0:T(8,128)(2,1)S(1)}, bf16[128,896]{1,0:T(8,128)(2,1)S(1)}, u32[]{:S(2)}, u32[]{:S(2)}) %collective-permute-start.14) | collective-permute-done | bytes 229408 | tf_op jit(solution)/shard_map/ppermute | solution.py:74
  97.3 1.3 collective-permute-done.12.m1
  98.6 1.3 collective-permute-start.21
  99.9 4.8 %collective-permute-start.20 = (bf16[640,896]{1,0:T(8,128)(2,1)S(1)}, bf16[640,896]{1,0:T(8,128)(2,1)S(1)}, u32[]{:S(2)}, u32[]{:S(2)}) collective-permute-start(bf16[640,896]{1,0:T(8,128)(2,1)S(1)} %slice.37), channel_id=1, source_target_pairs={{0,2},{1,3},{2,6},{3,7},{6,4},{7,5},{12,14},{13,15},{14,10},{15,11... | collective-permute-start | bytes 3440648 | tf_op jit(solution)/shard_map/ppermute | solution.py:74
  104.9 1.8 collective-permute-done.15
  106.8 1.3 shard_map.104
  108.2 1.4 collective-permute-start.18
  109.9 1.3 collective-permute-start.17
  112.3 13.9 %collective-permute-done.21 = bf16[640,896]{1,0:T(8,128)(2,1)S(1)} collective-permute-done((bf16[640,896]{1,0:T(8,128)(2,1)S(1)}, bf16[640,896]{1,0:T(8,128)(2,1)S(1)}, u32[]{:S(2)}, u32[]{:S(2)}) %collective-permute-start.21) | collective-permute-done | bytes 1146912 | tf_op jit(solution)/shard_map/ppermute | solution.py:74
  129.4 3.4 %collective-permute-start.27 = (bf16[128,64]{1,0:T(8,128)(2,1)S(1)}, bf16[128,64]{1,0:T(8,128)(2,1)S(1)}, u32[]{:S(2)}, u32[]{:S(2)}) collective-permute-start(bf16[128,64]{1,0:T(8,128)(2,1)S(1)} %shard_map.106), channel_id=1, source_target_pairs={{24,0},{25,1},{26,2},{27,3},{28,4},{29,5},{30,6},{31,7},{16,8},{17... | collective-permute-start | bytes 49160 | tf_op jit(solution)/shard_map/ppermute | solution.py:89
  132.9 3.7 %collective-permute-start.26 = (bf16[128,64]{1,0:T(8,128)(2,1)S(1)}, bf16[128,64]{1,0:T(8,128)(2,1)S(1)}, u32[]{:S(2)}, u32[]{:S(2)}) collective-permute-start(bf16[128,64]{1,0:T(8,128)(2,1)S(1)} %shard_map.106), channel_id=1, source_target_pairs={{16,0},{17,1},{18,2},{19,3},{20,4},{21,5},{22,6},{23,7},{24,8},{25... | collective-permute-start | bytes 49160 | tf_op jit(solution)/shard_map/ppermute | solution.py:89
  136.5 3.1 %collective-permute-start.25 = (bf16[128,896]{1,0:T(8,128)(2,1)S(1)}, bf16[128,896]{1,0:T(8,128)(2,1)S(1)}, u32[]{:S(2)}, u32[]{:S(2)}) collective-permute-start(bf16[128,896]{1,0:T(8,128)(2,1)S(1)} %shard_map.105), channel_id=1, source_target_pairs={{24,0},{25,1},{26,2},{27,3},{28,4},{29,5},{30,6},{31,7},{0,24},{1,... | collective-permute-start | bytes 688136 | tf_op jit(solution)/shard_map/ppermute | solution.py:89
  139.8 15.3 %shard_map.107 = (f32[1024,64]{1,0:T(8,128)S(1)}, f32[1024,64]{1,0:T(8,128)S(1)}, bf16[1024,192]{1,0:T(8,128)(2,1)S(1)}) custom-call(s32[10]{0:T(128)S(1)} %concatenate.6.info, s32[32,24]{1,0:T(8,128)S(1)} %maximum_convert_fusion.mask_ref, bf16[1024,896]{1,0:T(8,128)(2,1)S(1)} %bitcast.31, bf16[1024,896]{1,0:T(8,128)(2,1)} %collective-permute-done.5.other_ref.q2.x2_ref, ...), custom_call_target="tpu_custom_call" | custom-call | flops 6442450944 | tf_op jit(solution)/shard_map/pallas_call | solution.py:725
  155.1 2.1 %collective-permute-done.24.rest_2_ = bf16[128,896]{1,0:T(8,128)(2,1)S(1)} collective-permute-done((bf16[128,896]{1,0:T(8,128)(2,1)S(1)}, bf16[128,896]{1,0:T(8,128)(2,1)S(1)}, u32[]{:S(2)}, u32[]{:S(2)}) %collective-permute-start.24) | collective-permute-done | bytes 229408 | tf_op jit(solution)/shard_map/ppermute | solution.py:89
  157.2 10.3 %shard_map.108 = bf16[512,640]{1,0:T(8,128)(2,1)S(1)} custom-call(s32[10]{0:T(128)S(1)} %concatenate.6.info, s32[32,24]{1,0:T(8,128)S(1)} %maximum_convert_fusion.mask_ref, bf16[1024,896]{1,0:T(8,128)(2,1)S(1)} %bitcast.32, bf16[1024,896]{1,0:T(8,128)(2,1)} %collective-permute-done.5.other_ref.q2.x2_ref, f32[1024,1]{1,0:T(8,128)S(1)} %copy-done.2, ...), custom_call_target="tpu_custom_call" | custom-call | flops 3221225472 | tf_op jit(solution)/shard_map/pallas_call | solution.py:735
  167.5 20.7 %all_to_all.23 = bf16[32,16,640]{2,1,0:T(8,128)(2,1)S(1)} all-to-all(bf16[32,16,640]{2,1,0:T(8,128)(2,1)S(1)} %bitcast.34), channel_id=1, replica_groups=mesh['leaf'=32] {'leaf'}, dimensions={0} | all-to-all | bytes 1310720 | tf_op jit(solution)/shard_map/all_to_all | solution.py:747
  188.2 1.7 shard_map.109
  (85 shorter events, 13.5 us)
Async XLA Ops:
  6.6 50.7 %all-to-all-start = ((bf16[32,32,896]{2,1,0:T(8,128)(2,1)}), bf16[32,32,896]{2,1,0:T(8,128)(2,1)S(1)}, u32[]{:S(2)}, u32[]{:S(2)}) async-start(bf16[32,32,896]{2,1,0:T(8,128)(2,1)} %bitcast.35), calls=%async_computation | async-start | bytes 3670016 | tf_op jit(solution)/shard_map/all_to_all | solution.py:607
  13.9 39.8 %collective-permute-start = (bf16[256,1024]{1,0:T(8,128)(2,1)}, bf16[256,1024]{1,0:T(8,128)(2,1)S(1)}, u32[]{:S(2)}, u32[]{:S(2)}) collective-permute-start(bf16[256,1024]{1,0:T(8,128)(2,1)} %bitcast.4), channel_id=1, source_target_pairs={{0,0},{1,1},{2,2},{3,3},{4,6},{5,7},{6,4},{7,5},{8,12},{9,13},{10,... | collective-permute-start | bytes 1572872 | tf_op jit(solution)/shard_map/ppermute | solution.py:634
  15.6 38.1 %collective-permute-start.1 = (bf16[128,512]{1,0:T(8,128)(2,1)S(1)}, bf16[128,512]{1,0:T(8,128)(2,1)S(1)}, u32[]{:S(2)}, u32[]{:S(2)}) collective-permute-start(bf16[128,512]{1,0:T(8,128)(2,1)S(1)} %slice.29), channel_id=1, source_target_pairs={{0,0},{1,1},{2,2},{3,3},{4,6},{5,7},{6,4},{7,5},{8,12},{9,13},{10,... | collective-permute-start | bytes 393224 | tf_op jit(solution)/shard_map/ppermute | solution.py:635
  16.3 37.4 %collective-permute-start.4 = (bf16[112,512]{1,0:T(8,128)(2,1)S(1)}, bf16[112,512]{1,0:T(8,128)(2,1)S(1)}, u32[]{:S(2)}, u32[]{:S(2)}) collective-permute-start(bf16[112,512]{1,0:T(8,128)(2,1)S(1)} %get-tuple-element.92), channel_id=1, source_target_pairs={{0,6},{1,7},{2,4},{3,5},{4,2},{5,3},{6,0},{7,1},{8,14},{9,15},{10,... | collective-permute-start | bytes 344072 | tf_op jit(solution)/shard_map/ppermute | solution.py:637
  22.5 31.1 %collective-permute-start.3 = (bf16[112,512]{1,0:T(8,128)(2,1)S(1)}, bf16[112,512]{1,0:T(8,128)(2,1)S(1)}, u32[]{:S(2)}, u32[]{:S(2)}) collective-permute-start(bf16[112,512]{1,0:T(8,128)(2,1)S(1)} %get-tuple-element.92), channel_id=1, source_target_pairs={{0,4},{1,5},{2,6},{3,7},{4,0},{5,1},{6,2},{7,3},{8,12},{9,13},{10,... | collective-permute-start | bytes 344072 | tf_op jit(solution)/shard_map/ppermute | solution.py:637
  22.5 31.1 %collective-permute-start.2 = (bf16[112,512]{1,0:T(8,128)(2,1)S(1)}, bf16[112,512]{1,0:T(8,128)(2,1)S(1)}, u32[]{:S(2)}, u32[]{:S(2)}) collective-permute-start(bf16[112,512]{1,0:T(8,128)(2,1)S(1)} %get-tuple-element.92), channel_id=1, source_target_pairs={{0,2},{1,3},{2,0},{3,1},{4,6},{5,7},{6,4},{7,5},{8,10},{9,11},{10,... | collective-permute-start | bytes 344072 | tf_op jit(solution)/shard_map/ppermute | solution.py:637
  57.3 9.8 %collective-permute-start.5 = (bf16[1024,896]{1,0:T(8,128)(2,1)S(1)}, bf16[1024,896]{1,0:T(8,128)(2,1)}, u32[]{:S(2)}, u32[]{:S(2)}) collective-permute-start(bf16[1024,896]{1,0:T(8,128)(2,1)S(1)} %bitcast.25), channel_id=1, source_target_pairs={{0,1},{1,0},{2,3},{3,2},{6,7},{7,6},{4,5},{5,4},{12,13},{13,12},{1... | collective-permute-start | bytes 5505032 | tf_op jit(solution)/shard_map/ppermute | solution.py:74
  58.8 19.5 %collective-permute-start.10 = (bf16[384,896]{1,0:T(8,128)(2,1)}, bf16[384,896]{1,0:T(8,128)(2,1)}, u32[]{:S(2)}, u32[]{:S(2)}) collective-permute-start(bf16[384,896]{1,0:T(8,128)(2,1)} %slice.36), channel_id=1, source_target_pairs={{4,12},{12,4},{5,13},{13,5},{8,16},{16,8},{9,17},{17,9},{20,28},{2... | collective-permute-start | bytes 2064392 | tf_op jit(solution)/shard_map/ppermute | solution.py:622
  60.3 20.0 %collective-permute-start.9 = (bf16[384,896]{1,0:T(8,128)(2,1)}, bf16[384,896]{1,0:T(8,128)(2,1)}, u32[]{:S(2)}, u32[]{:S(2)}) collective-permute-start(bf16[384,896]{1,0:T(8,128)(2,1)} %slice.36), channel_id=1, source_target_pairs={{2,0},{3,1},{6,2},{7,3},{4,6},{5,7},{14,12},{15,13},{10,14},{11,15... | collective-permute-start | bytes 2064392 | tf_op jit(solution)/shard_map/ppermute | solution.py:74
  61.6 19.9 %collective-permute-start.8 = (bf16[384,896]{1,0:T(8,128)(2,1)}, bf16[384,896]{1,0:T(8,128)(2,1)}, u32[]{:S(2)}, u32[]{:S(2)}) collective-permute-start(bf16[384,896]{1,0:T(8,128)(2,1)} %slice.36), channel_id=1, source_target_pairs={{0,2},{1,3},{2,6},{3,7},{6,4},{7,5},{12,14},{13,15},{14,10},{15,11... | collective-permute-start | bytes 2064392 | tf_op jit(solution)/shard_map/ppermute | solution.py:74
  75.7 1.7 collective-permute-start.6
  75.7 1.7 collective-permute-start.7
  81.5 23.1 %copy-start.11 = (bf16[112,512]{1,0:T(8,128)(2,1)S(1)}, bf16[112,512]{1,0:T(8,128)(2,1)}, u32[]{:S(2)}) copy-start(bf16[112,512]{1,0:T(8,128)(2,1)} %copy-done.10) | copy-start | bytes 344068
  81.5 23.1 %copy-start.13 = (bf16[112,512]{1,0:T(8,128)(2,1)S(1)}, bf16[112,512]{1,0:T(8,128)(2,1)}, u32[]{:S(2)}) copy-start(bf16[112,512]{1,0:T(8,128)(2,1)} %copy-done.12) | copy-start | bytes 344068
  81.5 23.1 %copy-start.15 = (bf16[112,512]{1,0:T(8,128)(2,1)S(1)}, bf16[112,512]{1,0:T(8,128)(2,1)}, u32[]{:S(2)}) copy-start(bf16[112,512]{1,0:T(8,128)(2,1)} %copy-done.14) | copy-start | bytes 344068
  81.6 15.7 %collective-permute-start.14 = (bf16[128,896]{1,0:T(8,128)(2,1)S(1)}, bf16[128,896]{1,0:T(8,128)(2,1)S(1)}, u32[]{:S(2)}, u32[]{:S(2)}) collective-permute-start(bf16[128,896]{1,0:T(8,128)(2,1)S(1)} %get-tuple-element.64.m0), channel_id=1, source_target_pairs={{0,4},{1,5},{2,6},{3,7},{6,2},{7,3},{4,0},{5,1},{12,8},{13,9},{14,... | collective-permute-start | bytes 688136 | tf_op jit(solution)/shard_map/ppermute | solution.py:74
  87.2 10.1 %collective-permute-start.13 = (bf16[128,896]{1,0:T(8,128)(2,1)S(1)}, bf16[128,896]{1,0:T(8,128)(2,1)S(1)}, u32[]{:S(2)}, u32[]{:S(2)}) collective-permute-start(bf16[128,896]{1,0:T(8,128)(2,1)S(1)} %get-tuple-element.64.m0), channel_id=1, source_target_pairs={{0,6},{1,7},{2,4},{3,5},{6,0},{7,1},{4,2},{5,3},{12,10},{13,11},{1... | collective-permute-start | bytes 688136 | tf_op jit(solution)/shard_map/ppermute | solution.py:74
  87.2 11.4 %collective-permute-start.12 = (bf16[128,896]{1,0:T(8,128)(2,1)S(1)}, bf16[128,896]{1,0:T(8,128)(2,1)S(1)}, u32[]{:S(2)}, u32[]{:S(2)}) collective-permute-start(bf16[128,896]{1,0:T(8,128)(2,1)S(1)} %get-tuple-element.64.m0), channel_id=1, source_target_pairs={{0,2},{1,3},{2,0},{3,1},{6,4},{7,5},{4,6},{5,7},{12,14},{13,15},{1... | collective-permute-start | bytes 688136 | tf_op jit(solution)/shard_map/ppermute | solution.py:74
  90.2 16.6 %collective-permute-start.11 = (bf16[384,896]{1,0:T(8,128)(2,1)S(1)}, bf16[384,896]{1,0:T(8,128)(2,1)S(1)}, u32[]{:S(2)}, u32[]{:S(2)}) collective-permute-start(bf16[384,896]{1,0:T(8,128)(2,1)S(1)} %get-tuple-element.88.p1a), channel_id=1, source_target_pairs={{0,1},{1,0},{2,3},{3,2},{6,7},{7,6},{4,5},{5,4},{12,13},{13,12},{1... | collective-permute-start | bytes 2064392 | tf_op jit(solution)/shard_map/ppermute | solution.py:74
  90.2 22.0 %collective-permute-start.19 = (bf16[640,896]{1,0:T(8,128)(2,1)S(1)}, bf16[640,896]{1,0:T(8,128)(2,1)S(1)}, u32[]{:S(2)}, u32[]{:S(2)}) collective-permute-start(bf16[640,896]{1,0:T(8,128)(2,1)S(1)} %slice.37), channel_id=1, source_target_pairs={{4,12},{12,4},{5,13},{13,5},{8,16},{16,8},{9,17},{17,9},{20,28},{2... | collective-permute-start | bytes 3440648 | tf_op jit(solution)/shard_map/ppermute | solution.py:622
  98.6 27.6 %collective-permute-start.21 = (bf16[640,896]{1,0:T(8,128)(2,1)S(1)}, bf16[640,896]{1,0:T(8,128)(2,1)S(1)}, u32[]{:S(2)}, u32[]{:S(2)}) collective-permute-start(bf16[640,896]{1,0:T(8,128)(2,1)S(1)} %slice.37), channel_id=1, source_target_pairs={{2,0},{3,1},{6,2},{7,3},{4,6},{5,7},{14,12},{15,13},{10,14},{11,15... | collective-permute-start | bytes 3440648 | tf_op jit(solution)/shard_map/ppermute | solution.py:74
  99.9 27.5 %collective-permute-start.20 = (bf16[640,896]{1,0:T(8,128)(2,1)S(1)}, bf16[640,896]{1,0:T(8,128)(2,1)S(1)}, u32[]{:S(2)}, u32[]{:S(2)}) collective-permute-start(bf16[640,896]{1,0:T(8,128)(2,1)S(1)} %slice.37), channel_id=1, source_target_pairs={{0,2},{1,3},{2,6},{3,7},{6,4},{7,5},{12,14},{13,15},{14,10},{15,11... | collective-permute-start | bytes 3440648 | tf_op jit(solution)/shard_map/ppermute | solution.py:74
  104.8 1.9 collective-permute-start.15
  108.0 1.9 collective-permute-start.16
  108.2 19.3 %collective-permute-start.18 = (bf16[256,896]{1,0:T(8,128)(2,1)S(1)}, bf16[256,896]{1,0:T(8,128)(2,1)S(1)}, u32[]{:S(2)}, u32[]{:S(2)}) collective-permute-start(bf16[256,896]{1,0:T(8,128)(2,1)S(1)} %get-tuple-element.68.own_ref.half_ref), channel_id=1, source_target_pairs={{0,8},{1,9},{2,10},{3,11},{4,12},{5,13},{6,14},{7,15},{8,16},{9,17... | collective-permute-start | bytes 1376264 | tf_op jit(solution)/shard_map/ppermute | solution.py:89
  109.9 17.7 %collective-permute-start.17 = (bf16[256,896]{1,0:T(8,128)(2,1)S(1)}, bf16[256,896]{1,0:T(8,128)(2,1)S(1)}, u32[]{:S(2)}, u32[]{:S(2)}) collective-permute-start(bf16[256,896]{1,0:T(8,128)(2,1)S(1)} %get-tuple-element.68.own_ref.half_ref), channel_id=1, source_target_pairs={{8,0},{9,1},{10,2},{11,3},{12,4},{13,5},{14,6},{15,7},{16,8},{17,9... | collective-permute-start | bytes 1376264 | tf_op jit(solution)/shard_map/ppermute | solution.py:89
  127.6 12.2 %collective-permute-start.22 = (bf16[640,896]{1,0:T(8,128)(2,1)S(1)}, bf16[640,896]{1,0:T(8,128)(2,1)S(1)}, u32[]{:S(2)}, u32[]{:S(2)}) collective-permute-start(bf16[640,896]{1,0:T(8,128)(2,1)S(1)} %get-tuple-element.75.p1b), channel_id=1, source_target_pairs={{0,1},{1,0},{2,3},{3,2},{6,7},{7,6},{4,5},{5,4},{12,13},{13,12},{1... | collective-permute-start | bytes 3440648 | tf_op jit(solution)/shard_map/ppermute | solution.py:74
  127.7 12.0 %collective-permute-start.23 = (bf16[256,64]{1,0:T(8,128)(2,1)S(1)}, bf16[256,64]{1,0:T(8,128)(2,1)S(1)}, u32[]{:S(2)}, u32[]{:S(2)}) collective-permute-start(bf16[256,64]{1,0:T(8,128)(2,1)S(1)} %get-tuple-element.79), channel_id=1, source_target_pairs={{4,12},{12,4},{5,13},{13,5},{8,16},{16,8},{9,17},{17,9},{20,28},{2... | collective-permute-start | bytes 98312 | tf_op jit(solution)/shard_map/ppermute | solution.py:622
  129.4 25.7 %collective-permute-start.27 = (bf16[128,64]{1,0:T(8,128)(2,1)S(1)}, bf16[128,64]{1,0:T(8,128)(2,1)S(1)}, u32[]{:S(2)}, u32[]{:S(2)}) collective-permute-start(bf16[128,64]{1,0:T(8,128)(2,1)S(1)} %shard_map.106), channel_id=1, source_target_pairs={{24,0},{25,1},{26,2},{27,3},{28,4},{29,5},{30,6},{31,7},{16,8},{17... | collective-permute-start | bytes 49160 | tf_op jit(solution)/shard_map/ppermute | solution.py:89
  132.9 22.3 %collective-permute-start.26 = (bf16[128,64]{1,0:T(8,128)(2,1)S(1)}, bf16[128,64]{1,0:T(8,128)(2,1)S(1)}, u32[]{:S(2)}, u32[]{:S(2)}) collective-permute-start(bf16[128,64]{1,0:T(8,128)(2,1)S(1)} %shard_map.106), channel_id=1, source_target_pairs={{16,0},{17,1},{18,2},{19,3},{20,4},{21,5},{22,6},{23,7},{24,8},{25... | collective-permute-start | bytes 49160 | tf_op jit(solution)/shard_map/ppermute | solution.py:89
  136.5 18.6 %collective-permute-start.25 = (bf16[128,896]{1,0:T(8,128)(2,1)S(1)}, bf16[128,896]{1,0:T(8,128)(2,1)S(1)}, u32[]{:S(2)}, u32[]{:S(2)}) collective-permute-start(bf16[128,896]{1,0:T(8,128)(2,1)S(1)} %shard_map.105), channel_id=1, source_target_pairs={{24,0},{25,1},{26,2},{27,3},{28,4},{29,5},{30,6},{31,7},{0,24},{1,... | collective-permute-start | bytes 688136 | tf_op jit(solution)/shard_map/ppermute | solution.py:89
  139.7 17.5 %collective-permute-start.24 = (bf16[128,896]{1,0:T(8,128)(2,1)S(1)}, bf16[128,896]{1,0:T(8,128)(2,1)S(1)}, u32[]{:S(2)}, u32[]{:S(2)}) collective-permute-start(bf16[128,896]{1,0:T(8,128)(2,1)S(1)} %shard_map.105), channel_id=1, source_target_pairs={{16,0},{17,1},{18,2},{19,3},{20,4},{21,5},{22,6},{23,7},{24,8},{25... | collective-permute-start | bytes 688136 | tf_op jit(solution)/shard_map/ppermute | solution.py:89
  (13 other events, 103.2 us)

commit v3 on v2

--- a/solution.py
+++ b/solution.py
@@ -679,7 +679,7 @@
                  [whole((half, message)), whole((rank, columns))]),
         shapes(((half, message), BF16), ((rank, columns), BF16)),
     )(info, move(give, lambda i: i ^ 1), keep, weight0, first, first_other)
-    sent, behind_a, ahead_a, over_a = lax.optimization_barrier((sent, behind_a, ahead_a, over_a))
+    sent, behind_a, ahead_a, over_a, pieces = lax.optimization_barrier((sent, behind_a, ahead_a, over_a, pieces))
     over_b = over_end(after(got_b, over_a))
 
     def merged(behind, ahead, over):
@@ -720,7 +720,7 @@
             weight4.append(send_each(half4, [f[0] if f else -1 for f in found]))
     weight_1, sums, leaf_c = whole((rank, columns)), whole((rows, columns)), whole((rows, 1))
     behind_b, ahead_b = merged(behind_b, ahead_b, over_b)
-    before_b = after(behind_b, ahead_b, half3, *far_parts[:2])
+    before_b = after(behind_b, ahead_b, half3, cross1, *far_parts[:2])
     behind_other = [behind_other_a, move(before_b, lambda i: i ^ 1)]
     pair_1, pair_2, pair_sum = call(
         functools.partial(pair_kernel, scale_inv, width),

time: 190 us -> 189 us (level)
  waiting for transfers between devices: 64.4 us -> 59 us
  other arithmetic: 2.04 us -> 3.99 us
    ppermute x14, waiting for transfers between devices: 29.1 us -> 24.7 us  [move(): return lax.ppermute(value, 'leaf', pairs)]
    another operation x2, other arithmetic: 0.16 us -> 2.11 us  [local(): pieces = jnp.stack([group_pieces, move(group_pieces, lambda i: i ^ 1)])]
  transfers between devices with their start and end apart: 29 -> 29, of which waited for: 12 -> 9; matrix products, arithmetic and copies ran while one was open for 2% -> 3% of each run, Pallas kernels for 15% -> 16%
where the time goes in v3:
time: 189 us; the launch traced here: 188 us
  waiting for transfers between devices  59 us (31%)
  starting transfers between devices  52.4 us (28%)
  Pallas kernels  48.1 us (25%)
  blocking collectives  22.1 us (12%)
  other arithmetic  3.99 us (2%)
  local copies, waits for them, and re-layouts  2.23 us (1%)
    ppermute x3, waiting for transfers between devices, local(): lax.ppermute(upper, 'leaf', [(i, i ^ 2 * k) for i in range(leaves)])  29.7 us
    ppermute x14, waiting for transfers between devices, move(): return lax.ppermute(value, 'leaf', pairs)  24.7 us
    all_to_all x1, blocking collectives, local(): lax.all_to_all(all_sums, 'leaf', split_axis=0, concat_axis=0, tiled=True)  22.1 us
    ppermute x14, starting transfers between devices, move(): return lax.ppermute(value, 'leaf', pairs)  20 us
    pallas_call x1, Pallas kernels, local(): call(functools.partial(pair_kernel, scale_inv, width), prefetch(2, (), [l...  15.3 us
    ppermute x6, starting transfers between devices, send_each(): return lax.ppermute(value, 'leaf', pairs)  12.9 us
    pallas_call x1, Pallas kernels, local(): call(functools.partial(far_kernel, away, len(steps4), sides, per_peer //...  10.3 us
    all_to_all x1, starting transfers between devices, local(): got = lax.all_to_all(send, 'leaf', split_axis=0, concat_axis=0, tiled=True)  7.29 us
  transfers between devices with their start and end apart: 29, of which 9 were waited for; matrix products, arithmetic and copies ran while one was open for 3% of the time, Pallas kernels for 16%

profile of v3, /device:TPU:0, one launch (start us, length us, event | category | flops | bytes accessed | tf_op | source)
XLA Modules:
  0.0 188.3 jit_solution(16147509991567831827)
XLA Ops:
  0.0 6.6 %shard_map.100 = (bf16[1024,896]{1,0:T(8,128)(2,1)}, s32[1,1024]{1,0:T(1,128)}) custom-call(s32[1,1024]{1,0:T(1,128)} %bitcast.42, bf16[1024,768]{1,0:T(8,128)(2,1)} %points_ref.1, bf16[64,1024]{1,0:T(8,128)(2,1)} %bitcast.38, s32[1,256]{1,0:T(1,128)} %skel_ref.1, s32[1,240]{1,0:T(1,128)} %merge_ref.1, s32[1,8]{1,0:T(1,128)} %near_ref.1, s32[1,4,4]{2,1,0:T(4,128)} %far_ref.1), custom_call_target="tpu_custom_call" | custom-call | tf_op jit(solution)/shard_map/pallas_call | solution.py:592
  6.6 7.3 %all-to-all-start = ((bf16[32,32,896]{2,1,0:T(8,128)(2,1)}), bf16[32,32,896]{2,1,0:T(8,128)(2,1)S(1)}, u32[]{:S(2)}, u32[]{:S(2)}) async-start(bf16[32,32,896]{2,1,0:T(8,128)(2,1)} %bitcast.35), calls=%async_computation | async-start | bytes 3670016 | tf_op jit(solution)/shard_map/all_to_all | solution.py:607
  13.9 1.7 collective-permute-start
  16.3 6.2 %collective-permute-start.4 = (bf16[112,512]{1,0:T(8,128)(2,1)S(1)}, bf16[112,512]{1,0:T(8,128)(2,1)S(1)}, u32[]{:S(2)}, u32[]{:S(2)}) collective-permute-start(bf16[112,512]{1,0:T(8,128)(2,1)S(1)} %get-tuple-element.94), channel_id=1, source_target_pairs={{0,6},{1,7},{2,4},{3,5},{4,2},{5,3},{6,0},{7,1},{8,14},{9,15},{10,... | collective-permute-start | bytes 344072 | tf_op jit(solution)/shard_map/ppermute | solution.py:637
  23.9 29.7 %collective-permute-done.4 = bf16[112,512]{1,0:T(8,128)(2,1)S(1)} collective-permute-done((bf16[112,512]{1,0:T(8,128)(2,1)S(1)}, bf16[112,512]{1,0:T(8,128)(2,1)S(1)}, u32[]{:S(2)}, u32[]{:S(2)}) %collective-permute-start.4) | collective-permute-done | bytes 114720 | tf_op jit(solution)/shard_map/ppermute | solution.py:637
  53.7 3.6 %all-to-all-done = bf16[32,32,896]{2,1,0:T(8,128)(2,1)S(1)} async-done(((bf16[32,32,896]{2,1,0:T(8,128)(2,1)}), bf16[32,32,896]{2,1,0:T(8,128)(2,1)S(1)}, u32[]{:S(2)}, u32[]{:S(2)}) %all-to-all-start) | async-done | bytes 1835040 | tf_op jit(solution)/shard_map/all_to_all | solution.py:607
  58.2 1.5 collective-permute-start.10
  59.7 1.3 collective-permute-start.9
  61.0 5.4 %collective-permute-start.8 = (bf16[384,896]{1,0:T(8,128)(2,1)}, bf16[384,896]{1,0:T(8,128)(2,1)}, u32[]{:S(2)}, u32[]{:S(2)}) collective-permute-start(bf16[384,896]{1,0:T(8,128)(2,1)} %slice.36), channel_id=1, source_target_pairs={{0,2},{1,3},{2,6},{3,7},{6,4},{7,5},{12,14},{13,15},{14,10},{15,11... | collective-permute-start | bytes 2064392 | tf_op jit(solution)/shard_map/ppermute | solution.py:74
  68.0 6.8 %shard_map.101 = (f32[1024,64]{1,0:T(8,128)S(1)}, f32[1024,64]{1,0:T(8,128)S(1)}, f32[1024,1]{1,0:T(8,128)S(1)}, f32[1024,1]{1,0:T(8,128)S(1)}) custom-call(s32[10]{0:T(128)S(1)} %concatenate.6.info, s32[32,24]{1,0:T(8,128)S(1)} %maximum_convert_fusion.mask_ref, bf16[1024,896]{1,0:T(8,128)(2,1)S(1)} %bitcast.28, ...), custom_call_target="tpu_custom_call" | custom-call | flops 2415919104 | tf_op jit(solution)/shard_map/pallas_call | solution.py:663
  74.9 3.3 %shard_map.102 = (bf16[128,896]{1,0:T(8,128)(2,1)S(1)}, bf16[128,768]{1,0:T(8,128)(2,1)S(1)}, bf16[256,64]{1,0:T(8,128)(2,1)S(1)}) custom-call(s32[10]{0:T(128)S(1)} %concatenate.6.info, bf16[1024,896]{1,0:T(8,128)(2,1)S(1)} %bitcast.29, bf16[256,1024]{1,0:T(8,128)(2,1)S(1)} %collective-permute-done.interp_ref, f32[32,512]{1,0:T(8,128)S(1)} %slice_add_fusion.table_ref), custom_call_target="tpu_custom_call" | custom-call | tf_op jit(solution)/shard_map/pallas_call | solution.py:670
  78.9 1.1 pad_maximum_fusion.pieces_ref
  81.1 5.0 %collective-permute-start.15 = (bf16[128,896]{1,0:T(8,128)(2,1)S(1)}, bf16[128,896]{1,0:T(8,128)(2,1)S(1)}, u32[]{:S(2)}, u32[]{:S(2)}) collective-permute-start(bf16[128,896]{1,0:T(8,128)(2,1)S(1)} %get-tuple-element.68.m0), channel_id=1, source_target_pairs={{0,4},{1,5},{2,6},{3,7},{6,2},{7,3},{4,0},{5,1},{12,8},{13,9},{14,... | collective-permute-start | bytes 688136 | tf_op jit(solution)/shard_map/ppermute | solution.py:74
  86.1 1.5 collective-permute-start.13
  87.5 1.4 broadcast_select_fusion.2
  89.9 6.2 %collective-permute-done.15.m3 = bf16[128,896]{1,0:T(8,128)(2,1)S(1)} collective-permute-done((bf16[128,896]{1,0:T(8,128)(2,1)S(1)}, bf16[128,896]{1,0:T(8,128)(2,1)S(1)}, u32[]{:S(2)}, u32[]{:S(2)}) %collective-permute-start.15) | collective-permute-done | bytes 229408 | tf_op jit(solution)/shard_map/ppermute | solution.py:74
  96.2 1.2 collective-permute-done.13.m1
  97.4 1.5 collective-permute-start.21
  98.8 4.6 %collective-permute-start.20 = (bf16[640,896]{1,0:T(8,128)(2,1)S(1)}, bf16[640,896]{1,0:T(8,128)(2,1)S(1)}, u32[]{:S(2)}, u32[]{:S(2)}) collective-permute-start(bf16[640,896]{1,0:T(8,128)(2,1)S(1)} %slice.37), channel_id=1, source_target_pairs={{0,2},{1,3},{2,6},{3,7},{6,4},{7,5},{12,14},{13,15},{14,10},{15,11... | collective-permute-start | bytes 3440648 | tf_op jit(solution)/shard_map/ppermute | solution.py:74
  103.5 1.3 shard_map.104
  104.8 1.4 collective-permute-start.18
  106.6 1.3 collective-permute-start.17
  109.7 15.3 %collective-permute-done.21 = bf16[640,896]{1,0:T(8,128)(2,1)S(1)} collective-permute-done((bf16[640,896]{1,0:T(8,128)(2,1)S(1)}, bf16[640,896]{1,0:T(8,128)(2,1)S(1)}, u32[]{:S(2)}, u32[]{:S(2)}) %collective-permute-start.21) | collective-permute-done | bytes 1146912 | tf_op jit(solution)/shard_map/ppermute | solution.py:74
  125.0 1.4 collective-permute-done.20
  127.6 3.5 %collective-permute-start.27 = (bf16[128,64]{1,0:T(8,128)(2,1)S(1)}, bf16[128,64]{1,0:T(8,128)(2,1)S(1)}, u32[]{:S(2)}, u32[]{:S(2)}) collective-permute-start(bf16[128,64]{1,0:T(8,128)(2,1)S(1)} %shard_map.106), channel_id=1, source_target_pairs={{24,0},{25,1},{26,2},{27,3},{28,4},{29,5},{30,6},{31,7},{16,8},{17... | collective-permute-start | bytes 49160 | tf_op jit(solution)/shard_map/ppermute | solution.py:89
  131.1 2.2 %collective-permute-start.26 = (bf16[128,64]{1,0:T(8,128)(2,1)S(1)}, bf16[128,64]{1,0:T(8,128)(2,1)S(1)}, u32[]{:S(2)}, u32[]{:S(2)}) collective-permute-start(bf16[128,64]{1,0:T(8,128)(2,1)S(1)} %shard_map.106), channel_id=1, source_target_pairs={{16,0},{17,1},{18,2},{19,3},{20,4},{21,5},{22,6},{23,7},{24,8},{25... | collective-permute-start | bytes 49160 | tf_op jit(solution)/shard_map/ppermute | solution.py:89
  133.3 4.5 %collective-permute-start.25 = (bf16[128,896]{1,0:T(8,128)(2,1)S(1)}, bf16[128,896]{1,0:T(8,128)(2,1)S(1)}, u32[]{:S(2)}, u32[]{:S(2)}) collective-permute-start(bf16[128,896]{1,0:T(8,128)(2,1)S(1)} %shard_map.105), channel_id=1, source_target_pairs={{24,0},{25,1},{26,2},{27,3},{28,4},{29,5},{30,6},{31,7},{0,24},{1,... | collective-permute-start | bytes 688136 | tf_op jit(solution)/shard_map/ppermute | solution.py:89
  137.9 15.3 %shard_map.107 = (f32[1024,64]{1,0:T(8,128)S(1)}, f32[1024,64]{1,0:T(8,128)S(1)}, bf16[1024,192]{1,0:T(8,128)(2,1)S(1)}) custom-call(s32[10]{0:T(128)S(1)} %concatenate.6.info, s32[32,24]{1,0:T(8,128)S(1)} %maximum_convert_fusion.mask_ref, bf16[1024,896]{1,0:T(8,128)(2,1)S(1)} %bitcast.31, bf16[1024,896]{1,0:T(8,128)(2,1)} %collective-permute-done.5.other_ref.q2.x2_ref, ...), custom_call_target="tpu_custom_call" | custom-call | flops 6442450944 | tf_op jit(solution)/shard_map/pallas_call | solution.py:725
  153.2 1.0 collective-permute-done.24.rest_2_
  154.3 10.3 %shard_map.108 = bf16[512,640]{1,0:T(8,128)(2,1)S(1)} custom-call(s32[10]{0:T(128)S(1)} %concatenate.6.info, s32[32,24]{1,0:T(8,128)S(1)} %maximum_convert_fusion.mask_ref, bf16[1024,896]{1,0:T(8,128)(2,1)S(1)} %bitcast.32, bf16[1024,896]{1,0:T(8,128)(2,1)} %collective-permute-done.5.other_ref.q2.x2_ref, f32[1024,1]{1,0:T(8,128)S(1)} %copy-done.2, ...), custom_call_target="tpu_custom_call" | custom-call | flops 3221225472 | tf_op jit(solution)/shard_map/pallas_call | solution.py:735
  164.5 22.1 %all_to_all.23 = bf16[32,16,640]{2,1,0:T(8,128)(2,1)S(1)} all-to-all(bf16[32,16,640]{2,1,0:T(8,128)(2,1)S(1)} %bitcast.34), channel_id=1, replica_groups=mesh['leaf'=32] {'leaf'}, dimensions={0} | all-to-all | bytes 1310720 | tf_op jit(solution)/shard_map/all_to_all | solution.py:747
  186.7 1.7 shard_map.109
  (75 shorter events, 10.7 us)
Async XLA Ops:
  6.6 50.7 %all-to-all-start = ((bf16[32,32,896]{2,1,0:T(8,128)(2,1)}), bf16[32,32,896]{2,1,0:T(8,128)(2,1)S(1)}, u32[]{:S(2)}, u32[]{:S(2)}) async-start(bf16[32,32,896]{2,1,0:T(8,128)(2,1)} %bitcast.35), calls=%async_computation | async-start | bytes 3670016 | tf_op jit(solution)/shard_map/all_to_all | solution.py:607
  13.9 39.8 %collective-permute-start = (bf16[256,1024]{1,0:T(8,128)(2,1)}, bf16[256,1024]{1,0:T(8,128)(2,1)S(1)}, u32[]{:S(2)}, u32[]{:S(2)}) collective-permute-start(bf16[256,1024]{1,0:T(8,128)(2,1)} %bitcast.4), channel_id=1, source_target_pairs={{0,0},{1,1},{2,2},{3,3},{4,6},{5,7},{6,4},{7,5},{8,12},{9,13},{10,... | collective-permute-start | bytes 1572872 | tf_op jit(solution)/shard_map/ppermute | solution.py:634
  15.6 38.1 %collective-permute-start.1 = (bf16[128,512]{1,0:T(8,128)(2,1)S(1)}, bf16[128,512]{1,0:T(8,128)(2,1)S(1)}, u32[]{:S(2)}, u32[]{:S(2)}) collective-permute-start(bf16[128,512]{1,0:T(8,128)(2,1)S(1)} %slice.29), channel_id=1, source_target_pairs={{0,0},{1,1},{2,2},{3,3},{4,6},{5,7},{6,4},{7,5},{8,12},{9,13},{10,... | collective-permute-start | bytes 393224 | tf_op jit(solution)/shard_map/ppermute | solution.py:635
  16.3 37.4 %collective-permute-start.4 = (bf16[112,512]{1,0:T(8,128)(2,1)S(1)}, bf16[112,512]{1,0:T(8,128)(2,1)S(1)}, u32[]{:S(2)}, u32[]{:S(2)}) collective-permute-start(bf16[112,512]{1,0:T(8,128)(2,1)S(1)} %get-tuple-element.94), channel_id=1, source_target_pairs={{0,6},{1,7},{2,4},{3,5},{4,2},{5,3},{6,0},{7,1},{8,14},{9,15},{10,... | collective-permute-start | bytes 344072 | tf_op jit(solution)/shard_map/ppermute | solution.py:637
  22.5 31.1 %collective-permute-start.3 = (bf16[112,512]{1,0:T(8,128)(2,1)S(1)}, bf16[112,512]{1,0:T(8,128)(2,1)S(1)}, u32[]{:S(2)}, u32[]{:S(2)}) collective-permute-start(bf16[112,512]{1,0:T(8,128)(2,1)S(1)} %get-tuple-element.94), channel_id=1, source_target_pairs={{0,4},{1,5},{2,6},{3,7},{4,0},{5,1},{6,2},{7,3},{8,12},{9,13},{10,... | collective-permute-start | bytes 344072 | tf_op jit(solution)/shard_map/ppermute | solution.py:637
  22.5 31.1 %collective-permute-start.2 = (bf16[112,512]{1,0:T(8,128)(2,1)S(1)}, bf16[112,512]{1,0:T(8,128)(2,1)S(1)}, u32[]{:S(2)}, u32[]{:S(2)}) collective-permute-start(bf16[112,512]{1,0:T(8,128)(2,1)S(1)} %get-tuple-element.94), channel_id=1, source_target_pairs={{0,2},{1,3},{2,0},{3,1},{4,6},{5,7},{6,4},{7,5},{8,10},{9,11},{10,... | collective-permute-start | bytes 344072 | tf_op jit(solution)/shard_map/ppermute | solution.py:637
  57.3 10.8 %collective-permute-start.5 = (bf16[1024,896]{1,0:T(8,128)(2,1)S(1)}, bf16[1024,896]{1,0:T(8,128)(2,1)}, u32[]{:S(2)}, u32[]{:S(2)}) collective-permute-start(bf16[1024,896]{1,0:T(8,128)(2,1)S(1)} %bitcast.25), channel_id=1, source_target_pairs={{0,1},{1,0},{2,3},{3,2},{6,7},{7,6},{4,5},{5,4},{12,13},{13,12},{1... | collective-permute-start | bytes 5505032 | tf_op jit(solution)/shard_map/ppermute | solution.py:74
  58.2 22.9 %collective-permute-start.10 = (bf16[384,896]{1,0:T(8,128)(2,1)}, bf16[384,896]{1,0:T(8,128)(2,1)}, u32[]{:S(2)}, u32[]{:S(2)}) collective-permute-start(bf16[384,896]{1,0:T(8,128)(2,1)} %slice.36), channel_id=1, source_target_pairs={{4,12},{12,4},{5,13},{13,5},{8,16},{16,8},{9,17},{17,9},{20,28},{2... | collective-permute-start | bytes 2064392 | tf_op jit(solution)/shard_map/ppermute | solution.py:622
  59.7 21.4 %collective-permute-start.9 = (bf16[384,896]{1,0:T(8,128)(2,1)}, bf16[384,896]{1,0:T(8,128)(2,1)}, u32[]{:S(2)}, u32[]{:S(2)}) collective-permute-start(bf16[384,896]{1,0:T(8,128)(2,1)} %slice.36), channel_id=1, source_target_pairs={{2,0},{3,1},{6,2},{7,3},{4,6},{5,7},{14,12},{15,13},{10,14},{11,15... | collective-permute-start | bytes 2064392 | tf_op jit(solution)/shard_map/ppermute | solution.py:74
  61.0 20.1 %collective-permute-start.8 = (bf16[384,896]{1,0:T(8,128)(2,1)}, bf16[384,896]{1,0:T(8,128)(2,1)}, u32[]{:S(2)}, u32[]{:S(2)}) collective-permute-start(bf16[384,896]{1,0:T(8,128)(2,1)} %slice.36), channel_id=1, source_target_pairs={{0,2},{1,3},{2,6},{3,7},{6,4},{7,5},{12,14},{13,15},{14,10},{15,11... | collective-permute-start | bytes 2064392 | tf_op jit(solution)/shard_map/ppermute | solution.py:74
  67.4 11.4 %collective-permute-start.11 = (bf16[4,112,512]{2,1,0:T(8,128)(2,1)}, bf16[4,112,512]{2,1,0:T(8,128)(2,1)}, u32[]{:S(2)}, u32[]{:S(2)}) collective-permute-start(bf16[4,112,512]{2,1,0:T(8,128)(2,1)} %get-tuple-element.92), channel_id=1, source_target_pairs={{0,1},{1,0},{2,3},{3,2},{6,7},{7,6},{4,5},{5,4},{12,13},{13,12},{1... | collective-permute-start | bytes 1376264 | tf_op jit(solution)/shard_map/ppermute | solution.py:74
  78.3 1.9 collective-permute-start.6
  78.8 1.3 collective-permute-start.7
  81.1 15.0 %collective-permute-start.15 = (bf16[128,896]{1,0:T(8,128)(2,1)S(1)}, bf16[128,896]{1,0:T(8,128)(2,1)S(1)}, u32[]{:S(2)}, u32[]{:S(2)}) collective-permute-start(bf16[128,896]{1,0:T(8,128)(2,1)S(1)} %get-tuple-element.68.m0), channel_id=1, source_target_pairs={{0,4},{1,5},{2,6},{3,7},{6,2},{7,3},{4,0},{5,1},{12,8},{13,9},{14,... | collective-permute-start | bytes 688136 | tf_op jit(solution)/shard_map/ppermute | solution.py:74
  86.1 10.1 %collective-permute-start.14 = (bf16[128,896]{1,0:T(8,128)(2,1)S(1)}, bf16[128,896]{1,0:T(8,128)(2,1)S(1)}, u32[]{:S(2)}, u32[]{:S(2)}) collective-permute-start(bf16[128,896]{1,0:T(8,128)(2,1)S(1)} %get-tuple-element.68.m0), channel_id=1, source_target_pairs={{0,6},{1,7},{2,4},{3,5},{6,0},{7,1},{4,2},{5,3},{12,10},{13,11},{1... | collective-permute-start | bytes 688136 | tf_op jit(solution)/shard_map/ppermute | solution.py:74
  86.1 11.3 %collective-permute-start.13 = (bf16[128,896]{1,0:T(8,128)(2,1)S(1)}, bf16[128,896]{1,0:T(8,128)(2,1)S(1)}, u32[]{:S(2)}, u32[]{:S(2)}) collective-permute-start(bf16[128,896]{1,0:T(8,128)(2,1)S(1)} %get-tuple-element.68.m0), channel_id=1, source_target_pairs={{0,2},{1,3},{2,0},{3,1},{6,4},{7,5},{4,6},{5,7},{12,14},{13,15},{1... | collective-permute-start | bytes 688136 | tf_op jit(solution)/shard_map/ppermute | solution.py:74
  89.0 14.5 %collective-permute-start.12 = (bf16[384,896]{1,0:T(8,128)(2,1)S(1)}, bf16[384,896]{1,0:T(8,128)(2,1)S(1)}, u32[]{:S(2)}, u32[]{:S(2)}) collective-permute-start(bf16[384,896]{1,0:T(8,128)(2,1)S(1)} %get-tuple-element.90.p1a), channel_id=1, source_target_pairs={{0,1},{1,0},{2,3},{3,2},{6,7},{7,6},{4,5},{5,4},{12,13},{13,12},{1... | collective-permute-start | bytes 2064392 | tf_op jit(solution)/shard_map/ppermute | solution.py:74
  89.2 19.8 %collective-permute-start.19 = (bf16[640,896]{1,0:T(8,128)(2,1)S(1)}, bf16[640,896]{1,0:T(8,128)(2,1)S(1)}, u32[]{:S(2)}, u32[]{:S(2)}) collective-permute-start(bf16[640,896]{1,0:T(8,128)(2,1)S(1)} %slice.37), channel_id=1, source_target_pairs={{4,12},{12,4},{5,13},{13,5},{8,16},{16,8},{9,17},{17,9},{20,28},{2... | collective-permute-start | bytes 3440648 | tf_op jit(solution)/shard_map/ppermute | solution.py:622
  97.4 27.6 %collective-permute-start.21 = (bf16[640,896]{1,0:T(8,128)(2,1)S(1)}, bf16[640,896]{1,0:T(8,128)(2,1)S(1)}, u32[]{:S(2)}, u32[]{:S(2)}) collective-permute-start(bf16[640,896]{1,0:T(8,128)(2,1)S(1)} %slice.37), channel_id=1, source_target_pairs={{2,0},{3,1},{6,2},{7,3},{4,6},{5,7},{14,12},{15,13},{10,14},{11,15... | collective-permute-start | bytes 3440648 | tf_op jit(solution)/shard_map/ppermute | solution.py:74
  98.8 27.5 %collective-permute-start.20 = (bf16[640,896]{1,0:T(8,128)(2,1)S(1)}, bf16[640,896]{1,0:T(8,128)(2,1)S(1)}, u32[]{:S(2)}, u32[]{:S(2)}) collective-permute-start(bf16[640,896]{1,0:T(8,128)(2,1)S(1)} %slice.37), channel_id=1, source_target_pairs={{0,2},{1,3},{2,6},{3,7},{6,4},{7,5},{12,14},{13,15},{14,10},{15,11... | collective-permute-start | bytes 3440648 | tf_op jit(solution)/shard_map/ppermute | solution.py:74
  104.8 1.9 collective-permute-start.16
  104.8 21.7 %collective-permute-start.18 = (bf16[256,896]{1,0:T(8,128)(2,1)S(1)}, bf16[256,896]{1,0:T(8,128)(2,1)S(1)}, u32[]{:S(2)}, u32[]{:S(2)}) collective-permute-start(bf16[256,896]{1,0:T(8,128)(2,1)S(1)} %get-tuple-element.70.own_ref.half_ref), channel_id=1, source_target_pairs={{0,8},{1,9},{2,10},{3,11},{4,12},{5,13},{6,14},{7,15},{8,16},{9,17... | collective-permute-start | bytes 1376264 | tf_op jit(solution)/shard_map/ppermute | solution.py:89
  106.6 19.9 %collective-permute-start.17 = (bf16[256,896]{1,0:T(8,128)(2,1)S(1)}, bf16[256,896]{1,0:T(8,128)(2,1)S(1)}, u32[]{:S(2)}, u32[]{:S(2)}) collective-permute-start(bf16[256,896]{1,0:T(8,128)(2,1)S(1)} %get-tuple-element.70.own_ref.half_ref), channel_id=1, source_target_pairs={{8,0},{9,1},{10,2},{11,3},{12,4},{13,5},{14,6},{15,7},{16,8},{17,9... | collective-permute-start | bytes 1376264 | tf_op jit(solution)/shard_map/ppermute | solution.py:89
  109.0 17.6 %collective-permute-start.22 = (bf16[256,64]{1,0:T(8,128)(2,1)S(1)}, bf16[256,64]{1,0:T(8,128)(2,1)S(1)}, u32[]{:S(2)}, u32[]{:S(2)}) collective-permute-start(bf16[256,64]{1,0:T(8,128)(2,1)S(1)} %get-tuple-element.78), channel_id=1, source_target_pairs={{4,12},{12,4},{5,13},{13,5},{8,16},{16,8},{9,17},{17,9},{20,28},{2... | collective-permute-start | bytes 98312 | tf_op jit(solution)/shard_map/ppermute | solution.py:622
  126.3 11.5 %copy-start.8 = (f32[1024,64]{1,0:T(8,128)S(1)}, f32[1024,64]{1,0:T(8,128)}, u32[]{:S(2)}) copy-start(f32[1024,64]{1,0:T(8,128)} %copy-done.7) | copy-start | bytes 786436
  126.5 11.3 %copy-start.2 = (f32[1024,1]{1,0:T(8,128)S(1)}, f32[1024,1]{1,0:T(8,128)}, u32[]{:S(2)}) copy-start(f32[1024,1]{1,0:T(8,128)} %copy-done.1) | copy-start | bytes 12292
  126.6 11.3 %collective-permute-start.23 = (bf16[640,896]{1,0:T(8,128)(2,1)S(1)}, bf16[640,896]{1,0:T(8,128)(2,1)S(1)}, u32[]{:S(2)}, u32[]{:S(2)}) collective-permute-start(bf16[640,896]{1,0:T(8,128)(2,1)S(1)} %get-tuple-element.79.p1b), channel_id=1, source_target_pairs={{0,1},{1,0},{2,3},{3,2},{6,7},{7,6},{4,5},{5,4},{12,13},{13,12},{1... | collective-permute-start | bytes 3440648 | tf_op jit(solution)/shard_map/ppermute | solution.py:74
  127.6 25.6 %collective-permute-start.27 = (bf16[128,64]{1,0:T(8,128)(2,1)S(1)}, bf16[128,64]{1,0:T(8,128)(2,1)S(1)}, u32[]{:S(2)}, u32[]{:S(2)}) collective-permute-start(bf16[128,64]{1,0:T(8,128)(2,1)S(1)} %shard_map.106), channel_id=1, source_target_pairs={{24,0},{25,1},{26,2},{27,3},{28,4},{29,5},{30,6},{31,7},{16,8},{17... | collective-permute-start | bytes 49160 | tf_op jit(solution)/shard_map/ppermute | solution.py:89
  131.1 22.0 %collective-permute-start.26 = (bf16[128,64]{1,0:T(8,128)(2,1)S(1)}, bf16[128,64]{1,0:T(8,128)(2,1)S(1)}, u32[]{:S(2)}, u32[]{:S(2)}) collective-permute-start(bf16[128,64]{1,0:T(8,128)(2,1)S(1)} %shard_map.106), channel_id=1, source_target_pairs={{16,0},{17,1},{18,2},{19,3},{20,4},{21,5},{22,6},{23,7},{24,8},{25... | collective-permute-start | bytes 49160 | tf_op jit(solution)/shard_map/ppermute | solution.py:89
  133.3 19.9 %collective-permute-start.25 = (bf16[128,896]{1,0:T(8,128)(2,1)S(1)}, bf16[128,896]{1,0:T(8,128)(2,1)S(1)}, u32[]{:S(2)}, u32[]{:S(2)}) collective-permute-start(bf16[128,896]{1,0:T(8,128)(2,1)S(1)} %shard_map.105), channel_id=1, source_target_pairs={{24,0},{25,1},{26,2},{27,3},{28,4},{29,5},{30,6},{31,7},{0,24},{1,... | collective-permute-start | bytes 688136 | tf_op jit(solution)/shard_map/ppermute | solution.py:89
  137.8 16.5 %collective-permute-start.24 = (bf16[128,896]{1,0:T(8,128)(2,1)S(1)}, bf16[128,896]{1,0:T(8,128)(2,1)S(1)}, u32[]{:S(2)}, u32[]{:S(2)}) collective-permute-start(bf16[128,896]{1,0:T(8,128)(2,1)S(1)} %shard_map.105), channel_id=1, source_target_pairs={{16,0},{17,1},{18,2},{19,3},{20,4},{21,5},{22,6},{23,7},{24,8},{25... | collective-permute-start | bytes 688136 | tf_op jit(solution)/shard_map/ppermute | solution.py:89
  164.5 22.1 %copy-start = (s32[1,1024]{1,0:T(1,128)S(1)}, s32[1,1024]{1,0:T(1,128)}, u32[]{:S(2)}) copy-start(s32[1,1024]{1,0:T(1,128)} %get-tuple-element.46.place_ref) | copy-start | bytes 12292
  (8 other events, 49.3 us)

commit v4 on v3

--- a/solution.py
+++ b/solution.py
@@ -265,14 +265,16 @@
     for n in (0, 1):
         at = pl.ds(pl.multiple_of(n * rank + core * half, half), half)
         out_ref[n * half : (n + 1) * half, width : width + columns] = weight2_ref[at]
-    out_ref[:, width + columns :] = weight3.astype(BF16)
+    out_ref[:, width + columns : width + 2 * columns] = weight3.astype(BF16)
+    out_ref[:, width + 2 * columns : width + 3 * columns] = w1_s[:rank]
+    out_ref[:, width + 3 * columns :] = w1_s[3 * rank :]
 
 
 def level3_kernel(info, own_ref, other_ref, table_ref, out_ref):
     half = out_ref.shape[0]
     rank = 2 * half
     columns = 64
-    width = own_ref.shape[1] - 2 * columns
+    width = out_ref.shape[1] - 2 * columns
     core = info[CORE]
     index = node_picks(table_of(table_ref, info[AT]), rank, 3, 4 * core, 4)
     entry = index % rank
@@ -281,8 +283,8 @@
     mine = (hit & (entry // half == core)).astype(BF16)
     theirs = (hit & (entry // half != core)).astype(BF16)
     out_ref[:, :width] = (mm(mine, own_ref[:, :width]) + mm(theirs, other_ref[:, :width])).astype(BF16)
-    out_ref[:, width : width + columns] = own_ref[:half, width + columns :]
-    out_ref[:, width + columns :] = own_ref[half:, width + columns :]
+    out_ref[:, width : width + columns] = own_ref[:half, width + columns : width + 2 * columns]
+    out_ref[:, width + columns :] = own_ref[half:, width + columns : width + 2 * columns]
 
 
 def level4_kernel(info, weight3_ref, next_ref, before_ref, pieces_ref, out_ref):
@@ -358,7 +360,7 @@
 
     def spread_of(i, distance, part, source):
         if distance == 1:
-            w3 = part[:, width + columns :]
+            w3 = part[:, width + columns : width + 2 * columns]
         else:
             w3 = jnp.concatenate([part[:, width : width + columns], part[:, width + columns :]])
         step = source // 2 - info[AT] // 2
@@ -514,21 +516,23 @@
     return sums, acc
 
 
-def pair_kernel(scale_inv, width, info, mask_ref, q1, q2, c1, c2, p1a, p1b, p2a, p2b, ra, rb, w_all, w_cross,
+def pair_kernel(scale_inv, width, info, mask_ref, q1, q2, c1, c2, p1a, p1b, p2a, p2b, ra, rb, w_all, w_next, w_before,
                 init1, init2, table_ref, out1, out2, result, p1, p2, r):
     for ref, parts in ((p1, (p1a, p1b)), (p2, (p2a, p2b)), (r, (ra, rb))):
         join(ref, *parts)
     columns = out1.shape[1]
     masks, names, r_leaf = pair_masks(info, mask_ref)
     refs = (q1, q2, p1, p2)
-    chip, rank = info[CHIP], w_cross.shape[0]
+    chip, rank = info[CHIP], w_next.shape[0]
     last = w_all.shape[0] // rank - 1
 
-    def of(index, inside):
+    def of(index, inside, w_cross):
         at = pl.ds(pl.multiple_of(jnp.clip(index, 0, last) * rank, rank), rank)
-        return jnp.where(inside, w_all[at], w_cross[...])
-
-    w_q, w_p, w_r = of(chip, True), of(chip - 1, chip > 0), of(chip + 1, chip < last)
+        return jnp.where(inside, w_all[at], w_cross)
+
+    over_next, over_before = w_next[:, :columns], w_before[:, columns:]
+    w_q = of(chip, True, over_next)
+    w_p, w_r = of(chip - 1, chip > 0, over_before), of(chip + 1, chip < last, over_next)
     r_weights = leaf_weights(r, width, columns, w_r, table_ref, r_leaf)
     r_row = as_row(row_offset(r[:, :width], scale_inv))
     acc = jnp.zeros((2 * columns, r.shape[0]), F32)
@@ -580,7 +584,7 @@
     wide = width + -(-(columns + 16 + lanes) // 128) * 128
     half = rank // 2
     scale_inv = 1.0 / (1.75 * math.sqrt(width))
-    message = width + 2 * columns
+    message, message2 = width + 2 * columns, width + 4 * columns
     slots = slot_sources(groups)
     away = [a for a, _ in slots]
 
@@ -688,19 +692,18 @@
 
     behind_a, ahead_a = merged(behind_a, ahead_a, over_a)
     plane = [move(sent, lambda i, k=k: i ^ (2 * k)) for k in (1, 2, 3)]
-    cross1 = over_end(after(weight1, sent))
     behind_other_a = move(behind_a, lambda i: i ^ 1)
     behind_b, ahead_b = halo(after(got_b, *plane))
     half2, weight2, weight3, weight1_all = call(
         level23_kernel,
         prefetch(1, (), [whole((half, message))] * 4 + [whole(piece_shape)],
-                 [whole((rank, message)), whole((2 * rank, columns)), whole((rank, columns)), whole((4 * rank, columns))]),
-        shapes(((rank, message), BF16), ((2 * rank, columns), BF16), ((rank, columns), BF16), ((4 * rank, columns), BF16)),
+                 [whole((rank, message2)), whole((2 * rank, columns)), whole((rank, columns)), whole((4 * rank, columns))]),
+        shapes(((rank, message2), BF16), ((2 * rank, columns), BF16), ((rank, columns), BF16), ((4 * rank, columns), BF16)),
     )(info, after(sent, behind_other_a), *plane, pieces)
     half2_other = move(half2, lambda i: i ^ 1)
     half3 = call(
         level3_kernel,
-        prefetch(1, (), [whole((rank, message))] * 2 + [whole(table_shape)], whole((half, message))),
+        prefetch(1, (), [whole((rank, message2))] * 2 + [whole(table_shape)], whole((half, message))),
         jax.ShapeDtypeStruct((half, message), BF16),
     )(info, half2, half2_other, tables)
     half3_late = after(half3, over_b)
@@ -718,23 +721,24 @@
         for h in (0, 1):
             found = [[2 * (g // 2 + s) + (g % 2 ^ h) for s in steps if 0 <= g // 2 + s < nodes4] for g in range(groups)]
             weight4.append(send_each(half4, [f[0] if f else -1 for f in found]))
-    weight_1, sums, leaf_c = whole((rank, columns)), whole((rows, columns)), whole((rows, 1))
+    ends1 = pl.BlockSpec((rank, 2 * columns), lambda *_: (0, message // (2 * columns)))
+    sums, leaf_c = whole((rows, columns)), whole((rows, 1))
     behind_b, ahead_b = merged(behind_b, ahead_b, over_b)
-    before_b = after(behind_b, ahead_b, half3, cross1, *far_parts[:2])
+    before_b = after(behind_b, ahead_b, half3, *far_parts[:2])
     behind_other = [behind_other_a, move(before_b, lambda i: i ^ 1)]
     pair_1, pair_2, pair_sum = call(
         functools.partial(pair_kernel, scale_inv, width),
-        prefetch(2, (), [leaf_x] * 2 + [leaf_c] * 2 + [whole((cut, wide)), whole((rows - cut, wide))] * 3 + [whole((4 * rank, columns)), weight_1] + [sums] * 2 + [whole(table_shape)],
+        prefetch(2, (1,), [leaf_x] * 2 + [leaf_c] * 2 + [whole((cut, wide)), whole((rows - cut, wide))] * 3 + [whole((4 * rank, columns)), ends1, ends1] + [sums] * 2 + [whole(table_shape)],
                  [sums] * 2 + [whole((rows, 3 * columns))], [joined] * 3),
         shapes(((rows, columns), F32), ((rows, columns), F32), ((rows, 3 * columns), BF16)),
         flops=8 * rows * rows * width,
     )(info, masks, after(got, half4), other, own_column, other_column, behind_a, behind_b,
-      *behind_other, ahead_a, ahead_b, weight1_all, cross1, own_sum, other_sum, tables)
+      *behind_other, ahead_a, ahead_b, weight1_all, far_parts[0], far_parts[1], own_sum, other_sum, tables)
 
     sides = 2 if per_peer % 32 == 0 else 1
     all_sums = call(
         functools.partial(far_kernel, away, len(steps4), sides, per_peer // sides, scale_inv, width),
-        prefetch(2, (), [leaf_x] * 2 + [leaf_c] * 2 + [whole((rank, message)), whole((2 * rank, columns)),
+        prefetch(2, (), [leaf_x] * 2 + [leaf_c] * 2 + [whole((rank, message2)), whole((2 * rank, columns)),
                  whole(table_shape), sums, sums, whole((rows, 3 * columns))]
                  + [whole(p.shape) for p in (*far_parts, *weight4)], whole((rows // sides, 5 * sides * columns)),
                  [pltpu.VMEM((rows, columns), F32)] * 2

time: 189 us -> 189 us (level)
  transfers between devices with their start and end apart: 29 -> 28, of which waited for: 9 -> 9; matrix products, arithmetic and copies ran while one was open for 3% -> 3% of each run, Pallas kernels for 16% -> 16%
where the time goes in v4:
time: 189 us; the launch traced here: 188 us
  waiting for transfers between devices  59.7 us (32%)
  starting transfers between devices  51.2 us (27%)
  Pallas kernels  48.8 us (26%)
  blocking collectives  22.1 us (12%)
  other arithmetic  3.99 us (2%)
  local copies, waits for them, and re-layouts  2.23 us (1%)
    ppermute x3, waiting for transfers between devices, local(): lax.ppermute(upper, 'leaf', [(i, i ^ 2 * k) for i in range(leaves)])  29.7 us
    ppermute x14, waiting for transfers between devices, move(): return lax.ppermute(value, 'leaf', pairs)  25.3 us
    all_to_all x1, blocking collectives, local(): lax.all_to_all(all_sums, 'leaf', split_axis=0, concat_axis=0, tiled=True)  22.1 us
    ppermute x14, starting transfers between devices, move(): return lax.ppermute(value, 'leaf', pairs)  19.5 us
    pallas_call x1, Pallas kernels, local(): call(functools.partial(pair_kernel, scale_inv, width), prefetch(2, (1,),...  15.3 us
    ppermute x6, starting transfers between devices, send_each(): return lax.ppermute(value, 'leaf', pairs)  12.9 us
    pallas_call x1, Pallas kernels, local(): call(functools.partial(far_kernel, away, len(steps4), sides, per_peer //...  10.3 us
    all_to_all x1, starting transfers between devices, local(): got = lax.all_to_all(send, 'leaf', split_axis=0, concat_axis=0, tiled=True)  7.29 us
  transfers between devices with their start and end apart: 28, of which 9 were waited for; matrix products, arithmetic and copies ran while one was open for 3% of the time, Pallas kernels for 16%

profile of v4, /device:TPU:0, one launch (start us, length us, event | category | flops | bytes accessed | tf_op | source)
XLA Modules:
  0.0 188.3 jit_solution(1991603727624359365)
XLA Ops:
  0.0 6.6 %shard_map.100 = (bf16[1024,896]{1,0:T(8,128)(2,1)}, s32[1,1024]{1,0:T(1,128)}) custom-call(s32[1,1024]{1,0:T(1,128)} %bitcast.42, bf16[1024,768]{1,0:T(8,128)(2,1)} %points_ref.1, bf16[64,1024]{1,0:T(8,128)(2,1)} %bitcast.38, s32[1,256]{1,0:T(1,128)} %skel_ref.1, s32[1,240]{1,0:T(1,128)} %merge_ref.1, s32[1,8]{1,0:T(1,128)} %near_ref.1, s32[1,4,4]{2,1,0:T(4,128)} %far_ref.1), custom_call_target="tpu_custom_call" | custom-call | tf_op jit(solution)/shard_map/pallas_call | solution.py:596
  6.6 7.3 %all-to-all-start = ((bf16[32,32,896]{2,1,0:T(8,128)(2,1)}), bf16[32,32,896]{2,1,0:T(8,128)(2,1)S(1)}, u32[]{:S(2)}, u32[]{:S(2)}) async-start(bf16[32,32,896]{2,1,0:T(8,128)(2,1)} %bitcast.35), calls=%async_computation | async-start | bytes 3670016 | tf_op jit(solution)/shard_map/all_to_all | solution.py:611
  13.9 1.7 collective-permute-start
  16.3 6.2 %collective-permute-start.4 = (bf16[112,512]{1,0:T(8,128)(2,1)S(1)}, bf16[112,512]{1,0:T(8,128)(2,1)S(1)}, u32[]{:S(2)}, u32[]{:S(2)}) collective-permute-start(bf16[112,512]{1,0:T(8,128)(2,1)S(1)} %get-tuple-element.90), channel_id=1, source_target_pairs={{0,6},{1,7},{2,4},{3,5},{4,2},{5,3},{6,0},{7,1},{8,14},{9,15},{10,... | collective-permute-start | bytes 344072 | tf_op jit(solution)/shard_map/ppermute | solution.py:641
  23.9 29.7 %collective-permute-done.4 = bf16[112,512]{1,0:T(8,128)(2,1)S(1)} collective-permute-done((bf16[112,512]{1,0:T(8,128)(2,1)S(1)}, bf16[112,512]{1,0:T(8,128)(2,1)S(1)}, u32[]{:S(2)}, u32[]{:S(2)}) %collective-permute-start.4) | collective-permute-done | bytes 114720 | tf_op jit(solution)/shard_map/ppermute | solution.py:641
  53.7 3.6 %all-to-all-done = bf16[32,32,896]{2,1,0:T(8,128)(2,1)S(1)} async-done(((bf16[32,32,896]{2,1,0:T(8,128)(2,1)}), bf16[32,32,896]{2,1,0:T(8,128)(2,1)S(1)}, u32[]{:S(2)}, u32[]{:S(2)}) %all-to-all-start) | async-done | bytes 1835040 | tf_op jit(solution)/shard_map/all_to_all | solution.py:611
  58.2 1.5 collective-permute-start.10
  59.7 1.3 collective-permute-start.9
  61.0 5.4 %collective-permute-start.8 = (bf16[384,896]{1,0:T(8,128)(2,1)}, bf16[384,896]{1,0:T(8,128)(2,1)}, u32[]{:S(2)}, u32[]{:S(2)}) collective-permute-start(bf16[384,896]{1,0:T(8,128)(2,1)} %slice.36), channel_id=1, source_target_pairs={{0,2},{1,3},{2,6},{3,7},{6,4},{7,5},{12,14},{13,15},{14,10},{15,11... | collective-permute-start | bytes 2064392 | tf_op jit(solution)/shard_map/ppermute | solution.py:74
  68.0 6.8 %shard_map.101 = (f32[1024,64]{1,0:T(8,128)S(1)}, f32[1024,64]{1,0:T(8,128)S(1)}, f32[1024,1]{1,0:T(8,128)S(1)}, f32[1024,1]{1,0:T(8,128)S(1)}) custom-call(s32[10]{0:T(128)S(1)} %concatenate.6.info, s32[32,24]{1,0:T(8,128)S(1)} %maximum_convert_fusion.mask_ref, bf16[1024,896]{1,0:T(8,128)(2,1)S(1)} %bitcast.28, ...), custom_call_target="tpu_custom_call" | custom-call | flops 2415919104 | tf_op jit(solution)/shard_map/pallas_call | solution.py:667
  74.9 3.3 %shard_map.102 = (bf16[128,896]{1,0:T(8,128)(2,1)S(1)}, bf16[128,768]{1,0:T(8,128)(2,1)S(1)}, bf16[256,64]{1,0:T(8,128)(2,1)S(1)}) custom-call(s32[10]{0:T(128)S(1)} %concatenate.6.info, bf16[1024,896]{1,0:T(8,128)(2,1)S(1)} %bitcast.29, bf16[256,1024]{1,0:T(8,128)(2,1)S(1)} %collective-permute-done.interp_ref, f32[32,512]{1,0:T(8,128)S(1)} %slice_add_fusion.table_ref), custom_call_target="tpu_custom_call" | custom-call | tf_op jit(solution)/shard_map/pallas_call | solution.py:674
  78.9 1.1 pad_maximum_fusion.pieces_ref
  80.2 1.5 shard_map.103
  81.7 4.4 %collective-permute-start.15 = (bf16[128,896]{1,0:T(8,128)(2,1)S(1)}, bf16[128,896]{1,0:T(8,128)(2,1)S(1)}, u32[]{:S(2)}, u32[]{:S(2)}) collective-permute-start(bf16[128,896]{1,0:T(8,128)(2,1)S(1)} %get-tuple-element.66.m0), channel_id=1, source_target_pairs={{0,4},{1,5},{2,6},{3,7},{6,2},{7,3},{4,0},{5,1},{12,8},{13,9},{14,... | collective-permute-start | bytes 688136 | tf_op jit(solution)/shard_map/ppermute | solution.py:74
  86.1 1.5 collective-permute-start.13
  87.5 1.4 broadcast_select_fusion.2
  89.9 6.2 %collective-permute-done.15.m3 = bf16[128,896]{1,0:T(8,128)(2,1)S(1)} collective-permute-done((bf16[128,896]{1,0:T(8,128)(2,1)S(1)}, bf16[128,896]{1,0:T(8,128)(2,1)S(1)}, u32[]{:S(2)}, u32[]{:S(2)}) %collective-permute-start.15) | collective-permute-done | bytes 229408 | tf_op jit(solution)/shard_map/ppermute | solution.py:74
  96.2 1.2 collective-permute-done.13.m1
  97.4 1.5 collective-permute-start.21
  98.9 4.6 %collective-permute-start.20 = (bf16[640,896]{1,0:T(8,128)(2,1)S(1)}, bf16[640,896]{1,0:T(8,128)(2,1)S(1)}, u32[]{:S(2)}, u32[]{:S(2)}) collective-permute-start(bf16[640,896]{1,0:T(8,128)(2,1)S(1)} %slice.37), channel_id=1, source_target_pairs={{0,2},{1,3},{2,6},{3,7},{6,4},{7,5},{12,14},{13,15},{14,10},{15,11... | collective-permute-start | bytes 3440648 | tf_op jit(solution)/shard_map/ppermute | solution.py:74
  103.5 1.3 shard_map.104
  104.9 1.4 collective-permute-start.18
  106.8 1.3 collective-permute-start.17
  109.1 15.9 %collective-permute-done.21 = bf16[640,896]{1,0:T(8,128)(2,1)S(1)} collective-permute-done((bf16[640,896]{1,0:T(8,128)(2,1)S(1)}, bf16[640,896]{1,0:T(8,128)(2,1)S(1)}, u32[]{:S(2)}, u32[]{:S(2)}) %collective-permute-start.21) | collective-permute-done | bytes 1146912 | tf_op jit(solution)/shard_map/ppermute | solution.py:74
  125.0 1.4 collective-permute-done.20
  127.6 3.7 %collective-permute-start.26 = (bf16[128,64]{1,0:T(8,128)(2,1)S(1)}, bf16[128,64]{1,0:T(8,128)(2,1)S(1)}, u32[]{:S(2)}, u32[]{:S(2)}) collective-permute-start(bf16[128,64]{1,0:T(8,128)(2,1)S(1)} %shard_map.106), channel_id=1, source_target_pairs={{24,0},{25,1},{26,2},{27,3},{28,4},{29,5},{30,6},{31,7},{16,8},{17... | collective-permute-start | bytes 49160 | tf_op jit(solution)/shard_map/ppermute | solution.py:89
  131.3 2.0 %collective-permute-start.25 = (bf16[128,64]{1,0:T(8,128)(2,1)S(1)}, bf16[128,64]{1,0:T(8,128)(2,1)S(1)}, u32[]{:S(2)}, u32[]{:S(2)}) collective-permute-start(bf16[128,64]{1,0:T(8,128)(2,1)S(1)} %shard_map.106), channel_id=1, source_target_pairs={{16,0},{17,1},{18,2},{19,3},{20,4},{21,5},{22,6},{23,7},{24,8},{25... | collective-permute-start | bytes 49160 | tf_op jit(solution)/shard_map/ppermute | solution.py:89
  133.3 4.5 %collective-permute-start.24 = (bf16[128,896]{1,0:T(8,128)(2,1)S(1)}, bf16[128,896]{1,0:T(8,128)(2,1)S(1)}, u32[]{:S(2)}, u32[]{:S(2)}) collective-permute-start(bf16[128,896]{1,0:T(8,128)(2,1)S(1)} %shard_map.105), channel_id=1, source_target_pairs={{24,0},{25,1},{26,2},{27,3},{28,4},{29,5},{30,6},{31,7},{0,24},{1,... | collective-permute-start | bytes 688136 | tf_op jit(solution)/shard_map/ppermute | solution.py:89
  137.9 15.3 %shard_map.107 = (f32[1024,64]{1,0:T(8,128)S(1)}, f32[1024,64]{1,0:T(8,128)S(1)}, bf16[1024,192]{1,0:T(8,128)(2,1)S(1)}) custom-call(s32[10]{0:T(128)S(1)} %concatenate.6.info, s32[32,24]{1,0:T(8,128)S(1)} %maximum_convert_fusion.mask_ref, bf16[1024,896]{1,0:T(8,128)(2,1)S(1)} %bitcast.31, bf16[1024,896]{1,0:T(8,128)(2,1)} %collective-permute-done.5.other_ref.q2.x2_ref, ...), custom_call_target="tpu_custom_call" | custom-call | flops 6442450944 | tf_op jit(solution)/shard_map/pallas_call | solution.py:729
  154.3 10.3 %shard_map.108 = bf16[512,640]{1,0:T(8,128)(2,1)S(1)} custom-call(s32[10]{0:T(128)S(1)} %concatenate.6.info, s32[32,24]{1,0:T(8,128)S(1)} %maximum_convert_fusion.mask_ref, bf16[1024,896]{1,0:T(8,128)(2,1)S(1)} %bitcast.32, bf16[1024,896]{1,0:T(8,128)(2,1)} %collective-permute-done.5.other_ref.q2.x2_ref, f32[1024,1]{1,0:T(8,128)S(1)} %copy-done.2, ...), custom_call_target="tpu_custom_call" | custom-call | flops 3221225472 | tf_op jit(solution)/shard_map/pallas_call | solution.py:739
  164.6 22.1 %all_to_all.23 = bf16[32,16,640]{2,1,0:T(8,128)(2,1)S(1)} all-to-all(bf16[32,16,640]{2,1,0:T(8,128)(2,1)S(1)} %bitcast.34), channel_id=1, replica_groups=mesh['leaf'=32] {'leaf'}, dimensions={0} | all-to-all | bytes 1310720 | tf_op jit(solution)/shard_map/all_to_all | solution.py:751
  186.7 1.7 shard_map.109
  (73 shorter events, 10.3 us)
Async XLA Ops:
  6.6 50.7 %all-to-all-start = ((bf16[32,32,896]{2,1,0:T(8,128)(2,1)}), bf16[32,32,896]{2,1,0:T(8,128)(2,1)S(1)}, u32[]{:S(2)}, u32[]{:S(2)}) async-start(bf16[32,32,896]{2,1,0:T(8,128)(2,1)} %bitcast.35), calls=%async_computation | async-start | bytes 3670016 | tf_op jit(solution)/shard_map/all_to_all | solution.py:611
  13.9 39.8 %collective-permute-start = (bf16[256,1024]{1,0:T(8,128)(2,1)}, bf16[256,1024]{1,0:T(8,128)(2,1)S(1)}, u32[]{:S(2)}, u32[]{:S(2)}) collective-permute-start(bf16[256,1024]{1,0:T(8,128)(2,1)} %bitcast.4), channel_id=1, source_target_pairs={{0,0},{1,1},{2,2},{3,3},{4,6},{5,7},{6,4},{7,5},{8,12},{9,13},{10,... | collective-permute-start | bytes 1572872 | tf_op jit(solution)/shard_map/ppermute | solution.py:638
  15.6 38.1 %collective-permute-start.1 = (bf16[128,512]{1,0:T(8,128)(2,1)S(1)}, bf16[128,512]{1,0:T(8,128)(2,1)S(1)}, u32[]{:S(2)}, u32[]{:S(2)}) collective-permute-start(bf16[128,512]{1,0:T(8,128)(2,1)S(1)} %slice.29), channel_id=1, source_target_pairs={{0,0},{1,1},{2,2},{3,3},{4,6},{5,7},{6,4},{7,5},{8,12},{9,13},{10,... | collective-permute-start | bytes 393224 | tf_op jit(solution)/shard_map/ppermute | solution.py:639
  16.3 37.4 %collective-permute-start.4 = (bf16[112,512]{1,0:T(8,128)(2,1)S(1)}, bf16[112,512]{1,0:T(8,128)(2,1)S(1)}, u32[]{:S(2)}, u32[]{:S(2)}) collective-permute-start(bf16[112,512]{1,0:T(8,128)(2,1)S(1)} %get-tuple-element.90), channel_id=1, source_target_pairs={{0,6},{1,7},{2,4},{3,5},{4,2},{5,3},{6,0},{7,1},{8,14},{9,15},{10,... | collective-permute-start | bytes 344072 | tf_op jit(solution)/shard_map/ppermute | solution.py:641
  22.5 31.1 %collective-permute-start.3 = (bf16[112,512]{1,0:T(8,128)(2,1)S(1)}, bf16[112,512]{1,0:T(8,128)(2,1)S(1)}, u32[]{:S(2)}, u32[]{:S(2)}) collective-permute-start(bf16[112,512]{1,0:T(8,128)(2,1)S(1)} %get-tuple-element.90), channel_id=1, source_target_pairs={{0,4},{1,5},{2,6},{3,7},{4,0},{5,1},{6,2},{7,3},{8,12},{9,13},{10,... | collective-permute-start | bytes 344072 | tf_op jit(solution)/shard_map/ppermute | solution.py:641
  22.5 31.1 %collective-permute-start.2 = (bf16[112,512]{1,0:T(8,128)(2,1)S(1)}, bf16[112,512]{1,0:T(8,128)(2,1)S(1)}, u32[]{:S(2)}, u32[]{:S(2)}) collective-permute-start(bf16[112,512]{1,0:T(8,128)(2,1)S(1)} %get-tuple-element.90), channel_id=1, source_target_pairs={{0,2},{1,3},{2,0},{3,1},{4,6},{5,7},{6,4},{7,5},{8,10},{9,11},{10,... | collective-permute-start | bytes 344072 | tf_op jit(solution)/shard_map/ppermute | solution.py:641
  57.3 10.8 %collective-permute-start.5 = (bf16[1024,896]{1,0:T(8,128)(2,1)S(1)}, bf16[1024,896]{1,0:T(8,128)(2,1)}, u32[]{:S(2)}, u32[]{:S(2)}) collective-permute-start(bf16[1024,896]{1,0:T(8,128)(2,1)S(1)} %bitcast.25), channel_id=1, source_target_pairs={{0,1},{1,0},{2,3},{3,2},{6,7},{7,6},{4,5},{5,4},{12,13},{13,12},{1... | collective-permute-start | bytes 5505032 | tf_op jit(solution)/shard_map/ppermute | solution.py:74
  58.2 23.5 %collective-permute-start.10 = (bf16[384,896]{1,0:T(8,128)(2,1)}, bf16[384,896]{1,0:T(8,128)(2,1)}, u32[]{:S(2)}, u32[]{:S(2)}) collective-permute-start(bf16[384,896]{1,0:T(8,128)(2,1)} %slice.36), channel_id=1, source_target_pairs={{4,12},{12,4},{5,13},{13,5},{8,16},{16,8},{9,17},{17,9},{20,28},{2... | collective-permute-start | bytes 2064392 | tf_op jit(solution)/shard_map/ppermute | solution.py:626
  59.7 22.0 %collective-permute-start.9 = (bf16[384,896]{1,0:T(8,128)(2,1)}, bf16[384,896]{1,0:T(8,128)(2,1)}, u32[]{:S(2)}, u32[]{:S(2)}) collective-permute-start(bf16[384,896]{1,0:T(8,128)(2,1)} %slice.36), channel_id=1, source_target_pairs={{2,0},{3,1},{6,2},{7,3},{4,6},{5,7},{14,12},{15,13},{10,14},{11,15... | collective-permute-start | bytes 2064392 | tf_op jit(solution)/shard_map/ppermute | solution.py:74
  61.0 20.7 %collective-permute-start.8 = (bf16[384,896]{1,0:T(8,128)(2,1)}, bf16[384,896]{1,0:T(8,128)(2,1)}, u32[]{:S(2)}, u32[]{:S(2)}) collective-permute-start(bf16[384,896]{1,0:T(8,128)(2,1)} %slice.36), channel_id=1, source_target_pairs={{0,2},{1,3},{2,6},{3,7},{6,4},{7,5},{12,14},{13,15},{14,10},{15,11... | collective-permute-start | bytes 2064392 | tf_op jit(solution)/shard_map/ppermute | solution.py:74
  67.4 11.4 %collective-permute-start.11 = (bf16[4,112,512]{2,1,0:T(8,128)(2,1)}, bf16[4,112,512]{2,1,0:T(8,128)(2,1)}, u32[]{:S(2)}, u32[]{:S(2)}) collective-permute-start(bf16[4,112,512]{2,1,0:T(8,128)(2,1)} %get-tuple-element.88), channel_id=1, source_target_pairs={{0,1},{1,0},{2,3},{3,2},{6,7},{7,6},{4,5},{5,4},{12,13},{13,12},{1... | collective-permute-start | bytes 1376264 | tf_op jit(solution)/shard_map/ppermute | solution.py:74
  78.3 1.9 collective-permute-start.6
  78.8 1.3 collective-permute-start.7
  81.7 14.5 %collective-permute-start.15 = (bf16[128,896]{1,0:T(8,128)(2,1)S(1)}, bf16[128,896]{1,0:T(8,128)(2,1)S(1)}, u32[]{:S(2)}, u32[]{:S(2)}) collective-permute-start(bf16[128,896]{1,0:T(8,128)(2,1)S(1)} %get-tuple-element.66.m0), channel_id=1, source_target_pairs={{0,4},{1,5},{2,6},{3,7},{6,2},{7,3},{4,0},{5,1},{12,8},{13,9},{14,... | collective-permute-start | bytes 688136 | tf_op jit(solution)/shard_map/ppermute | solution.py:74
  86.1 10.1 %collective-permute-start.14 = (bf16[128,896]{1,0:T(8,128)(2,1)S(1)}, bf16[128,896]{1,0:T(8,128)(2,1)S(1)}, u32[]{:S(2)}, u32[]{:S(2)}) collective-permute-start(bf16[128,896]{1,0:T(8,128)(2,1)S(1)} %get-tuple-element.66.m0), channel_id=1, source_target_pairs={{0,6},{1,7},{2,4},{3,5},{6,0},{7,1},{4,2},{5,3},{12,10},{13,11},{1... | collective-permute-start | bytes 688136 | tf_op jit(solution)/shard_map/ppermute | solution.py:74
  86.1 11.3 %collective-permute-start.13 = (bf16[128,896]{1,0:T(8,128)(2,1)S(1)}, bf16[128,896]{1,0:T(8,128)(2,1)S(1)}, u32[]{:S(2)}, u32[]{:S(2)}) collective-permute-start(bf16[128,896]{1,0:T(8,128)(2,1)S(1)} %get-tuple-element.66.m0), channel_id=1, source_target_pairs={{0,2},{1,3},{2,0},{3,1},{6,4},{7,5},{4,6},{5,7},{12,14},{13,15},{1... | collective-permute-start | bytes 688136 | tf_op jit(solution)/shard_map/ppermute | solution.py:74
  89.0 14.5 %collective-permute-start.12 = (bf16[384,896]{1,0:T(8,128)(2,1)S(1)}, bf16[384,896]{1,0:T(8,128)(2,1)S(1)}, u32[]{:S(2)}, u32[]{:S(2)}) collective-permute-start(bf16[384,896]{1,0:T(8,128)(2,1)S(1)} %get-tuple-element.86.p1a), channel_id=1, source_target_pairs={{0,1},{1,0},{2,3},{3,2},{6,7},{7,6},{4,5},{5,4},{12,13},{13,12},{1... | collective-permute-start | bytes 2064392 | tf_op jit(solution)/shard_map/ppermute | solution.py:74
  89.2 19.9 %collective-permute-start.19 = (bf16[640,896]{1,0:T(8,128)(2,1)S(1)}, bf16[640,896]{1,0:T(8,128)(2,1)S(1)}, u32[]{:S(2)}, u32[]{:S(2)}) collective-permute-start(bf16[640,896]{1,0:T(8,128)(2,1)S(1)} %slice.37), channel_id=1, source_target_pairs={{4,12},{12,4},{5,13},{13,5},{8,16},{16,8},{9,17},{17,9},{20,28},{2... | collective-permute-start | bytes 3440648 | tf_op jit(solution)/shard_map/ppermute | solution.py:626
  97.4 27.6 %collective-permute-start.21 = (bf16[640,896]{1,0:T(8,128)(2,1)S(1)}, bf16[640,896]{1,0:T(8,128)(2,1)S(1)}, u32[]{:S(2)}, u32[]{:S(2)}) collective-permute-start(bf16[640,896]{1,0:T(8,128)(2,1)S(1)} %slice.37), channel_id=1, source_target_pairs={{2,0},{3,1},{6,2},{7,3},{4,6},{5,7},{14,12},{15,13},{10,14},{11,15... | collective-permute-start | bytes 3440648 | tf_op jit(solution)/shard_map/ppermute | solution.py:74
  98.9 27.5 %collective-permute-start.20 = (bf16[640,896]{1,0:T(8,128)(2,1)S(1)}, bf16[640,896]{1,0:T(8,128)(2,1)S(1)}, u32[]{:S(2)}, u32[]{:S(2)}) collective-permute-start(bf16[640,896]{1,0:T(8,128)(2,1)S(1)} %slice.37), channel_id=1, source_target_pairs={{0,2},{1,3},{2,6},{3,7},{6,4},{7,5},{12,14},{13,15},{14,10},{15,11... | collective-permute-start | bytes 3440648 | tf_op jit(solution)/shard_map/ppermute | solution.py:74
  104.8 2.0 %collective-permute-start.16 = (bf16[256,1024]{1,0:T(8,128)(2,1)S(1)}, bf16[256,1024]{1,0:T(8,128)(2,1)S(1)}, u32[]{:S(2)}, u32[]{:S(2)}) collective-permute-start(bf16[256,1024]{1,0:T(8,128)(2,1)S(1)} %get-tuple-element.68.own_ref.half_ref), channel_id=1, source_target_pairs={{0,1},{1,0},{2,3},{3,2},{6,7},{7,6},{4,5},{5,4},{12,13},{13,12},{1... | collective-permute-start | bytes 1572872 | tf_op jit(solution)/shard_map/ppermute | solution.py:74
  104.9 21.7 %collective-permute-start.18 = (bf16[256,1024]{1,0:T(8,128)(2,1)S(1)}, bf16[256,1024]{1,0:T(8,128)(2,1)S(1)}, u32[]{:S(2)}, u32[]{:S(2)}) collective-permute-start(bf16[256,1024]{1,0:T(8,128)(2,1)S(1)} %get-tuple-element.68.own_ref.half_ref), channel_id=1, source_target_pairs={{0,8},{1,9},{2,10},{3,11},{4,12},{5,13},{6,14},{7,15},{8,16},{9,17... | collective-permute-start | bytes 1572872 | tf_op jit(solution)/shard_map/ppermute | solution.py:89
  106.8 19.8 %collective-permute-start.17 = (bf16[256,1024]{1,0:T(8,128)(2,1)S(1)}, bf16[256,1024]{1,0:T(8,128)(2,1)S(1)}, u32[]{:S(2)}, u32[]{:S(2)}) collective-permute-start(bf16[256,1024]{1,0:T(8,128)(2,1)S(1)} %get-tuple-element.68.own_ref.half_ref), channel_id=1, source_target_pairs={{8,0},{9,1},{10,2},{11,3},{12,4},{13,5},{14,6},{15,7},{16,8},{17,9... | collective-permute-start | bytes 1572872 | tf_op jit(solution)/shard_map/ppermute | solution.py:89
  126.3 11.5 %copy-start.8 = (f32[1024,64]{1,0:T(8,128)S(1)}, f32[1024,64]{1,0:T(8,128)}, u32[]{:S(2)}) copy-start(f32[1024,64]{1,0:T(8,128)} %copy-done.7) | copy-start | bytes 786436
  126.5 11.3 %copy-start.2 = (f32[1024,1]{1,0:T(8,128)S(1)}, f32[1024,1]{1,0:T(8,128)}, u32[]{:S(2)}) copy-start(f32[1024,1]{1,0:T(8,128)} %copy-done.1) | copy-start | bytes 12292
  126.5 11.3 %copy-start.4 = (f32[1024,1]{1,0:T(8,128)S(1)}, f32[1024,1]{1,0:T(8,128)}, u32[]{:S(2)}) copy-start(f32[1024,1]{1,0:T(8,128)} %copy-done.3) | copy-start | bytes 12292
  126.6 11.3 %collective-permute-start.22 = (bf16[640,896]{1,0:T(8,128)(2,1)S(1)}, bf16[640,896]{1,0:T(8,128)(2,1)S(1)}, u32[]{:S(2)}, u32[]{:S(2)}) collective-permute-start(bf16[640,896]{1,0:T(8,128)(2,1)S(1)} %get-tuple-element.75.p1b), channel_id=1, source_target_pairs={{0,1},{1,0},{2,3},{3,2},{6,7},{7,6},{4,5},{5,4},{12,13},{13,12},{1... | collective-permute-start | bytes 3440648 | tf_op jit(solution)/shard_map/ppermute | solution.py:74
  127.6 25.6 %collective-permute-start.26 = (bf16[128,64]{1,0:T(8,128)(2,1)S(1)}, bf16[128,64]{1,0:T(8,128)(2,1)S(1)}, u32[]{:S(2)}, u32[]{:S(2)}) collective-permute-start(bf16[128,64]{1,0:T(8,128)(2,1)S(1)} %shard_map.106), channel_id=1, source_target_pairs={{24,0},{25,1},{26,2},{27,3},{28,4},{29,5},{30,6},{31,7},{16,8},{17... | collective-permute-start | bytes 49160 | tf_op jit(solution)/shard_map/ppermute | solution.py:89
  131.3 22.0 %collective-permute-start.25 = (bf16[128,64]{1,0:T(8,128)(2,1)S(1)}, bf16[128,64]{1,0:T(8,128)(2,1)S(1)}, u32[]{:S(2)}, u32[]{:S(2)}) collective-permute-start(bf16[128,64]{1,0:T(8,128)(2,1)S(1)} %shard_map.106), channel_id=1, source_target_pairs={{16,0},{17,1},{18,2},{19,3},{20,4},{21,5},{22,6},{23,7},{24,8},{25... | collective-permute-start | bytes 49160 | tf_op jit(solution)/shard_map/ppermute | solution.py:89
  133.3 20.0 %collective-permute-start.24 = (bf16[128,896]{1,0:T(8,128)(2,1)S(1)}, bf16[128,896]{1,0:T(8,128)(2,1)S(1)}, u32[]{:S(2)}, u32[]{:S(2)}) collective-permute-start(bf16[128,896]{1,0:T(8,128)(2,1)S(1)} %shard_map.105), channel_id=1, source_target_pairs={{24,0},{25,1},{26,2},{27,3},{28,4},{29,5},{30,6},{31,7},{0,24},{1,... | collective-permute-start | bytes 688136 | tf_op jit(solution)/shard_map/ppermute | solution.py:89
  137.8 16.5 %collective-permute-start.23 = (bf16[128,896]{1,0:T(8,128)(2,1)S(1)}, bf16[128,896]{1,0:T(8,128)(2,1)S(1)}, u32[]{:S(2)}, u32[]{:S(2)}) collective-permute-start(bf16[128,896]{1,0:T(8,128)(2,1)S(1)} %shard_map.105), channel_id=1, source_target_pairs={{16,0},{17,1},{18,2},{19,3},{20,4},{21,5},{22,6},{23,7},{24,8},{25... | collective-permute-start | bytes 688136 | tf_op jit(solution)/shard_map/ppermute | solution.py:89
  164.5 22.1 %copy-start = (s32[1,1024]{1,0:T(1,128)S(1)}, s32[1,1024]{1,0:T(1,128)}, u32[]{:S(2)}) copy-start(s32[1,1024]{1,0:T(1,128)} %get-tuple-element.44.place_ref) | copy-start | bytes 12292
  (7 other events, 37.9 us)

commit v5 on v4

--- a/solution.py
+++ b/solution.py
@@ -596,11 +596,11 @@
     send, place = call(
         functools.partial(sort_kernel, rows, per_peer, leaves, lanes),
         pl.GridSpec(
-            grid=(4,),
+            grid=(2,),
             in_specs=[whole((1, rows)), whole((rows, width)), whole((columns, rows))]
             + [whole(a.shape) for a in (skel_leaf, merge_index, near_mask, far_mask)],
             out_specs=[
-                pl.BlockSpec((rows // 4, wide), lambda i: (i, 0)),
+                pl.BlockSpec((rows // 2, wide), lambda i: (i, 0)),
                 whole((1, rows)),
             ],
             scratch_shapes=[pltpu.VMEM((1, rows), I32), pltpu.VMEM((per_peer, lanes), BF16)],

time: 189 us -> 189 us (level)
  no operation moved by 1% of the time
where the time goes in v5:
time: 189 us; the launch traced here: 188 us
  waiting for transfers between devices  59.4 us (31%)
  starting transfers between devices  51.2 us (27%)
  Pallas kernels  48.6 us (26%)
  blocking collectives  22.1 us (12%)
  other arithmetic  3.99 us (2%)
  local copies, waits for them, and re-layouts  2.23 us (1%)
    ppermute x3, waiting for transfers between devices, local(): lax.ppermute(upper, 'leaf', [(i, i ^ 2 * k) for i in range(leaves)])  29.7 us
    ppermute x14, waiting for transfers between devices, move(): return lax.ppermute(value, 'leaf', pairs)  25.3 us
    all_to_all x1, blocking collectives, local(): lax.all_to_all(all_sums, 'leaf', split_axis=0, concat_axis=0, tiled=True)  22.1 us
    ppermute x14, starting transfers between devices, move(): return lax.ppermute(value, 'leaf', pairs)  19.1 us
    pallas_call x1, Pallas kernels, local(): call(functools.partial(pair_kernel, scale_inv, width), prefetch(2, (1,),...  15.3 us
    ppermute x6, starting transfers between devices, send_each(): return lax.ppermute(value, 'leaf', pairs)  13.3 us
    pallas_call x1, Pallas kernels, local(): call(functools.partial(far_kernel, away, len(steps4), sides, per_peer //...  10.3 us
    all_to_all x1, starting transfers between devices, local(): got = lax.all_to_all(send, 'leaf', split_axis=0, concat_axis=0, tiled=True)  7.29 us
  transfers between devices with their start and end apart: 28, of which 9 were waited for; matrix products, arithmetic and copies ran while one was open for 3% of the time, Pallas kernels for 16%

profile of v5, /device:TPU:0, one launch (start us, length us, event | category | flops | bytes accessed | tf_op | source)
XLA Modules:
  0.0 188.0 jit_solution(7652669200801602204)
XLA Ops:
  0.0 6.2 %shard_map.100 = (bf16[1024,896]{1,0:T(8,128)(2,1)}, s32[1,1024]{1,0:T(1,128)}) custom-call(s32[1,1024]{1,0:T(1,128)} %bitcast.42, bf16[1024,768]{1,0:T(8,128)(2,1)} %points_ref.1, bf16[64,1024]{1,0:T(8,128)(2,1)} %bitcast.38, s32[1,256]{1,0:T(1,128)} %skel_ref.1, s32[1,240]{1,0:T(1,128)} %merge_ref.1, s32[1,8]{1,0:T(1,128)} %near_ref.1, s32[1,4,4]{2,1,0:T(4,128)} %far_ref.1), custom_call_target="tpu_custom_call" | custom-call | tf_op jit(solution)/shard_map/pallas_call | solution.py:596
  6.2 7.3 %all-to-all-start = ((bf16[32,32,896]{2,1,0:T(8,128)(2,1)}), bf16[32,32,896]{2,1,0:T(8,128)(2,1)S(1)}, u32[]{:S(2)}, u32[]{:S(2)}) async-start(bf16[32,32,896]{2,1,0:T(8,128)(2,1)} %bitcast.35), calls=%async_computation | async-start | bytes 3670016 | tf_op jit(solution)/shard_map/all_to_all | solution.py:611
  13.5 1.7 collective-permute-start
  15.9 6.2 %collective-permute-start.4 = (bf16[112,512]{1,0:T(8,128)(2,1)S(1)}, bf16[112,512]{1,0:T(8,128)(2,1)S(1)}, u32[]{:S(2)}, u32[]{:S(2)}) collective-permute-start(bf16[112,512]{1,0:T(8,128)(2,1)S(1)} %get-tuple-element.90), channel_id=1, source_target_pairs={{0,6},{1,7},{2,4},{3,5},{4,2},{5,3},{6,0},{7,1},{8,14},{9,15},{10,... | collective-permute-start | bytes 344072 | tf_op jit(solution)/shard_map/ppermute | solution.py:641
  23.6 29.7 %collective-permute-done.4 = bf16[112,512]{1,0:T(8,128)(2,1)S(1)} collective-permute-done((bf16[112,512]{1,0:T(8,128)(2,1)S(1)}, bf16[112,512]{1,0:T(8,128)(2,1)S(1)}, u32[]{:S(2)}, u32[]{:S(2)}) %collective-permute-start.4) | collective-permute-done | bytes 114720 | tf_op jit(solution)/shard_map/ppermute | solution.py:641
  53.3 3.6 %all-to-all-done = bf16[32,32,896]{2,1,0:T(8,128)(2,1)S(1)} async-done(((bf16[32,32,896]{2,1,0:T(8,128)(2,1)}), bf16[32,32,896]{2,1,0:T(8,128)(2,1)S(1)}, u32[]{:S(2)}, u32[]{:S(2)}) %all-to-all-start) | async-done | bytes 1835040 | tf_op jit(solution)/shard_map/all_to_all | solution.py:611
  57.8 1.5 collective-permute-start.10
  59.3 1.3 collective-permute-start.9
  60.6 5.4 %collective-permute-start.8 = (bf16[384,896]{1,0:T(8,128)(2,1)}, bf16[384,896]{1,0:T(8,128)(2,1)}, u32[]{:S(2)}, u32[]{:S(2)}) collective-permute-start(bf16[384,896]{1,0:T(8,128)(2,1)} %slice.36), channel_id=1, source_target_pairs={{0,2},{1,3},{2,6},{3,7},{6,4},{7,5},{12,14},{13,15},{14,10},{15,11... | collective-permute-start | bytes 2064392 | tf_op jit(solution)/shard_map/ppermute | solution.py:74
  67.6 7.0 %shard_map.101 = (f32[1024,64]{1,0:T(8,128)S(1)}, f32[1024,64]{1,0:T(8,128)S(1)}, f32[1024,1]{1,0:T(8,128)S(1)}, f32[1024,1]{1,0:T(8,128)S(1)}) custom-call(s32[10]{0:T(128)S(1)} %concatenate.6.info, s32[32,24]{1,0:T(8,128)S(1)} %maximum_convert_fusion.mask_ref, bf16[1024,896]{1,0:T(8,128)(2,1)S(1)} %bitcast.28, ...), custom_call_target="tpu_custom_call" | custom-call | flops 2415919104 | tf_op jit(solution)/shard_map/pallas_call | solution.py:667
  74.7 3.3 %shard_map.102 = (bf16[128,896]{1,0:T(8,128)(2,1)S(1)}, bf16[128,768]{1,0:T(8,128)(2,1)S(1)}, bf16[256,64]{1,0:T(8,128)(2,1)S(1)}) custom-call(s32[10]{0:T(128)S(1)} %concatenate.6.info, bf16[1024,896]{1,0:T(8,128)(2,1)S(1)} %bitcast.29, bf16[256,1024]{1,0:T(8,128)(2,1)S(1)} %collective-permute-done.interp_ref, f32[32,512]{1,0:T(8,128)S(1)} %slice_add_fusion.table_ref), custom_call_target="tpu_custom_call" | custom-call | tf_op jit(solution)/shard_map/pallas_call | solution.py:674
  78.7 1.1 pad_maximum_fusion.pieces_ref
  80.0 1.5 shard_map.103
  81.4 4.2 %collective-permute-start.15 = (bf16[128,896]{1,0:T(8,128)(2,1)S(1)}, bf16[128,896]{1,0:T(8,128)(2,1)S(1)}, u32[]{:S(2)}, u32[]{:S(2)}) collective-permute-start(bf16[128,896]{1,0:T(8,128)(2,1)S(1)} %get-tuple-element.66.m0), channel_id=1, source_target_pairs={{0,4},{1,5},{2,6},{3,7},{6,2},{7,3},{4,0},{5,1},{12,8},{13,9},{14,... | collective-permute-start | bytes 688136 | tf_op jit(solution)/shard_map/ppermute | solution.py:74
  85.7 1.5 collective-permute-start.13
  87.1 1.4 broadcast_select_fusion.2
  89.5 6.2 %collective-permute-done.15.m3 = bf16[128,896]{1,0:T(8,128)(2,1)S(1)} collective-permute-done((bf16[128,896]{1,0:T(8,128)(2,1)S(1)}, bf16[128,896]{1,0:T(8,128)(2,1)S(1)}, u32[]{:S(2)}, u32[]{:S(2)}) %collective-permute-start.15) | collective-permute-done | bytes 229408 | tf_op jit(solution)/shard_map/ppermute | solution.py:74
  95.8 1.2 collective-permute-done.13.m1
  97.0 1.3 collective-permute-start.21
  98.3 4.6 %collective-permute-start.20 = (bf16[640,896]{1,0:T(8,128)(2,1)S(1)}, bf16[640,896]{1,0:T(8,128)(2,1)S(1)}, u32[]{:S(2)}, u32[]{:S(2)}) collective-permute-start(bf16[640,896]{1,0:T(8,128)(2,1)S(1)} %slice.37), channel_id=1, source_target_pairs={{0,2},{1,3},{2,6},{3,7},{6,4},{7,5},{12,14},{13,15},{14,10},{15,11... | collective-permute-start | bytes 3440648 | tf_op jit(solution)/shard_map/ppermute | solution.py:74
  102.9 1.3 shard_map.104
  104.3 1.4 collective-permute-start.18
  106.2 1.3 collective-permute-start.17
  108.5 16.0 %collective-permute-done.21 = bf16[640,896]{1,0:T(8,128)(2,1)S(1)} collective-permute-done((bf16[640,896]{1,0:T(8,128)(2,1)S(1)}, bf16[640,896]{1,0:T(8,128)(2,1)S(1)}, u32[]{:S(2)}, u32[]{:S(2)}) %collective-permute-start.21) | collective-permute-done | bytes 1146912 | tf_op jit(solution)/shard_map/ppermute | solution.py:74
  124.6 1.2 collective-permute-done.20
  127.0 4.0 %collective-permute-start.26 = (bf16[128,64]{1,0:T(8,128)(2,1)S(1)}, bf16[128,64]{1,0:T(8,128)(2,1)S(1)}, u32[]{:S(2)}, u32[]{:S(2)}) collective-permute-start(bf16[128,64]{1,0:T(8,128)(2,1)S(1)} %shard_map.106), channel_id=1, source_target_pairs={{24,0},{25,1},{26,2},{27,3},{28,4},{29,5},{30,6},{31,7},{16,8},{17... | collective-permute-start | bytes 49160 | tf_op jit(solution)/shard_map/ppermute | solution.py:89
  131.1 1.8 collective-permute-start.25
  132.9 4.7 %collective-permute-start.24 = (bf16[128,896]{1,0:T(8,128)(2,1)S(1)}, bf16[128,896]{1,0:T(8,128)(2,1)S(1)}, u32[]{:S(2)}, u32[]{:S(2)}) collective-permute-start(bf16[128,896]{1,0:T(8,128)(2,1)S(1)} %shard_map.105), channel_id=1, source_target_pairs={{24,0},{25,1},{26,2},{27,3},{28,4},{29,5},{30,6},{31,7},{0,24},{1,... | collective-permute-start | bytes 688136 | tf_op jit(solution)/shard_map/ppermute | solution.py:89
  137.7 15.3 %shard_map.107 = (f32[1024,64]{1,0:T(8,128)S(1)}, f32[1024,64]{1,0:T(8,128)S(1)}, bf16[1024,192]{1,0:T(8,128)(2,1)S(1)}) custom-call(s32[10]{0:T(128)S(1)} %concatenate.6.info, s32[32,24]{1,0:T(8,128)S(1)} %maximum_convert_fusion.mask_ref, bf16[1024,896]{1,0:T(8,128)(2,1)S(1)} %bitcast.31, bf16[1024,896]{1,0:T(8,128)(2,1)} %collective-permute-done.5.other_ref.q2.x2_ref, ...), custom_call_target="tpu_custom_call" | custom-call | flops 6442450944 | tf_op jit(solution)/shard_map/pallas_call | solution.py:729
  153.9 10.3 %shard_map.108 = bf16[512,640]{1,0:T(8,128)(2,1)S(1)} custom-call(s32[10]{0:T(128)S(1)} %concatenate.6.info, s32[32,24]{1,0:T(8,128)S(1)} %maximum_convert_fusion.mask_ref, bf16[1024,896]{1,0:T(8,128)(2,1)S(1)} %bitcast.32, bf16[1024,896]{1,0:T(8,128)(2,1)} %collective-permute-done.5.other_ref.q2.x2_ref, f32[1024,1]{1,0:T(8,128)S(1)} %copy-done.2, ...), custom_call_target="tpu_custom_call" | custom-call | flops 3221225472 | tf_op jit(solution)/shard_map/pallas_call | solution.py:739
  164.2 22.1 %all_to_all.23 = bf16[32,16,640]{2,1,0:T(8,128)(2,1)S(1)} all-to-all(bf16[32,16,640]{2,1,0:T(8,128)(2,1)S(1)} %bitcast.34), channel_id=1, replica_groups=mesh['leaf'=32] {'leaf'}, dimensions={0} | all-to-all | bytes 1310720 | tf_op jit(solution)/shard_map/all_to_all | solution.py:751
  186.3 1.7 shard_map.109
  (73 shorter events, 10.0 us)
Async XLA Ops:
  6.2 50.7 %all-to-all-start = ((bf16[32,32,896]{2,1,0:T(8,128)(2,1)}), bf16[32,32,896]{2,1,0:T(8,128)(2,1)S(1)}, u32[]{:S(2)}, u32[]{:S(2)}) async-start(bf16[32,32,896]{2,1,0:T(8,128)(2,1)} %bitcast.35), calls=%async_computation | async-start | bytes 3670016 | tf_op jit(solution)/shard_map/all_to_all | solution.py:611
  13.5 39.8 %collective-permute-start = (bf16[256,1024]{1,0:T(8,128)(2,1)}, bf16[256,1024]{1,0:T(8,128)(2,1)S(1)}, u32[]{:S(2)}, u32[]{:S(2)}) collective-permute-start(bf16[256,1024]{1,0:T(8,128)(2,1)} %bitcast.4), channel_id=1, source_target_pairs={{0,0},{1,1},{2,2},{3,3},{4,6},{5,7},{6,4},{7,5},{8,12},{9,13},{10,... | collective-permute-start | bytes 1572872 | tf_op jit(solution)/shard_map/ppermute | solution.py:638
  15.2 38.1 %collective-permute-start.1 = (bf16[128,512]{1,0:T(8,128)(2,1)S(1)}, bf16[128,512]{1,0:T(8,128)(2,1)S(1)}, u32[]{:S(2)}, u32[]{:S(2)}) collective-permute-start(bf16[128,512]{1,0:T(8,128)(2,1)S(1)} %slice.29), channel_id=1, source_target_pairs={{0,0},{1,1},{2,2},{3,3},{4,6},{5,7},{6,4},{7,5},{8,12},{9,13},{10,... | collective-permute-start | bytes 393224 | tf_op jit(solution)/shard_map/ppermute | solution.py:639
  15.9 37.4 %collective-permute-start.4 = (bf16[112,512]{1,0:T(8,128)(2,1)S(1)}, bf16[112,512]{1,0:T(8,128)(2,1)S(1)}, u32[]{:S(2)}, u32[]{:S(2)}) collective-permute-start(bf16[112,512]{1,0:T(8,128)(2,1)S(1)} %get-tuple-element.90), channel_id=1, source_target_pairs={{0,6},{1,7},{2,4},{3,5},{4,2},{5,3},{6,0},{7,1},{8,14},{9,15},{10,... | collective-permute-start | bytes 344072 | tf_op jit(solution)/shard_map/ppermute | solution.py:641
  22.1 31.1 %collective-permute-start.3 = (bf16[112,512]{1,0:T(8,128)(2,1)S(1)}, bf16[112,512]{1,0:T(8,128)(2,1)S(1)}, u32[]{:S(2)}, u32[]{:S(2)}) collective-permute-start(bf16[112,512]{1,0:T(8,128)(2,1)S(1)} %get-tuple-element.90), channel_id=1, source_target_pairs={{0,4},{1,5},{2,6},{3,7},{4,0},{5,1},{6,2},{7,3},{8,12},{9,13},{10,... | collective-permute-start | bytes 344072 | tf_op jit(solution)/shard_map/ppermute | solution.py:641
  22.1 31.1 %collective-permute-start.2 = (bf16[112,512]{1,0:T(8,128)(2,1)S(1)}, bf16[112,512]{1,0:T(8,128)(2,1)S(1)}, u32[]{:S(2)}, u32[]{:S(2)}) collective-permute-start(bf16[112,512]{1,0:T(8,128)(2,1)S(1)} %get-tuple-element.90), channel_id=1, source_target_pairs={{0,2},{1,3},{2,0},{3,1},{4,6},{5,7},{6,4},{7,5},{8,10},{9,11},{10,... | collective-permute-start | bytes 344072 | tf_op jit(solution)/shard_map/ppermute | solution.py:641
  56.9 10.8 %collective-permute-start.5 = (bf16[1024,896]{1,0:T(8,128)(2,1)S(1)}, bf16[1024,896]{1,0:T(8,128)(2,1)}, u32[]{:S(2)}, u32[]{:S(2)}) collective-permute-start(bf16[1024,896]{1,0:T(8,128)(2,1)S(1)} %bitcast.25), channel_id=1, source_target_pairs={{0,1},{1,0},{2,3},{3,2},{6,7},{7,6},{4,5},{5,4},{12,13},{13,12},{1... | collective-permute-start | bytes 5505032 | tf_op jit(solution)/shard_map/ppermute | solution.py:74
  57.8 23.6 %collective-permute-start.10 = (bf16[384,896]{1,0:T(8,128)(2,1)}, bf16[384,896]{1,0:T(8,128)(2,1)}, u32[]{:S(2)}, u32[]{:S(2)}) collective-permute-start(bf16[384,896]{1,0:T(8,128)(2,1)} %slice.36), channel_id=1, source_target_pairs={{4,12},{12,4},{5,13},{13,5},{8,16},{16,8},{9,17},{17,9},{20,28},{2... | collective-permute-start | bytes 2064392 | tf_op jit(solution)/shard_map/ppermute | solution.py:626
  59.3 22.1 %collective-permute-start.9 = (bf16[384,896]{1,0:T(8,128)(2,1)}, bf16[384,896]{1,0:T(8,128)(2,1)}, u32[]{:S(2)}, u32[]{:S(2)}) collective-permute-start(bf16[384,896]{1,0:T(8,128)(2,1)} %slice.36), channel_id=1, source_target_pairs={{2,0},{3,1},{6,2},{7,3},{4,6},{5,7},{14,12},{15,13},{10,14},{11,15... | collective-permute-start | bytes 2064392 | tf_op jit(solution)/shard_map/ppermute | solution.py:74
  60.6 20.8 %collective-permute-start.8 = (bf16[384,896]{1,0:T(8,128)(2,1)}, bf16[384,896]{1,0:T(8,128)(2,1)}, u32[]{:S(2)}, u32[]{:S(2)}) collective-permute-start(bf16[384,896]{1,0:T(8,128)(2,1)} %slice.36), channel_id=1, source_target_pairs={{0,2},{1,3},{2,6},{3,7},{6,4},{7,5},{12,14},{13,15},{14,10},{15,11... | collective-permute-start | bytes 2064392 | tf_op jit(solution)/shard_map/ppermute | solution.py:74
  67.0 11.6 %collective-permute-start.11 = (bf16[4,112,512]{2,1,0:T(8,128)(2,1)}, bf16[4,112,512]{2,1,0:T(8,128)(2,1)}, u32[]{:S(2)}, u32[]{:S(2)}) collective-permute-start(bf16[4,112,512]{2,1,0:T(8,128)(2,1)} %get-tuple-element.88), channel_id=1, source_target_pairs={{0,1},{1,0},{2,3},{3,2},{6,7},{7,6},{4,5},{5,4},{12,13},{13,12},{1... | collective-permute-start | bytes 1376264 | tf_op jit(solution)/shard_map/ppermute | solution.py:74
  78.1 1.9 collective-permute-start.6
  78.6 1.3 collective-permute-start.7
  81.4 14.3 %collective-permute-start.15 = (bf16[128,896]{1,0:T(8,128)(2,1)S(1)}, bf16[128,896]{1,0:T(8,128)(2,1)S(1)}, u32[]{:S(2)}, u32[]{:S(2)}) collective-permute-start(bf16[128,896]{1,0:T(8,128)(2,1)S(1)} %get-tuple-element.66.m0), channel_id=1, source_target_pairs={{0,4},{1,5},{2,6},{3,7},{6,2},{7,3},{4,0},{5,1},{12,8},{13,9},{14,... | collective-permute-start | bytes 688136 | tf_op jit(solution)/shard_map/ppermute | solution.py:74
  85.7 10.1 %collective-permute-start.14 = (bf16[128,896]{1,0:T(8,128)(2,1)S(1)}, bf16[128,896]{1,0:T(8,128)(2,1)S(1)}, u32[]{:S(2)}, u32[]{:S(2)}) collective-permute-start(bf16[128,896]{1,0:T(8,128)(2,1)S(1)} %get-tuple-element.66.m0), channel_id=1, source_target_pairs={{0,6},{1,7},{2,4},{3,5},{6,0},{7,1},{4,2},{5,3},{12,10},{13,11},{1... | collective-permute-start | bytes 688136 | tf_op jit(solution)/shard_map/ppermute | solution.py:74
  85.7 11.3 %collective-permute-start.13 = (bf16[128,896]{1,0:T(8,128)(2,1)S(1)}, bf16[128,896]{1,0:T(8,128)(2,1)S(1)}, u32[]{:S(2)}, u32[]{:S(2)}) collective-permute-start(bf16[128,896]{1,0:T(8,128)(2,1)S(1)} %get-tuple-element.66.m0), channel_id=1, source_target_pairs={{0,2},{1,3},{2,0},{3,1},{6,4},{7,5},{4,6},{5,7},{12,14},{13,15},{1... | collective-permute-start | bytes 688136 | tf_op jit(solution)/shard_map/ppermute | solution.py:74
  88.6 14.3 %collective-permute-start.12 = (bf16[384,896]{1,0:T(8,128)(2,1)S(1)}, bf16[384,896]{1,0:T(8,128)(2,1)S(1)}, u32[]{:S(2)}, u32[]{:S(2)}) collective-permute-start(bf16[384,896]{1,0:T(8,128)(2,1)S(1)} %get-tuple-element.86.p1a), channel_id=1, source_target_pairs={{0,1},{1,0},{2,3},{3,2},{6,7},{7,6},{4,5},{5,4},{12,13},{13,12},{1... | collective-permute-start | bytes 2064392 | tf_op jit(solution)/shard_map/ppermute | solution.py:74
  88.8 19.8 %collective-permute-start.19 = (bf16[640,896]{1,0:T(8,128)(2,1)S(1)}, bf16[640,896]{1,0:T(8,128)(2,1)S(1)}, u32[]{:S(2)}, u32[]{:S(2)}) collective-permute-start(bf16[640,896]{1,0:T(8,128)(2,1)S(1)} %slice.37), channel_id=1, source_target_pairs={{4,12},{12,4},{5,13},{13,5},{8,16},{16,8},{9,17},{17,9},{20,28},{2... | collective-permute-start | bytes 3440648 | tf_op jit(solution)/shard_map/ppermute | solution.py:626
  97.0 27.6 %collective-permute-start.21 = (bf16[640,896]{1,0:T(8,128)(2,1)S(1)}, bf16[640,896]{1,0:T(8,128)(2,1)S(1)}, u32[]{:S(2)}, u32[]{:S(2)}) collective-permute-start(bf16[640,896]{1,0:T(8,128)(2,1)S(1)} %slice.37), channel_id=1, source_target_pairs={{2,0},{3,1},{6,2},{7,3},{4,6},{5,7},{14,12},{15,13},{10,14},{11,15... | collective-permute-start | bytes 3440648 | tf_op jit(solution)/shard_map/ppermute | solution.py:74
  98.3 27.5 %collective-permute-start.20 = (bf16[640,896]{1,0:T(8,128)(2,1)S(1)}, bf16[640,896]{1,0:T(8,128)(2,1)S(1)}, u32[]{:S(2)}, u32[]{:S(2)}) collective-permute-start(bf16[640,896]{1,0:T(8,128)(2,1)S(1)} %slice.37), channel_id=1, source_target_pairs={{0,2},{1,3},{2,6},{3,7},{6,4},{7,5},{12,14},{13,15},{14,10},{15,11... | collective-permute-start | bytes 3440648 | tf_op jit(solution)/shard_map/ppermute | solution.py:74
  104.2 2.0 %collective-permute-start.16 = (bf16[256,1024]{1,0:T(8,128)(2,1)S(1)}, bf16[256,1024]{1,0:T(8,128)(2,1)S(1)}, u32[]{:S(2)}, u32[]{:S(2)}) collective-permute-start(bf16[256,1024]{1,0:T(8,128)(2,1)S(1)} %get-tuple-element.68.own_ref.half_ref), channel_id=1, source_target_pairs={{0,1},{1,0},{2,3},{3,2},{6,7},{7,6},{4,5},{5,4},{12,13},{13,12},{1... | collective-permute-start | bytes 1572872 | tf_op jit(solution)/shard_map/ppermute | solution.py:74
  104.3 21.7 %collective-permute-start.18 = (bf16[256,1024]{1,0:T(8,128)(2,1)S(1)}, bf16[256,1024]{1,0:T(8,128)(2,1)S(1)}, u32[]{:S(2)}, u32[]{:S(2)}) collective-permute-start(bf16[256,1024]{1,0:T(8,128)(2,1)S(1)} %get-tuple-element.68.own_ref.half_ref), channel_id=1, source_target_pairs={{0,8},{1,9},{2,10},{3,11},{4,12},{5,13},{6,14},{7,15},{8,16},{9,17... | collective-permute-start | bytes 1572872 | tf_op jit(solution)/shard_map/ppermute | solution.py:89
  106.2 19.8 %collective-permute-start.17 = (bf16[256,1024]{1,0:T(8,128)(2,1)S(1)}, bf16[256,1024]{1,0:T(8,128)(2,1)S(1)}, u32[]{:S(2)}, u32[]{:S(2)}) collective-permute-start(bf16[256,1024]{1,0:T(8,128)(2,1)S(1)} %get-tuple-element.68.own_ref.half_ref), channel_id=1, source_target_pairs={{8,0},{9,1},{10,2},{11,3},{12,4},{13,5},{14,6},{15,7},{16,8},{17,9... | collective-permute-start | bytes 1572872 | tf_op jit(solution)/shard_map/ppermute | solution.py:89
  125.7 11.9 %copy-start.8 = (f32[1024,64]{1,0:T(8,128)S(1)}, f32[1024,64]{1,0:T(8,128)}, u32[]{:S(2)}) copy-start(f32[1024,64]{1,0:T(8,128)} %copy-done.7) | copy-start | bytes 786436
  126.0 11.7 %copy-start.2 = (f32[1024,1]{1,0:T(8,128)S(1)}, f32[1024,1]{1,0:T(8,128)}, u32[]{:S(2)}) copy-start(f32[1024,1]{1,0:T(8,128)} %copy-done.1) | copy-start | bytes 12292
  126.0 11.7 %copy-start.4 = (f32[1024,1]{1,0:T(8,128)S(1)}, f32[1024,1]{1,0:T(8,128)}, u32[]{:S(2)}) copy-start(f32[1024,1]{1,0:T(8,128)} %copy-done.3) | copy-start | bytes 12292
  126.0 11.7 %collective-permute-start.22 = (bf16[640,896]{1,0:T(8,128)(2,1)S(1)}, bf16[640,896]{1,0:T(8,128)(2,1)S(1)}, u32[]{:S(2)}, u32[]{:S(2)}) collective-permute-start(bf16[640,896]{1,0:T(8,128)(2,1)S(1)} %get-tuple-element.75.p1b), channel_id=1, source_target_pairs={{0,1},{1,0},{2,3},{3,2},{6,7},{7,6},{4,5},{5,4},{12,13},{13,12},{1... | collective-permute-start | bytes 3440648 | tf_op jit(solution)/shard_map/ppermute | solution.py:74
  127.0 26.0 %collective-permute-start.26 = (bf16[128,64]{1,0:T(8,128)(2,1)S(1)}, bf16[128,64]{1,0:T(8,128)(2,1)S(1)}, u32[]{:S(2)}, u32[]{:S(2)}) collective-permute-start(bf16[128,64]{1,0:T(8,128)(2,1)S(1)} %shard_map.106), channel_id=1, source_target_pairs={{24,0},{25,1},{26,2},{27,3},{28,4},{29,5},{30,6},{31,7},{16,8},{17... | collective-permute-start | bytes 49160 | tf_op jit(solution)/shard_map/ppermute | solution.py:89
  131.1 22.0 %collective-permute-start.25 = (bf16[128,64]{1,0:T(8,128)(2,1)S(1)}, bf16[128,64]{1,0:T(8,128)(2,1)S(1)}, u32[]{:S(2)}, u32[]{:S(2)}) collective-permute-start(bf16[128,64]{1,0:T(8,128)(2,1)S(1)} %shard_map.106), channel_id=1, source_target_pairs={{16,0},{17,1},{18,2},{19,3},{20,4},{21,5},{22,6},{23,7},{24,8},{25... | collective-permute-start | bytes 49160 | tf_op jit(solution)/shard_map/ppermute | solution.py:89
  132.9 20.2 %collective-permute-start.24 = (bf16[128,896]{1,0:T(8,128)(2,1)S(1)}, bf16[128,896]{1,0:T(8,128)(2,1)S(1)}, u32[]{:S(2)}, u32[]{:S(2)}) collective-permute-start(bf16[128,896]{1,0:T(8,128)(2,1)S(1)} %shard_map.105), channel_id=1, source_target_pairs={{24,0},{25,1},{26,2},{27,3},{28,4},{29,5},{30,6},{31,7},{0,24},{1,... | collective-permute-start | bytes 688136 | tf_op jit(solution)/shard_map/ppermute | solution.py:89
  137.6 16.3 %collective-permute-start.23 = (bf16[128,896]{1,0:T(8,128)(2,1)S(1)}, bf16[128,896]{1,0:T(8,128)(2,1)S(1)}, u32[]{:S(2)}, u32[]{:S(2)}) collective-permute-start(bf16[128,896]{1,0:T(8,128)(2,1)S(1)} %shard_map.105), channel_id=1, source_target_pairs={{16,0},{17,1},{18,2},{19,3},{20,4},{21,5},{22,6},{23,7},{24,8},{25... | collective-permute-start | bytes 688136 | tf_op jit(solution)/shard_map/ppermute | solution.py:89
  164.2 22.1 %copy-start = (s32[1,1024]{1,0:T(1,128)S(1)}, s32[1,1024]{1,0:T(1,128)}, u32[]{:S(2)}) copy-start(s32[1,1024]{1,0:T(1,128)} %get-tuple-element.44.place_ref) | copy-start | bytes 12292
  (7 other events, 38.4 us)
